TPU v7x, 768 devices: a whole 4x8x12 slice. The times are simulated.
768 devices in a mesh: row: 48 (over y_lo, z, core), col: 16 (over y_hi, x).
Axes of the slice: x: 4, y: 8 (y_hi: 4, y_lo: 2; y = y_hi * 2 + y_lo), z: 12, core: 2. Of those that a mesh axis runs over, the one named last changes fastest.
Arguments:
- df_blocks: bfloat16 [576, 576, 1024], P('row', 'col'), may hold values from -1 to 1
- amplitudes: bfloat16 [48, 576, 576], P(None, 'col'), may hold values from -0.009765625 to 0.009765625
Outputs:
- ladder_ab: float32 [576, 4, 48], P('row')
- ladder_ba: float32 [576, 4, 48], P('row')
All inputs are finite; a program needn't handle non-finite values.
Results may differ from a plain program's by a relative error of at most 0.0029.
Values may be sent and summed in bfloat16 or wider, within the bound.
No kernel may reach another device: no remote copies, remote signals or barrier semaphores. Data moves between devices by JAX's collectives and lax.ppermute only.
A program may use at most 64 MiB of HBM per device.

v0:
```python
import jax
import jax.numpy as jnp
from jax import lax
from jax.sharding import PartitionSpec as P

WIN = 4


def shifted_2(value, axis, steps):
    count = lax.axis_size(axis)
    pairs = [(source, (source + steps) % count) for source in range(count)]
    return lax.ppermute(value, axis, pairs)


def sent_to_all(shard, axis):
    copies = jnp.broadcast_to(shard, (lax.axis_size(axis), *shard.shape))
    return lax.all_to_all(copies, axis, split_axis=0, concat_axis=0, tiled=True)


def of_everyone(shard, axis):
    everything = sent_to_all(shard, axis)
    return jnp.sum(everything, axis=0)


def together(arrays, axis):
    line, at, gathered = (jnp.concatenate([a.reshape(-1) for a in arrays]), 0, [])
    so_far = of_everyone(line, axis)
    for a in arrays:
        gathered.append(so_far[at : at + a.size].reshape(a.shape))
        at += a.size
    return tuple(gathered)


def form_tile(resident, incoming):
    v_tile = jnp.einsum("acq,jdq->ajcd", resident, incoming, preferred_element_type=jnp.float32)
    return v_tile.astype(jnp.bfloat16)


def shards(df_blocks, amplitudes):
    shifted = shifted_2(df_blocks[:WIN], "row", -1)
    flipped = lax.all_to_all(amplitudes, "col", split_axis=2, concat_axis=1, tiled=True)
    v_tile = form_tile(df_blocks, lax.all_gather(shifted, "col", axis=1, tiled=True))
    first = jnp.einsum("ajcd,pcd->ajp", v_tile, amplitudes, preferred_element_type=jnp.float32)
    second = jnp.einsum("ajcd,pdc->ajp", v_tile, flipped, preferred_element_type=jnp.float32)
    forward = first
    backward = second
    forward, backward = together((forward, backward), "col")
    return (forward, backward)


def solution(mesh):
    in_specs = (P("row", "col", None), P(None, "col", None))
    out_specs = (P("row", None, None), P("row", None, None))
    return jax.shard_map(shards, mesh=mesh, in_specs=in_specs, out_specs=out_specs, check_vma=False)
```

profile of v0, /device:TPU:264, one launch (start us, length us, event | category | flops | bytes accessed | tf_op | source)
XLA Modules:
  0.0 182.4 jit_solution(13736868803572838217)
XLA Ops:
  7.2 0.0 all-gather.2.cloned.1.call-start
  7.2 1.0 slice.25
  8.2 0.2 copy.48
  8.4 1.9 %collective-permute-start = (bf16[4,36,1024]{2,0,1:T(4,128)(2,1)S(1)}, bf16[4,36,1024]{2,0,1:T(4,128)(2,1)S(1)}, u32[]{:S(2)}, u32[]{:S(2)}) collective-permute-start(bf16[4,36,1024]{2,0,1:T(4,128)(2,1)S(1)} %copy.48), channel_id=1, source_target_pairs={{0,752},{16,0},{32,16},{48,32},{64,48},{80,64},{96,80},{112,96},{1... | collective-permute-start | bytes 884744 | tf_op jit(solution)/shard_map/ppermute | solution.py:12
  10.4 4.2 %collective-permute-done = bf16[4,36,1024]{2,0,1:T(4,128)(2,1)S(1)} collective-permute-done((bf16[4,36,1024]{2,0,1:T(4,128)(2,1)S(1)}, bf16[4,36,1024]{2,0,1:T(4,128)(2,1)S(1)}, u32[]{:S(2)}, u32[]{:S(2)}) %collective-permute-start) | collective-permute-done | bytes 294944 | tf_op jit(solution)/shard_map/ppermute | solution.py:12
  14.6 0.0 copy-start.1
  14.6 0.7 copy-done.1
  15.3 0.0 all-gather.2.cloned.1.call-update
  15.3 10.7 %copy.34 = bf16[48,36,576]{0,1,2:T(8,128)(2,1)} copy(bf16[48,36,576]{2,0,1:T(8,128)(2,1)} %param.3) | data formatting | bytes 3981312 | tf_op args[1]
  26.1 9.4 %reshape.47 = bf16[16,2,31104]{2,1,0:T(2,128)(2,1)S(1)} reshape(bf16[576,36,48]{2,1,0:T(8,128)(2,1)} %bitcast.29) | data formatting | bytes 3981312
  35.5 64.5 %all_to_all.24 = bf16[16,2,31104]{2,1,0:T(2,128)(2,1)} all-to-all(bf16[16,2,31104]{2,1,0:T(2,128)(2,1)S(1)} %reshape.47), channel_id=1, replica_groups=mesh['row'=48,'col'=16] {'col'}, dimensions={0} | all-to-all | bytes 3981312 | tf_op jit(solution)/shard_map/all_to_all | solution.py:41
  100.0 11.2 %reshape.48 = bf16[576,36,48]{2,1,0:T(8,128)(2,1)} reshape(bf16[16,2,31104]{2,1,0:T(2,128)(2,1)} %all_to_all.24) | data formatting | bytes 3981312
  111.2 10.9 %copy.36 = bf16[48,16,36,36]{2,1,0,3:T(8,128)(2,1)} copy(bf16[48,16,36,36]{0,2,3,1:T(8,128)(2,1)} %bitcast.28) | data formatting | bytes 3981312 | tf_op jit(solution)/shard_map/all_to_all | solution.py:41
  122.1 0.0 copy-start.2
  122.1 9.8 %reshape.44 = bf16[48,576,36,1]{1,0,2,3:T(8,128)(2,1)S(1)} reshape(bf16[48,16,36,36]{2,1,0,3:T(8,128)(2,1)} %copy.36) | data formatting | bytes 3981312 | tf_op jit(solution)/shard_map/all_to_all | solution.py:41
  132.0 1.1 all-gather.2.cloned.1.call-done
  133.1 0.0 copy-done.2
  133.1 0.0 copy-start
  133.1 8.8 %convert_bitcast_fusion = bf16[12,4,36,576]{3,2,0,1:T(8,128)(2,1)S(1)} fusion(bf16[4,576,1024,1]{2,0,1,3:T(4,128)(2,1)} %bitcast.30, bf16[12,36,1024]{2,1,0:T(8,128)(2,1)S(1)} %copy-done.2), kind=kOutput, calls=%fused_computation.6 | convolution fusion | flops 2039427072 | bytes 7593984 | tf_op jit(solution)/shard_map/acq,jdq->ajcd/dot_general | solution.py:35
  141.9 0.0 copy-done
  141.9 0.9 fusion.9
  142.8 0.9 fusion.14
  143.7 0.1 reshape.37
  143.8 0.1 reshape.36
  143.9 0.2 broadcast_in_dim.3
  144.1 29.9 %all_to_all.25 = f32[16,1,4608]{2,1,0:T(1,128)S(1)} all-to-all(f32[16,1,4608]{2,1,0:T(1,128)S(1)} %broadcast_in_dim.3), channel_id=1, replica_groups=mesh['row'=48,'col'=16] {'col'}, dimensions={0} | all-to-all | bytes 589824 | tf_op jit(solution)/shard_map/all_to_all | solution.py:17
  174.0 0.2 reduce_sum.9
  174.2 0.7 reshape.38
  174.9 0.7 reshape.39
  (4 shorter events, 0.0 us)
Async XLA Ops:
  7.2 125.9 %all-gather.2.cloned.1.call-start = ((), (), s32[]{:S(2)}) async-start(), calls=%async_computation.2 | async-start | bytes 5013504 | tf_op jit(solution)/shard_map/all_gather | solution.py:42
  8.4 6.1 %collective-permute-start = (bf16[4,36,1024]{2,0,1:T(4,128)(2,1)S(1)}, bf16[4,36,1024]{2,0,1:T(4,128)(2,1)S(1)}, u32[]{:S(2)}, u32[]{:S(2)}) collective-permute-start(bf16[4,36,1024]{2,0,1:T(4,128)(2,1)S(1)} %copy.48), channel_id=1, source_target_pairs={{0,752},{16,0},{32,16},{48,32},{64,48},{80,64},{96,80},{112,96},{1... | collective-permute-start | bytes 884744 | tf_op jit(solution)/shard_map/ppermute | solution.py:12
  14.6 0.7 copy-start.1
  122.1 11.0 %copy-start.2 = (bf16[12,36,1024]{2,1,0:T(8,128)(2,1)S(1)}, bf16[12,36,1024]{2,1,0:T(8,128)(2,1)}, u32[]{:S(2)}) copy-start(bf16[12,36,1024]{2,1,0:T(8,128)(2,1)} %param.2) | copy-start | bytes 2654212
  133.1 8.8 %copy-start = (bf16[48,36,576]{2,0,1:T(8,128)(2,1)S(1)}, bf16[48,36,576]{2,0,1:T(8,128)(2,1)}, u32[]{:S(2)}) copy-start(bf16[48,36,576]{2,0,1:T(8,128)(2,1)} %param.3) | copy-start | bytes 5971972
Sparse Core Ops, SparseCore 0:
  15.5 117.5 all-gather.1
where the time goes:
time: 184 us; the launch traced here: 182 us
  blocking collectives  94.4 us (51%)
  local copies, waits for them, and re-layouts  55.8 us (30%)
  between operations  14.1 us (8%)
  matrix products  10.6 us (6%)
  waiting for transfers between devices  5.35 us (3%)
  starting transfers between devices  1.96 us (1%)
    all_to_all x1, blocking collectives, shards(): lax.all_to_all(amplitudes, 'col', split_axis=2, concat_axis=1, tiled=True)  64.5 us
    unnamed x10, local copies, waits for them, and re-layouts  32.3 us
    all_to_all x1, blocking collectives, sent_to_all(): return lax.all_to_all(copies, axis, split_axis=0, concat_axis=0, tiled=True)  29.9 us
    all_to_all x2, local copies, waits for them, and re-layouts, shards(): lax.all_to_all(amplitudes, 'col', split_axis=2, concat_axis=1, tiled=True)  20.8 us
    dot_general x1, matrix products, form_tile(): jnp.einsum('acq,jdq->ajcd', resident, incoming, preferred_element_type=jn...  8.77 us
    ppermute x1, waiting for transfers between devices, shifted_2(): return lax.ppermute(value, axis, pairs)  4.22 us
  transfers between devices with their start and end apart: 2, of which 2 were waited for; matrix products, arithmetic and copies ran while one was open for 29% of the time, Pallas kernels for 0%

commit v1 on v0

v1 whole, which is shorter than its diff:
```python
import functools

import jax
import jax.numpy as jnp
from jax import lax
from jax.experimental import pallas as pl
from jax.experimental.pallas import tpu as pltpu
from jax.sharding import PartitionSpec as P

WIN = 4
SIDE = 4
LANES = 128
CHUNKS = 6
GROUP = 4
HIGHEST = lax.Precision.HIGHEST
ROWS_BY_ROWS = (((1,), (1,)), ((), ()))


def moved(value, dx, dy):
    pairs = [(yh * SIDE + x, (yh + dy) % SIDE * SIDE + (x + dx) % SIDE) for yh in range(SIDE) for x in range(SIDE)]
    return lax.ppermute(value, "col", pairs)


def from_next_row(value):
    rows = lax.axis_size("row")
    return lax.ppermute(value, "row", [(source, (source - 1) % rows) for source in range(rows)])


def between_cores(value):
    rows = lax.axis_size("row")
    return lax.ppermute(value, "row", [(source, source ^ 1) for source in range(rows)])


def core_0_along_x_core_1_along_y(value, step):
    pairs = []
    for row in range(lax.axis_size("row")):
        for yh in range(SIDE):
            for x in range(SIDE):
                to = (yh, (x + step) % SIDE) if row % 2 == 0 else ((yh + step) % SIDE, x)
                pairs.append((row * SIDE * SIDE + yh * SIDE + x, row * SIDE * SIDE + to[0] * SIDE + to[1]))
    return lax.ppermute(value, ("row", "col"), pairs)


def pack_kernel(own_c, at_ref, amps_ref, sent_ref, own_ref):
    x, yh, core = at_ref[0], at_ref[1], at_ref[2]
    rows, nv = amps_ref.shape
    tail = SIDE * own_c - LANES
    part = rows // CHUNKS

    def source(n, kind, step):
        near, e = n // own_c, n % own_c
        ab = ((yh - near + SIDE) % SIDE) * SIDE + (x + step) % SIDE
        ba = ((yh + step) % SIDE) * SIDE + (x - near + SIDE) % SIDE
        return jnp.where(kind == 0, ab, ba) * own_c + e

    kinds = [(core, 1), (core, 2), (core, 3), (0, 0), (1, 0)]
    lane = lax.broadcasted_iota(jnp.int32, (1, LANES), 1)
    wanted = [source(lane, kind, step) for kind, step in kinds]
    ends = jnp.full((1, LANES), -1, jnp.int32)
    for i, (kind, step) in enumerate(kinds):
        here = (lane >= i * tail) & (lane < (i + 1) * tail)
        ends = jnp.where(here, source(lane - i * tail + LANES, kind, step), ends)
    wanted = jnp.concatenate(wanted + [ends], 1)
    chosen = lax.broadcasted_iota(jnp.int32, (nv, wanted.shape[1]), 0) == wanted
    chosen = jnp.where(chosen, 1.0, 0.0).astype(jnp.bfloat16)

    def one(k, carry):
        at = pl.multiple_of(k * part, 16)
        got = jnp.dot(amps_ref[pl.ds(at, part), :], chosen, preferred_element_type=jnp.float32)
        end = got[:, 5 * LANES :]
        for i in range(3):
            sent_ref[i, pl.ds(at, part), :] = got[:, i * LANES : (i + 1) * LANES].astype(jnp.bfloat16)
        for i in (3, 4):
            own_ref[i - 3, pl.ds(at, part), :LANES] = got[:, i * LANES : (i + 1) * LANES].astype(jnp.bfloat16)
            own_ref[i - 3, pl.ds(at, part), LANES:] = pltpu.roll(end, LANES - i * tail, 1)[:, :tail].astype(jnp.bfloat16)
        new = []
        for i in range(3):
            turned = pltpu.roll(end, (k * tail + LANES - i * tail) % LANES, 1)
            new.append(jnp.where((lane >= k * tail) & (lane < (k + 1) * tail), turned, carry[i]))
        return tuple(new)

    carry = tuple(jnp.zeros((part, LANES), jnp.float32) for _ in range(3))
    for k in range(CHUNKS):
        carry = one(k, carry)
    for i in range(3):
        sent_ref[i, rows:, :] = carry[i].astype(jnp.bfloat16)


def unpack_kernel(core_ref, own_ref, mine_ref, other_ref, ab_ref, ba_ref):
    core = core_ref[0]
    rows = ab_ref.shape[1]
    part = rows // CHUNKS
    tail = ab_ref.shape[2] - LANES

    def put(from_ref, to_ref):
        for s in range(3):
            to_ref[s + 1, :, :LANES] = from_ref[s, :rows, :]
            end = from_ref[s, rows:, :].astype(jnp.float32)
            for k in range(CHUNKS):
                turned = end if k == 0 else pltpu.roll(end, LANES - k * tail, 1)
                to_ref[s + 1, k * part : (k + 1) * part, LANES:] = turned[:, :tail].astype(jnp.bfloat16)

    ab_ref[0] = own_ref[0]
    ba_ref[0] = own_ref[1]

    @pl.when(core == 0)
    def _():
        put(mine_ref, ab_ref)
        put(other_ref, ba_ref)

    @pl.when(core == 1)
    def _():
        put(other_ref, ab_ref)
        put(mine_ref, ba_ref)


def one_hot(shape, row_of, column_of, dtype):
    row = lax.broadcasted_iota(jnp.int32, shape, 0)
    column = lax.broadcasted_iota(jnp.int32, shape, 1)
    return jnp.where(row_of(row) == column_of(column), 1.0, 0.0).astype(dtype)


def ladder_kernel(own_a, own_c, pairs_p, *refs):
    lines, partners = refs[:SIDE], refs[SIDE : 2 * SIDE]
    ab_ref, ba_ref, out_ref, window, tile, total = refs[2 * SIDE :]
    wide = SIDE * own_c
    high = GROUP * own_a
    for j in range(WIN):
        rows = 0.0
        for s in range(SIDE):
            place = one_hot((wide, WIN * own_c), lambda r: r - s * own_c, lambda c: jnp.where((c >= j * own_c) & (c < (j + 1) * own_c), c - j * own_c, -wide - 1), jnp.bfloat16)
            rows += jnp.dot(place, partners[s][...], preferred_element_type=jnp.float32)
        window[j] = rows.astype(jnp.bfloat16)
    total[...] = jnp.zeros_like(total)
    for s in range(SIDE):
        for j in range(WIN):
            v = lax.dot_general(lines[s][...], window[j], ROWS_BY_ROWS, preferred_element_type=jnp.float32)
            tile[:, j] = v.astype(jnp.bfloat16).reshape(own_c // GROUP, high, wide)

        def one(g, carry):
            v = tile[g].reshape(WIN * high, wide)
            at = pl.ds(pl.multiple_of(g * GROUP * pairs_p, 16), GROUP * pairs_p)
            for i, amps in enumerate((ab_ref, ba_ref)):
                total[i] += lax.dot_general(v, amps[s, at, :], ROWS_BY_ROWS, preferred_element_type=jnp.float32)
            return carry

        lax.fori_loop(0, own_c // GROUP, one, 0, unroll=True)
    shape = total.shape[1:]
    row = lax.broadcasted_iota(jnp.int32, shape, 0)
    column = lax.broadcasted_iota(jnp.int32, shape, 1)
    same = (row % high) // own_a == column // pairs_p
    fold = one_hot((own_a * WIN, shape[0]), lambda r: r, lambda c: (c % own_a) * WIN + c // high, jnp.float32)
    out = 0.0
    for i in range(2):
        to = one_hot((shape[1], LANES), lambda r: r % pairs_p + i * pairs_p, lambda c: c, jnp.float32)
        out += jnp.dot(jnp.where(same, total[i], 0.0), to, precision=HIGHEST, preferred_element_type=jnp.float32)
    out_ref[...] = jnp.dot(fold, out, precision=HIGHEST, preferred_element_type=jnp.float32)


def add_kernel(pairs_p, parts_ref, ab_ref, ba_ref):
    total = jnp.sum(parts_ref[...], axis=0)
    ab_ref[...] = total[:, :pairs_p]
    ba_ref[...] = pltpu.roll(total, LANES - pairs_p, 1)[:, :pairs_p]


def shards(df_blocks, amplitudes):
    own_a, own_c, aux = df_blocks.shape
    pairs_p, _, nv = amplitudes.shape
    bf16, f32 = jnp.bfloat16, jnp.float32
    vmem, smem = pl.BlockSpec(memory_space=pltpu.VMEM), pl.BlockSpec(memory_space=pltpu.SMEM)
    params = pltpu.CompilerParams(vmem_limit_bytes=48 * 1024 * 1024)
    rows, wide = own_c * pairs_p, SIDE * own_c
    place, core = lax.axis_index("col"), lax.axis_index("row") % 2
    at = jnp.stack([place % SIDE, place // SIDE, core]).astype(jnp.int32)

    partner = from_next_row(df_blocks[:WIN].reshape(WIN * own_c, aux))
    resident = jnp.transpose(df_blocks, (1, 0, 2)).reshape(own_c * own_a, aux)
    amps = jnp.transpose(amplitudes, (1, 0, 2)).reshape(rows, nv)
    sent, own = pl.pallas_call(
        functools.partial(pack_kernel, own_c),
        out_shape=(jax.ShapeDtypeStruct((3, rows + rows // CHUNKS, LANES), bf16), jax.ShapeDtypeStruct((2, rows, wide), bf16)),
        in_specs=[smem, vmem],
        out_specs=(vmem, vmem),
        compiler_params=params,
        name="pack",
    )(at, amps)
    mine = [core_0_along_x_core_1_along_y(sent[s - 1], s) for s in (1, 3, 2)]
    mine = jnp.stack([mine[0], mine[2], mine[1]])
    lines = [resident] + [moved(resident, s, 0) for s in (1, 2, 3)]
    partners = [partner] + [moved(partner, 0, s) for s in (1, 2, 3)]
    other = between_cores(mine)
    ab, ba = pl.pallas_call(
        unpack_kernel,
        out_shape=(jax.ShapeDtypeStruct((SIDE, rows, wide), bf16),) * 2,
        in_specs=[smem, vmem, vmem, vmem],
        out_specs=(vmem, vmem),
        compiler_params=params,
        name="unpack",
    )(at[2:], own, mine, other)
    ba = jnp.transpose(ba.reshape(wide, pairs_p, wide), (2, 1, 0)).reshape(SIDE, rows, wide)
    part = pl.pallas_call(
        functools.partial(ladder_kernel, own_a, own_c, pairs_p),
        out_shape=jax.ShapeDtypeStruct((own_a * WIN, LANES), f32),
        in_specs=[vmem] * (2 * SIDE + 2),
        out_specs=vmem,
        scratch_shapes=[
            pltpu.VMEM((WIN, wide, aux), bf16),
            pltpu.VMEM((own_c // GROUP, WIN, GROUP * own_a, wide), bf16),
            pltpu.VMEM((2, WIN * GROUP * own_a, GROUP * pairs_p), f32),
        ],
        compiler_params=params,
        name="ladders",
    )(*lines, *partners, ab, ba)
    parts = lax.all_to_all(jnp.broadcast_to(part, (SIDE * SIDE, *part.shape)), "col", 0, 0, tiled=True)
    ab, ba = pl.pallas_call(
        functools.partial(add_kernel, pairs_p),
        out_shape=(jax.ShapeDtypeStruct((own_a * WIN, pairs_p), f32),) * 2,
        in_specs=[vmem],
        out_specs=(vmem, vmem),
        compiler_params=params,
        name="add",
    )(parts)
    return ab.reshape(own_a, WIN, pairs_p), ba.reshape(own_a, WIN, pairs_p)


def solution(mesh):
    in_specs = (P("row", "col", None), P(None, "col", None))
    out_specs = (P("row", None, None), P("row", None, None))
    return jax.shard_map(shards, mesh=mesh, in_specs=in_specs, out_specs=out_specs, check_vma=False)
```

time: 184 us -> 144 us (0.78)
  the two profiles are of different devices: /device:TPU:264 before, /device:TPU:8 now
where the time goes in v1:
time: 144 us; the launch traced here: 143 us
  starting transfers between devices  65.1 us (45%)
  waiting for transfers between devices  22.7 us (16%)
  Pallas kernels  21.3 us (15%)
  local copies, waits for them, and re-layouts  16.7 us (12%)
  blocking collectives  16.1 us (11%)
    ppermute x6, starting transfers between devices, moved(): return lax.ppermute(value, 'col', pairs)  32.2 us
    all_to_all x1, blocking collectives, shards(): lax.all_to_all(jnp.broadcast_to(part, (SIDE * SIDE, *part.shape)), 'col',...  16.1 us
    ppermute x1, starting transfers between devices, from_next_row(): lax.ppermute(value, 'row', [(source, (source - 1) % rows) for source in r...  14.3 us
    pallas_call x1, Pallas kernels, shards(): pl.pallas_call(functools.partial(ladder_kernel, own_a, own_c, pairs_p), o...  12 us
    ppermute x3, waiting for transfers between devices, core_0_along_x_core_1_along_y(): return lax.ppermute(value, ('row', 'col'), pairs)  11.6 us
    ppermute x6, waiting for transfers between devices, moved(): return lax.ppermute(value, 'col', pairs)  11.1 us
    ppermute x3, starting transfers between devices, core_0_along_x_core_1_along_y(): return lax.ppermute(value, ('row', 'col'), pairs)  10.8 us
    reshape x1, local copies, waits for them, and re-layouts, shards(): ba.reshape(wide, pairs_p, wide)  7.91 us
  transfers between devices with their start and end apart: 11, of which 3 were waited for; matrix products, arithmetic and copies ran while one was open for 8% of the time, Pallas kernels for 4%

profile of v1, /device:TPU:8, one launch (start us, length us, event | category | flops | bytes accessed | tf_op | source)
XLA Modules:
  0.0 143.1 jit_solution(12183657167094072010)
XLA Ops:
  0.7 0.1 pad_add_fusion.at_ref
  0.7 0.0 copy-start
  0.7 1.6 %copy-done = bf16[48,36,576]{2,0,1:T(8,128)(2,1)S(1)} copy-done((bf16[48,36,576]{2,0,1:T(8,128)(2,1)S(1)}, bf16[48,36,576]{2,0,1:T(8,128)(2,1)}, u32[]{:S(2)}) %copy-start) | copy-done | bytes 1990680
  2.4 2.9 %pack.1 = (bf16[3,2016,128]{2,1,0:T(8,128)(2,1)S(1)}, bf16[2,1728,144]{2,1,0:T(8,128)(2,1)S(1)}) custom-call(s32[3]{0:T(128)S(1)} %pad_add_fusion.at_ref, bf16[1728,576]{1,0:T(8,128)(2,1)S(1)} %bitcast.22), custom_call_target="tpu_custom_call" | custom-call | tf_op jit(solution)/shard_map/pack/pallas_call | solution.py:179
  5.3 0.0 copy-start.1
  5.3 0.1 slice_bitcast_fusion.2
  5.4 1.1 copy-done.1
  6.6 4.7 %collective-permute-start.9 = (bf16[2016,128]{1,0:T(8,128)(2,1)S(1)}, bf16[2016,128]{1,0:T(8,128)(2,1)S(1)}, u32[]{:S(2)}, u32[]{:S(2)}) collective-permute-start(bf16[2016,128]{1,0:T(8,128)(2,1)S(1)} %get-tuple-element.15), channel_id=1, source_target_pairs={{0,3},{1,0},{2,1},{3,2},{4,7},{5,4},{6,5},{7,6},{8,11},{9,8},{10,9... | collective-permute-start | bytes 1548296 | tf_op jit(solution)/shard_map/ppermute | solution.py:41
  11.2 1.9 %collective-permute-start.7 = (bf16[2016,128]{1,0:T(8,128)(2,1)S(1)}, bf16[2016,128]{1,0:T(8,128)(2,1)S(1)}, u32[]{:S(2)}, u32[]{:S(2)}) collective-permute-start(bf16[2016,128]{1,0:T(8,128)(2,1)S(1)} %get-tuple-element.14), channel_id=1, source_target_pairs={{0,1},{1,2},{2,3},{3,0},{4,5},{5,6},{6,7},{7,4},{8,9},{9,10},{10,1... | collective-permute-start | bytes 1548296 | tf_op jit(solution)/shard_map/ppermute | solution.py:41
  13.1 4.2 %collective-permute-start.8 = (bf16[2016,128]{1,0:T(8,128)(2,1)S(1)}, bf16[2016,128]{1,0:T(8,128)(2,1)S(1)}, u32[]{:S(2)}, u32[]{:S(2)}) collective-permute-start(bf16[2016,128]{1,0:T(8,128)(2,1)S(1)} %get-tuple-element.16), channel_id=1, source_target_pairs={{0,2},{1,3},{2,0},{3,1},{4,6},{5,7},{6,4},{7,5},{8,10},{9,11},{10,... | collective-permute-start | bytes 1548296 | tf_op jit(solution)/shard_map/ppermute | solution.py:41
  17.3 0.5 collective-permute-done.9
  17.8 11.1 %collective-permute-done.7 = bf16[2016,128]{1,0:T(8,128)(2,1)S(1)} collective-permute-done((bf16[2016,128]{1,0:T(8,128)(2,1)S(1)}, bf16[2016,128]{1,0:T(8,128)(2,1)S(1)}, u32[]{:S(2)}, u32[]{:S(2)}) %collective-permute-start.7) | collective-permute-done | bytes 516128 | tf_op jit(solution)/shard_map/ppermute | solution.py:41
  28.9 0.0 collective-permute-done.8
  28.9 0.0 slice-start
  28.9 0.0 copy-start.5
  28.9 0.2 pad_maximum_fusion.mine_ref
  29.1 7.8 %collective-permute-start.10 = (bf16[3,2016,128]{2,1,0:T(8,128)(2,1)S(1)}, bf16[3,2016,128]{2,1,0:T(8,128)(2,1)}, u32[]{:S(2)}, u32[]{:S(2)}) collective-permute-start(bf16[3,2016,128]{2,1,0:T(8,128)(2,1)S(1)} %pad_maximum_fusion.mine_ref), channel_id=1, source_target_pairs={{0,16},{16,0},{32,48},{48,32},{64,80},{80,64},{96,112},{112,96},{1... | collective-permute-start | bytes 4644872 | tf_op jit(solution)/shard_map/ppermute | solution.py:31
  37.0 0.0 slice-done
  37.0 0.8 reshape.26
  37.8 14.3 %collective-permute-start.3 = (bf16[144,1024]{1,0:T(8,128)(2,1)}, bf16[144,1024]{1,0:T(8,128)(2,1)}, u32[]{:S(2)}, u32[]{:S(2)}) collective-permute-start(bf16[144,1024]{1,0:T(8,128)(2,1)} %reshape.26), channel_id=1, source_target_pairs={{0,752},{16,0},{32,16},{48,32},{64,48},{80,64},{96,80},{112,96},{1... | collective-permute-start | bytes 884744 | tf_op jit(solution)/shard_map/ppermute | solution.py:26
  52.0 0.0 copy-done.5
  52.1 1.5 %copy.6 = bf16[36,12,1024]{2,1,0:T(8,128)(2,1)} copy(bf16[36,12,1024]{2,0,1:T(8,128)(2,1)S(1)} %bitcast.25) | data formatting | bytes 1769472 | tf_op jit(solution)/shard_map/transpose | solution.py:177
  53.6 1.3 reshape.25.refs_0_
  55.0 3.4 %collective-permute-start = (bf16[432,1024]{1,0:T(8,128)(2,1)S(1)}, bf16[432,1024]{1,0:T(8,128)(2,1)S(1)}, u32[]{:S(2)}, u32[]{:S(2)}) collective-permute-start(bf16[432,1024]{1,0:T(8,128)(2,1)S(1)} %reshape.25.refs_0_), channel_id=1, source_target_pairs={{0,1},{1,2},{2,3},{3,0},{4,5},{5,6},{6,7},{7,4},{8,9},{9,10},{10,1... | collective-permute-start | bytes 2654216 | tf_op jit(solution)/shard_map/ppermute | solution.py:21
  58.4 4.6 %collective-permute-start.1 = (bf16[432,1024]{1,0:T(8,128)(2,1)S(1)}, bf16[432,1024]{1,0:T(8,128)(2,1)}, u32[]{:S(2)}, u32[]{:S(2)}) collective-permute-start(bf16[432,1024]{1,0:T(8,128)(2,1)S(1)} %reshape.25.refs_0_), channel_id=1, source_target_pairs={{0,2},{1,3},{2,0},{3,1},{4,6},{5,7},{6,4},{7,5},{8,10},{9,11},{10,... | collective-permute-start | bytes 2654216 | tf_op jit(solution)/shard_map/ppermute | solution.py:21
  63.0 3.3 %collective-permute-start.2 = (bf16[432,1024]{1,0:T(8,128)(2,1)S(1)}, bf16[432,1024]{1,0:T(8,128)(2,1)}, u32[]{:S(2)}, u32[]{:S(2)}) collective-permute-start(bf16[432,1024]{1,0:T(8,128)(2,1)S(1)} %reshape.25.refs_0_), channel_id=1, source_target_pairs={{0,3},{1,0},{2,1},{3,2},{4,7},{5,4},{6,5},{7,6},{8,11},{9,8},{10,9... | collective-permute-start | bytes 2654216 | tf_op jit(solution)/shard_map/ppermute | solution.py:21
  66.4 0.0 collective-permute-done.3.refs_4_
  66.4 9.7 %collective-permute-start.4 = (bf16[144,1024]{1,0:T(8,128)(2,1)}, bf16[144,1024]{1,0:T(8,128)(2,1)S(1)}, u32[]{:S(2)}, u32[]{:S(2)}) collective-permute-start(bf16[144,1024]{1,0:T(8,128)(2,1)} %collective-permute-done.3.refs_4_), channel_id=1, source_target_pairs={{0,4},{1,5},{2,6},{3,7},{4,8},{5,9},{6,10},{7,11},{8,12},{9,13},{1... | collective-permute-start | bytes 884744 | tf_op jit(solution)/shard_map/ppermute | solution.py:21
  76.1 11.1 %collective-permute-done.4.refs_5_ = bf16[144,1024]{1,0:T(8,128)(2,1)S(1)} collective-permute-done((bf16[144,1024]{1,0:T(8,128)(2,1)}, bf16[144,1024]{1,0:T(8,128)(2,1)S(1)}, u32[]{:S(2)}, u32[]{:S(2)}) %collective-permute-start.4) | collective-permute-done | bytes 294944 | tf_op jit(solution)/shard_map/ppermute | solution.py:21
  87.2 0.0 copy-start.3
  87.2 0.7 copy-done.3
  88.0 6.9 %collective-permute-start.5 = (bf16[144,1024]{1,0:T(8,128)(2,1)}, bf16[144,1024]{1,0:T(8,128)(2,1)}, u32[]{:S(2)}, u32[]{:S(2)}) collective-permute-start(bf16[144,1024]{1,0:T(8,128)(2,1)} %collective-permute-done.3.refs_4_), channel_id=1, source_target_pairs={{0,8},{1,9},{2,10},{3,11},{4,12},{5,13},{6,14},{7,15},{8,0},{9,1},... | collective-permute-start | bytes 884744 | tf_op jit(solution)/shard_map/ppermute | solution.py:21
  94.8 0.0 collective-permute-done.10.other_ref
  94.9 4.2 %collective-permute-start.6 = (bf16[144,1024]{1,0:T(8,128)(2,1)}, bf16[144,1024]{1,0:T(8,128)(2,1)}, u32[]{:S(2)}, u32[]{:S(2)}) collective-permute-start(bf16[144,1024]{1,0:T(8,128)(2,1)} %collective-permute-done.3.refs_4_), channel_id=1, source_target_pairs={{0,12},{1,13},{2,14},{3,15},{4,0},{5,1},{6,2},{7,3},{8,4},{9,5},{1... | collective-permute-start | bytes 884744 | tf_op jit(solution)/shard_map/ppermute | solution.py:21
  99.1 0.0 copy-start.2
  99.1 1.5 %copy-done.2 = bf16[2,1728,144]{2,1,0:T(8,128)(2,1)S(1)} copy-done((bf16[2,1728,144]{2,1,0:T(8,128)(2,1)S(1)}, bf16[2,1728,144]{2,1,0:T(8,128)(2,1)}, u32[]{:S(2)}) %copy-start.2) | copy-done | bytes 995352
  100.5 5.7 %unpack.1 = (bf16[4,1728,144]{2,1,0:T(8,128)(2,1)}, bf16[4,1728,144]{2,1,0:T(8,128)(2,1)}) custom-call(s32[1]{0:T(128)} %bitcast.1.core_ref, bf16[2,1728,144]{2,1,0:T(8,128)(2,1)S(1)} %copy-done.2, bf16[3,2016,128]{2,1,0:T(8,128)(2,1)S(1)} %pad_maximum_fusion.mine_ref, bf16[3,2016,128]{2,1,0:T(8,128)(2,1)} %collective-permute-done.10.other_ref), custom_call_target="tpu_custom_call" | custom-call | tf_op jit(solution)/shard_map/unpack/pallas_call | solution.py:192
  106.2 0.0 copy-start.4
  106.2 7.9 %copy.7 = bf16[144,48,144]{0,1,2:T(8,128)(2,1)} copy(bf16[144,48,144]{2,1,0:T(8,128)(2,1)} %bitcast.24) | data formatting | bytes 3981312 | tf_op jit(solution)/shard_map/reshape | solution.py:200
  114.1 0.0 collective-permute-done.5.refs_6_
  114.1 0.0 collective-permute-done.6.refs_7_
  114.1 0.0 collective-permute-done.refs_1_
  114.1 0.0 collective-permute-done.1.refs_2_
  114.1 0.0 collective-permute-done.2.refs_3_
  114.2 0.0 copy-done.4
  114.2 12.0 %ladders.1 = f32[48,128]{1,0:T(8,128)S(1)} custom-call(bf16[432,1024]{1,0:T(8,128)(2,1)S(1)} %reshape.25.refs_0_, bf16[432,1024]{1,0:T(8,128)(2,1)S(1)} %collective-permute-done.refs_1_, bf16[432,1024]{1,0:T(8,128)(2,1)} %collective-permute-done.1.refs_2_, bf16[432,1024]{1,0:T(8,128)(2,1)} %collective-permute-done.2.refs_3_, ...), custom_call_target="tpu_custom_call" | custom-call | tf_op jit(solution)/shard_map/ladders/pallas_call | solution.py:201
  126.2 16.1 %all_to_all.5.parts_ref = f32[16,48,128]{2,1,0:T(8,128)S(1)} all-to-all(f32[16,48,128]{2,1,0:T(8,128)S(1)} %broadcast_in_dim.3), channel_id=1, replica_groups=mesh['row'=48,'col'=16] {'col'}, dimensions={0} | all-to-all | bytes 786432 | tf_op jit(solution)/shard_map/all_to_all | solution.py:214
  142.4 0.7 add.15
  (1 shorter events, 0.0 us)
Async XLA Ops:
  0.7 1.6 %copy-start = (bf16[48,36,576]{2,0,1:T(8,128)(2,1)S(1)}, bf16[48,36,576]{2,0,1:T(8,128)(2,1)}, u32[]{:S(2)}) copy-start(bf16[48,36,576]{2,0,1:T(8,128)(2,1)} %param.3) | copy-start | bytes 5971972
  5.3 1.2 copy-start.1
  6.6 11.3 %collective-permute-start.9 = (bf16[2016,128]{1,0:T(8,128)(2,1)S(1)}, bf16[2016,128]{1,0:T(8,128)(2,1)S(1)}, u32[]{:S(2)}, u32[]{:S(2)}) collective-permute-start(bf16[2016,128]{1,0:T(8,128)(2,1)S(1)} %get-tuple-element.15), channel_id=1, source_target_pairs={{0,3},{1,0},{2,1},{3,2},{4,7},{5,4},{6,5},{7,6},{8,11},{9,8},{10,9... | collective-permute-start | bytes 1548296 | tf_op jit(solution)/shard_map/ppermute | solution.py:41
  11.2 17.7 %collective-permute-start.7 = (bf16[2016,128]{1,0:T(8,128)(2,1)S(1)}, bf16[2016,128]{1,0:T(8,128)(2,1)S(1)}, u32[]{:S(2)}, u32[]{:S(2)}) collective-permute-start(bf16[2016,128]{1,0:T(8,128)(2,1)S(1)} %get-tuple-element.14), channel_id=1, source_target_pairs={{0,1},{1,2},{2,3},{3,0},{4,5},{5,6},{6,7},{7,4},{8,9},{9,10},{10,1... | collective-permute-start | bytes 1548296 | tf_op jit(solution)/shard_map/ppermute | solution.py:41
  13.1 15.8 %collective-permute-start.8 = (bf16[2016,128]{1,0:T(8,128)(2,1)S(1)}, bf16[2016,128]{1,0:T(8,128)(2,1)S(1)}, u32[]{:S(2)}, u32[]{:S(2)}) collective-permute-start(bf16[2016,128]{1,0:T(8,128)(2,1)S(1)} %get-tuple-element.16), channel_id=1, source_target_pairs={{0,2},{1,3},{2,0},{3,1},{4,6},{5,7},{6,4},{7,5},{8,10},{9,11},{10,... | collective-permute-start | bytes 1548296 | tf_op jit(solution)/shard_map/ppermute | solution.py:41
  28.9 8.0 %slice-start = ((bf16[12,36,1024]{2,1,0:T(8,128)(2,1)}), bf16[4,36,1024]{2,1,0:T(8,128)(2,1)S(1)}, s32[]{:S(2)}) async-start(bf16[12,36,1024]{2,1,0:T(8,128)(2,1)} %param.2), calls=%async_computation.1 | async-start | bytes 655360 | tf_op jit(solution)/shard_map/slice | solution.py:176
  28.9 23.1 %copy-start.5 = (bf16[12,36,1024]{2,1,0:T(8,128)(2,1)S(1)}, bf16[12,36,1024]{2,1,0:T(8,128)(2,1)}, u32[]{:S(2)}) copy-start(bf16[12,36,1024]{2,1,0:T(8,128)(2,1)} %param.2) | copy-start | bytes 2654212
  29.1 65.7 %collective-permute-start.10 = (bf16[3,2016,128]{2,1,0:T(8,128)(2,1)S(1)}, bf16[3,2016,128]{2,1,0:T(8,128)(2,1)}, u32[]{:S(2)}, u32[]{:S(2)}) collective-permute-start(bf16[3,2016,128]{2,1,0:T(8,128)(2,1)S(1)} %pad_maximum_fusion.mine_ref), channel_id=1, source_target_pairs={{0,16},{16,0},{32,48},{48,32},{64,80},{80,64},{96,112},{112,96},{1... | collective-permute-start | bytes 4644872 | tf_op jit(solution)/shard_map/ppermute | solution.py:31
  37.8 28.6 %collective-permute-start.3 = (bf16[144,1024]{1,0:T(8,128)(2,1)}, bf16[144,1024]{1,0:T(8,128)(2,1)}, u32[]{:S(2)}, u32[]{:S(2)}) collective-permute-start(bf16[144,1024]{1,0:T(8,128)(2,1)} %reshape.26), channel_id=1, source_target_pairs={{0,752},{16,0},{32,16},{48,32},{64,48},{80,64},{96,80},{112,96},{1... | collective-permute-start | bytes 884744 | tf_op jit(solution)/shard_map/ppermute | solution.py:26
  55.0 59.2 %collective-permute-start = (bf16[432,1024]{1,0:T(8,128)(2,1)S(1)}, bf16[432,1024]{1,0:T(8,128)(2,1)S(1)}, u32[]{:S(2)}, u32[]{:S(2)}) collective-permute-start(bf16[432,1024]{1,0:T(8,128)(2,1)S(1)} %reshape.25.refs_0_), channel_id=1, source_target_pairs={{0,1},{1,2},{2,3},{3,0},{4,5},{5,6},{6,7},{7,4},{8,9},{9,10},{10,1... | collective-permute-start | bytes 2654216 | tf_op jit(solution)/shard_map/ppermute | solution.py:21
  58.4 55.8 %collective-permute-start.1 = (bf16[432,1024]{1,0:T(8,128)(2,1)S(1)}, bf16[432,1024]{1,0:T(8,128)(2,1)}, u32[]{:S(2)}, u32[]{:S(2)}) collective-permute-start(bf16[432,1024]{1,0:T(8,128)(2,1)S(1)} %reshape.25.refs_0_), channel_id=1, source_target_pairs={{0,2},{1,3},{2,0},{3,1},{4,6},{5,7},{6,4},{7,5},{8,10},{9,11},{10,... | collective-permute-start | bytes 2654216 | tf_op jit(solution)/shard_map/ppermute | solution.py:21
  63.0 51.1 %collective-permute-start.2 = (bf16[432,1024]{1,0:T(8,128)(2,1)S(1)}, bf16[432,1024]{1,0:T(8,128)(2,1)}, u32[]{:S(2)}, u32[]{:S(2)}) collective-permute-start(bf16[432,1024]{1,0:T(8,128)(2,1)S(1)} %reshape.25.refs_0_), channel_id=1, source_target_pairs={{0,3},{1,0},{2,1},{3,2},{4,7},{5,4},{6,5},{7,6},{8,11},{9,8},{10,9... | collective-permute-start | bytes 2654216 | tf_op jit(solution)/shard_map/ppermute | solution.py:21
  66.4 20.9 %collective-permute-start.4 = (bf16[144,1024]{1,0:T(8,128)(2,1)}, bf16[144,1024]{1,0:T(8,128)(2,1)S(1)}, u32[]{:S(2)}, u32[]{:S(2)}) collective-permute-start(bf16[144,1024]{1,0:T(8,128)(2,1)} %collective-permute-done.3.refs_4_), channel_id=1, source_target_pairs={{0,4},{1,5},{2,6},{3,7},{4,8},{5,9},{6,10},{7,11},{8,12},{9,13},{1... | collective-permute-start | bytes 884744 | tf_op jit(solution)/shard_map/ppermute | solution.py:21
  87.2 0.7 copy-start.3
  88.0 26.2 %collective-permute-start.5 = (bf16[144,1024]{1,0:T(8,128)(2,1)}, bf16[144,1024]{1,0:T(8,128)(2,1)}, u32[]{:S(2)}, u32[]{:S(2)}) collective-permute-start(bf16[144,1024]{1,0:T(8,128)(2,1)} %collective-permute-done.3.refs_4_), channel_id=1, source_target_pairs={{0,8},{1,9},{2,10},{3,11},{4,12},{5,13},{6,14},{7,15},{8,0},{9,1},... | collective-permute-start | bytes 884744 | tf_op jit(solution)/shard_map/ppermute | solution.py:21
  94.9 19.3 %collective-permute-start.6 = (bf16[144,1024]{1,0:T(8,128)(2,1)}, bf16[144,1024]{1,0:T(8,128)(2,1)}, u32[]{:S(2)}, u32[]{:S(2)}) collective-permute-start(bf16[144,1024]{1,0:T(8,128)(2,1)} %collective-permute-done.3.refs_4_), channel_id=1, source_target_pairs={{0,12},{1,13},{2,14},{3,15},{4,0},{5,1},{6,2},{7,3},{8,4},{9,5},{1... | collective-permute-start | bytes 884744 | tf_op jit(solution)/shard_map/ppermute | solution.py:21
  99.1 1.5 %copy-start.2 = (bf16[2,1728,144]{2,1,0:T(8,128)(2,1)S(1)}, bf16[2,1728,144]{2,1,0:T(8,128)(2,1)}, u32[]{:S(2)}) copy-start(bf16[2,1728,144]{2,1,0:T(8,128)(2,1)} %copy-done.1) | copy-start | bytes 2985988
  106.2 7.9 %copy-start.4 = (bf16[144,1024]{1,0:T(8,128)(2,1)S(1)}, bf16[144,1024]{1,0:T(8,128)(2,1)}, u32[]{:S(2)}) copy-start(bf16[144,1024]{1,0:T(8,128)(2,1)} %copy-done.3) | copy-start | bytes 884740

commit v2 on v1

--- a/solution.py
+++ b/solution.py
@@ -17,8 +17,19 @@
 
 
 def moved(value, dx, dy):
-    pairs = [(yh * SIDE + x, (yh + dy) % SIDE * SIDE + (x + dx) % SIDE) for yh in range(SIDE) for x in range(SIDE)]
-    return lax.ppermute(value, "col", pairs)
+    pairs = []
+    for row in range(lax.axis_size("row")):
+        sign = 1 - 2 * (row % 2)
+        for yh in range(SIDE):
+            for x in range(SIDE):
+                to = (yh + sign * dy) % SIDE * SIDE + (x + sign * dx) % SIDE
+                pairs.append(((row * SIDE + yh) * SIDE + x, row * SIDE * SIDE + to))
+    return lax.ppermute(value, ("row", "col"), pairs)
+
+
+def gathered(value, dx, dy):
+    first = moved(value, dx, dy)
+    return [value, first, moved(first, dx, dy), moved(value, -dx, -dy)]
 
 
 def from_next_row(value):
@@ -41,7 +52,7 @@
     return lax.ppermute(value, ("row", "col"), pairs)
 
 
-def pack_kernel(own_c, at_ref, amps_ref, sent_ref, own_ref):
+def pack_kernel(own_c, at_ref, amps_ref, before_1, before_2, sent_ref, own_ref):
     x, yh, core = at_ref[0], at_ref[1], at_ref[2]
     rows, nv = amps_ref.shape
     tail = SIDE * own_c - LANES
@@ -114,13 +125,21 @@
         put(mine_ref, ba_ref)
 
 
+def join_kernel(first, second, third, *rest):
+    out_ref = rest[-1]
+    for i, ref in enumerate((first, second, third)):
+        out_ref[i] = ref[...]
+
+
 def one_hot(shape, row_of, column_of, dtype):
     row = lax.broadcasted_iota(jnp.int32, shape, 0)
     column = lax.broadcasted_iota(jnp.int32, shape, 1)
     return jnp.where(row_of(row) == column_of(column), 1.0, 0.0).astype(dtype)
 
 
-def ladder_kernel(own_a, own_c, pairs_p, *refs):
+def ladder_kernel(own_a, own_c, pairs_p, core_ref, *refs):
+    core = core_ref[0]
+    distance = (0, 1 + 2 * core, 2, 3 - 2 * core)
     lines, partners = refs[:SIDE], refs[SIDE : 2 * SIDE]
     ab_ref, ba_ref, out_ref, window, tile, total = refs[2 * SIDE :]
     wide = SIDE * own_c
@@ -128,7 +147,7 @@
     for j in range(WIN):
         rows = 0.0
         for s in range(SIDE):
-            place = one_hot((wide, WIN * own_c), lambda r: r - s * own_c, lambda c: jnp.where((c >= j * own_c) & (c < (j + 1) * own_c), c - j * own_c, -wide - 1), jnp.bfloat16)
+            place = one_hot((wide, WIN * own_c), lambda r: r - distance[s] * own_c, lambda c: jnp.where((c >= j * own_c) & (c < (j + 1) * own_c), c - j * own_c, -wide - 1), jnp.bfloat16)
             rows += jnp.dot(place, partners[s][...], preferred_element_type=jnp.float32)
         window[j] = rows.astype(jnp.bfloat16)
     total[...] = jnp.zeros_like(total)
@@ -141,7 +160,7 @@
             v = tile[g].reshape(WIN * high, wide)
             at = pl.ds(pl.multiple_of(g * GROUP * pairs_p, 16), GROUP * pairs_p)
             for i, amps in enumerate((ab_ref, ba_ref)):
-                total[i] += lax.dot_general(v, amps[s, at, :], ROWS_BY_ROWS, preferred_element_type=jnp.float32)
+                total[i] += lax.dot_general(v, amps[distance[s], at, :], ROWS_BY_ROWS, preferred_element_type=jnp.float32)
             return carry
 
         lax.fori_loop(0, own_c // GROUP, one, 0, unroll=True)
@@ -167,7 +186,7 @@
     own_a, own_c, aux = df_blocks.shape
     pairs_p, _, nv = amplitudes.shape
     bf16, f32 = jnp.bfloat16, jnp.float32
-    vmem, smem = pl.BlockSpec(memory_space=pltpu.VMEM), pl.BlockSpec(memory_space=pltpu.SMEM)
+    vmem, smem, hbm = pl.BlockSpec(memory_space=pltpu.VMEM), pl.BlockSpec(memory_space=pltpu.SMEM), pl.BlockSpec(memory_space=pl.ANY)
     params = pltpu.CompilerParams(vmem_limit_bytes=48 * 1024 * 1024)
     rows, wide = own_c * pairs_p, SIDE * own_c
     place, core = lax.axis_index("col"), lax.axis_index("row") % 2
@@ -179,15 +198,22 @@
     sent, own = pl.pallas_call(
         functools.partial(pack_kernel, own_c),
         out_shape=(jax.ShapeDtypeStruct((3, rows + rows // CHUNKS, LANES), bf16), jax.ShapeDtypeStruct((2, rows, wide), bf16)),
-        in_specs=[smem, vmem],
+        in_specs=[smem, vmem, hbm, hbm],
         out_specs=(vmem, vmem),
         compiler_params=params,
         name="pack",
-    )(at, amps)
-    mine = [core_0_along_x_core_1_along_y(sent[s - 1], s) for s in (1, 3, 2)]
-    mine = jnp.stack([mine[0], mine[2], mine[1]])
-    lines = [resident] + [moved(resident, s, 0) for s in (1, 2, 3)]
-    partners = [partner] + [moved(partner, 0, s) for s in (1, 2, 3)]
+    )(at, amps, partner, resident)
+    lines = gathered(resident, 1, 0)
+    mine = [core_0_along_x_core_1_along_y(sent[s - 1], s) for s in (1, 2, 3)]
+    partners = gathered(partner, 0, 1)
+    mine = pl.pallas_call(
+        join_kernel,
+        out_shape=jax.ShapeDtypeStruct(sent.shape, bf16),
+        in_specs=[vmem] * 3 + [hbm] * 4,
+        out_specs=vmem,
+        compiler_params=params,
+        name="join",
+    )(*mine, lines[1], lines[3], partners[1], partners[3])
     other = between_cores(mine)
     ab, ba = pl.pallas_call(
         unpack_kernel,
@@ -201,7 +227,7 @@
     part = pl.pallas_call(
         functools.partial(ladder_kernel, own_a, own_c, pairs_p),
         out_shape=jax.ShapeDtypeStruct((own_a * WIN, LANES), f32),
-        in_specs=[vmem] * (2 * SIDE + 2),
+        in_specs=[smem] + [vmem] * (2 * SIDE + 2),
         out_specs=vmem,
         scratch_shapes=[
             pltpu.VMEM((WIN, wide, aux), bf16),
@@ -210,7 +236,7 @@
         ],
         compiler_params=params,
         name="ladders",
-    )(*lines, *partners, ab, ba)
+    )(at[2:], *lines, *partners, ab, ba)
     parts = lax.all_to_all(jnp.broadcast_to(part, (SIDE * SIDE, *part.shape)), "col", 0, 0, tiled=True)
     ab, ba = pl.pallas_call(
         functools.partial(add_kernel, pairs_p),

time: 144 us -> 129 us (0.90)
  the two profiles are of different devices: /device:TPU:8 before, /device:TPU:1 now
where the time goes in v2:
time: 129 us
  starting transfers between devices  54.5 us (42%)
  waiting for transfers between devices  23.3 us (18%)
  Pallas kernels  20.7 us (16%)
  blocking collectives  18.4 us (14%)
  local copies, waits for them, and re-layouts  11 us (9%)
    ppermute x3, waiting for transfers between devices, core_0_along_x_core_1_along_y(): return lax.ppermute(value, ('row', 'col'), pairs)  23.3 us
    ppermute x6, starting transfers between devices, moved(): return lax.ppermute(value, ('row', 'col'), pairs)  21.2 us
    all_to_all x1, blocking collectives, shards(): lax.all_to_all(jnp.broadcast_to(part, (SIDE * SIDE, *part.shape)), 'col',...  18.4 us
    ppermute x1, starting transfers between devices, from_next_row(): lax.ppermute(value, 'row', [(source, (source - 1) % rows) for source in r...  12.4 us
    pallas_call x1, Pallas kernels, shards(): pl.pallas_call(functools.partial(ladder_kernel, own_a, own_c, pairs_p), o...  11.6 us
    ppermute x1, starting transfers between devices, between_cores(): lax.ppermute(value, 'row', [(source, source ^ 1) for source in range(rows)])  11.5 us
    ppermute x3, starting transfers between devices, core_0_along_x_core_1_along_y(): return lax.ppermute(value, ('row', 'col'), pairs)  9.31 us
    reshape x1, local copies, waits for them, and re-layouts, shards(): ba.reshape(wide, pairs_p, wide)  7.9 us
  transfers between devices with their start and end apart: 11, of which 3 were waited for; matrix products, arithmetic and copies ran while one was open for 8% of the time, Pallas kernels for 6%

profile of v2, /device:TPU:1, one launch (start us, length us, event | category | flops | bytes accessed | tf_op | source)
XLA Modules:
  0.0 128.8 jit_solution(5311008945808450135)
XLA Ops:
  0.6 1.0 slice.12
  1.6 0.1 reshape.26
  1.7 12.4 %collective-permute-start.3 = (bf16[144,1024]{1,0:T(8,128)(2,1)S(1)}, bf16[144,1024]{1,0:T(8,128)(2,1)S(1)}, u32[]{:S(2)}, u32[]{:S(2)}) collective-permute-start(bf16[144,1024]{1,0:T(8,128)(2,1)S(1)} %reshape.26), channel_id=1, source_target_pairs={{0,752},{16,0},{32,16},{48,32},{64,48},{80,64},{96,80},{112,96},{1... | collective-permute-start | bytes 884744 | tf_op jit(solution)/shard_map/ppermute | solution.py:37
  14.1 1.7 %copy.6 = bf16[36,12,1024]{2,1,0:T(8,128)(2,1)S(1)} copy(bf16[36,12,1024]{2,0,1:T(8,128)(2,1)} %bitcast.22) | data formatting | bytes 1769472 | tf_op jit(solution)/shard_map/transpose | solution.py:196
  15.8 0.2 reshape.25.before_2.refs_0_
  16.0 1.9 %collective-permute-start = (bf16[432,1024]{1,0:T(8,128)(2,1)S(1)}, bf16[432,1024]{1,0:T(8,128)(2,1)S(1)}, u32[]{:S(2)}, u32[]{:S(2)}) collective-permute-start(bf16[432,1024]{1,0:T(8,128)(2,1)S(1)} %reshape.25.before_2.refs_0_), channel_id=1, source_target_pairs={{0,1},{1,2},{2,3},{3,0},{4,5},{5,6},{6,7},{7,4},{8,9},{9,10},{10,1... | collective-permute-start | bytes 2654216 | tf_op jit(solution)/shard_map/ppermute | solution.py:27
  18.0 3.4 %collective-permute-start.2 = (bf16[432,1024]{1,0:T(8,128)(2,1)S(1)}, bf16[432,1024]{1,0:T(8,128)(2,1)S(1)}, u32[]{:S(2)}, u32[]{:S(2)}) collective-permute-start(bf16[432,1024]{1,0:T(8,128)(2,1)S(1)} %reshape.25.before_2.refs_0_), channel_id=1, source_target_pairs={{0,3},{1,0},{2,1},{3,2},{4,7},{5,4},{6,5},{7,6},{8,11},{9,8},{10,9... | collective-permute-start | bytes 2654216 | tf_op jit(solution)/shard_map/ppermute | solution.py:27
  21.4 0.1 pad_add_fusion.at_ref
  21.5 0.0 collective-permute-done.3.before_1.refs_4_
  21.5 1.9 %collective-permute-start.4 = (bf16[144,1024]{1,0:T(8,128)(2,1)S(1)}, bf16[144,1024]{1,0:T(8,128)(2,1)S(1)}, u32[]{:S(2)}, u32[]{:S(2)}) collective-permute-start(bf16[144,1024]{1,0:T(8,128)(2,1)S(1)} %collective-permute-done.3.before_1.refs_4_), channel_id=1, source_target_pairs={{0,4},{1,5},{2,6},{3,7},{4,8},{5,9},{6,10},{7,11},{8,12},{9,13},{1... | collective-permute-start | bytes 884744 | tf_op jit(solution)/shard_map/ppermute | solution.py:27
  23.4 4.3 %collective-permute-start.6 = (bf16[144,1024]{1,0:T(8,128)(2,1)S(1)}, bf16[144,1024]{1,0:T(8,128)(2,1)S(1)}, u32[]{:S(2)}, u32[]{:S(2)}) collective-permute-start(bf16[144,1024]{1,0:T(8,128)(2,1)S(1)} %collective-permute-done.3.before_1.refs_4_), channel_id=1, source_target_pairs={{0,12},{1,13},{2,14},{3,15},{4,0},{5,1},{6,2},{7,3},{8,4},{9,5},{1... | collective-permute-start | bytes 884744 | tf_op jit(solution)/shard_map/ppermute | solution.py:27
  27.6 4.0 %pack.1 = (bf16[3,2016,128]{2,1,0:T(8,128)(2,1)S(1)}, bf16[2,1728,144]{2,1,0:T(8,128)(2,1)S(1)}) custom-call(s32[3]{0:T(128)S(1)} %pad_add_fusion.at_ref, bf16[1728,576]{1,0:T(8,128)(2,1)} %bitcast.21, bf16[144,1024]{1,0:T(8,128)(2,1)S(1)} %collective-permute-done.3.before_1.refs_4_, bf16[432,1024]{1,0:T(8,128)(2,1)S(1)} %reshape.25.before_2.refs_0_), custom_call_target="tpu_custom_call" | custom-call | tf_op jit(solution)/shard_map/pack/pallas_call | solution.py:198
  31.7 0.1 slice_bitcast_fusion
  31.8 1.9 %collective-permute-start.7 = (bf16[2016,128]{1,0:T(8,128)(2,1)S(1)}, bf16[2016,128]{1,0:T(8,128)(2,1)S(1)}, u32[]{:S(2)}, u32[]{:S(2)}) collective-permute-start(bf16[2016,128]{1,0:T(8,128)(2,1)S(1)} %get-tuple-element.16), channel_id=1, source_target_pairs={{0,1},{1,2},{2,3},{3,0},{4,5},{5,6},{6,7},{7,4},{8,9},{9,10},{10,1... | collective-permute-start | bytes 1548296 | tf_op jit(solution)/shard_map/ppermute | solution.py:52
  33.7 0.0 collective-permute-done.4.rest_2_.refs_5_
  33.7 5.2 %collective-permute-start.8 = (bf16[2016,128]{1,0:T(8,128)(2,1)S(1)}, bf16[2016,128]{1,0:T(8,128)(2,1)S(1)}, u32[]{:S(2)}, u32[]{:S(2)}) collective-permute-start(bf16[2016,128]{1,0:T(8,128)(2,1)S(1)} %get-tuple-element.15), channel_id=1, source_target_pairs={{0,2},{1,3},{2,0},{3,1},{4,6},{5,7},{6,4},{7,5},{8,10},{9,11},{10,... | collective-permute-start | bytes 1548296 | tf_op jit(solution)/shard_map/ppermute | solution.py:52
  38.9 0.0 collective-permute-done.6.rest_3_.refs_7_
  38.9 2.2 %collective-permute-start.9 = (bf16[2016,128]{1,0:T(8,128)(2,1)S(1)}, bf16[2016,128]{1,0:T(8,128)(2,1)S(1)}, u32[]{:S(2)}, u32[]{:S(2)}) collective-permute-start(bf16[2016,128]{1,0:T(8,128)(2,1)S(1)} %get-tuple-element.14), channel_id=1, source_target_pairs={{0,3},{1,0},{2,1},{3,2},{4,7},{5,4},{6,5},{7,6},{8,11},{9,8},{10,9... | collective-permute-start | bytes 1548296 | tf_op jit(solution)/shard_map/ppermute | solution.py:52
  41.1 9.4 %collective-permute-done.7.first = bf16[2016,128]{1,0:T(8,128)(2,1)S(1)} collective-permute-done((bf16[2016,128]{1,0:T(8,128)(2,1)S(1)}, bf16[2016,128]{1,0:T(8,128)(2,1)S(1)}, u32[]{:S(2)}, u32[]{:S(2)}) %collective-permute-start.7) | collective-permute-done | bytes 516128 | tf_op jit(solution)/shard_map/ppermute | solution.py:52
  50.5 12.7 %collective-permute-done.8.second = bf16[2016,128]{1,0:T(8,128)(2,1)S(1)} collective-permute-done((bf16[2016,128]{1,0:T(8,128)(2,1)S(1)}, bf16[2016,128]{1,0:T(8,128)(2,1)S(1)}, u32[]{:S(2)}, u32[]{:S(2)}) %collective-permute-start.8) | collective-permute-done | bytes 516128 | tf_op jit(solution)/shard_map/ppermute | solution.py:52
  63.2 1.3 collective-permute-done.9.third
  64.4 0.0 collective-permute-done.rest_0_.refs_1_
  64.4 0.0 collective-permute-done.2.rest_1_.refs_3_
  64.4 0.1 join.1.mine_ref
  64.5 11.5 %collective-permute-start.10 = (bf16[3,2016,128]{2,1,0:T(8,128)(2,1)S(1)}, bf16[3,2016,128]{2,1,0:T(8,128)(2,1)S(1)}, u32[]{:S(2)}, u32[]{:S(2)}) collective-permute-start(bf16[3,2016,128]{2,1,0:T(8,128)(2,1)S(1)} %join.1.mine_ref), channel_id=1, source_target_pairs={{0,16},{16,0},{32,48},{48,32},{64,80},{80,64},{96,112},{112,96},{1... | collective-permute-start | bytes 4644872 | tf_op jit(solution)/shard_map/ppermute | solution.py:42
  76.1 5.3 %collective-permute-start.1 = (bf16[432,1024]{1,0:T(8,128)(2,1)S(1)}, bf16[432,1024]{1,0:T(8,128)(2,1)}, u32[]{:S(2)}, u32[]{:S(2)}) collective-permute-start(bf16[432,1024]{1,0:T(8,128)(2,1)S(1)} %collective-permute-done.rest_0_.refs_1_), channel_id=1, source_target_pairs={{0,1},{1,2},{2,3},{3,0},{4,5},{5,6},{6,7},{7,4},{8,9},{9,10},{10,1... | collective-permute-start | bytes 2654216 | tf_op jit(solution)/shard_map/ppermute | solution.py:27
  81.4 4.4 %collective-permute-start.5 = (bf16[144,1024]{1,0:T(8,128)(2,1)S(1)}, bf16[144,1024]{1,0:T(8,128)(2,1)}, u32[]{:S(2)}, u32[]{:S(2)}) collective-permute-start(bf16[144,1024]{1,0:T(8,128)(2,1)S(1)} %collective-permute-done.4.rest_2_.refs_5_), channel_id=1, source_target_pairs={{0,4},{1,5},{2,6},{3,7},{4,8},{5,9},{6,10},{7,11},{8,12},{9,13},{1... | collective-permute-start | bytes 884744 | tf_op jit(solution)/shard_map/ppermute | solution.py:27
  85.8 0.0 collective-permute-done.10.other_ref
  85.9 4.3 %unpack.1 = (bf16[4,1728,144]{2,1,0:T(8,128)(2,1)}, bf16[4,1728,144]{2,1,0:T(8,128)(2,1)}) custom-call(s32[1]{0:T(128)} %bitcast.core_ref, bf16[2,1728,144]{2,1,0:T(8,128)(2,1)S(1)} %get-tuple-element.8.own_ref, bf16[3,2016,128]{2,1,0:T(8,128)(2,1)S(1)} %join.1.mine_ref, bf16[3,2016,128]{2,1,0:T(8,128)(2,1)S(1)} %collective-permute-done.10.other_ref), custom_call_target="tpu_custom_call" | custom-call | tf_op jit(solution)/shard_map/unpack/pallas_call | solution.py:218
  90.1 7.9 %copy.7 = bf16[144,48,144]{0,1,2:T(8,128)(2,1)} copy(bf16[144,48,144]{2,1,0:T(8,128)(2,1)} %bitcast.20) | data formatting | bytes 3981312 | tf_op jit(solution)/shard_map/reshape | solution.py:226
  98.0 0.0 collective-permute-done.5.refs_6_
  98.0 0.0 collective-permute-done.1.refs_2_
  98.0 11.6 %ladders.1 = f32[48,128]{1,0:T(8,128)S(1)} custom-call(s32[1]{0:T(128)} %bitcast.core_ref, bf16[432,1024]{1,0:T(8,128)(2,1)S(1)} %reshape.25.before_2.refs_0_, bf16[432,1024]{1,0:T(8,128)(2,1)S(1)} %collective-permute-done.rest_0_.refs_1_, bf16[432,1024]{1,0:T(8,128)(2,1)} %collective-permute-done.1.refs_2_, ...), custom_call_target="tpu_custom_call" | custom-call | tf_op jit(solution)/shard_map/ladders/pallas_call | solution.py:227
  109.7 18.4 %all_to_all.5.parts_ref = f32[16,48,128]{2,1,0:T(8,128)S(1)} all-to-all(f32[16,48,128]{2,1,0:T(8,128)S(1)} %broadcast_in_dim.3), channel_id=1, replica_groups=mesh['row'=48,'col'=16] {'col'}, dimensions={0} | all-to-all | bytes 786432 | tf_op jit(solution)/shard_map/all_to_all | solution.py:240
  128.0 0.7 add.15
  (1 shorter events, 0.0 us)
Async XLA Ops:
  1.7 19.8 %collective-permute-start.3 = (bf16[144,1024]{1,0:T(8,128)(2,1)S(1)}, bf16[144,1024]{1,0:T(8,128)(2,1)S(1)}, u32[]{:S(2)}, u32[]{:S(2)}) collective-permute-start(bf16[144,1024]{1,0:T(8,128)(2,1)S(1)} %reshape.26), channel_id=1, source_target_pairs={{0,752},{16,0},{32,16},{48,32},{64,48},{80,64},{96,80},{112,96},{1... | collective-permute-start | bytes 884744 | tf_op jit(solution)/shard_map/ppermute | solution.py:37
  16.0 48.4 %collective-permute-start = (bf16[432,1024]{1,0:T(8,128)(2,1)S(1)}, bf16[432,1024]{1,0:T(8,128)(2,1)S(1)}, u32[]{:S(2)}, u32[]{:S(2)}) collective-permute-start(bf16[432,1024]{1,0:T(8,128)(2,1)S(1)} %reshape.25.before_2.refs_0_), channel_id=1, source_target_pairs={{0,1},{1,2},{2,3},{3,0},{4,5},{5,6},{6,7},{7,4},{8,9},{9,10},{10,1... | collective-permute-start | bytes 2654216 | tf_op jit(solution)/shard_map/ppermute | solution.py:27
  18.0 46.5 %collective-permute-start.2 = (bf16[432,1024]{1,0:T(8,128)(2,1)S(1)}, bf16[432,1024]{1,0:T(8,128)(2,1)S(1)}, u32[]{:S(2)}, u32[]{:S(2)}) collective-permute-start(bf16[432,1024]{1,0:T(8,128)(2,1)S(1)} %reshape.25.before_2.refs_0_), channel_id=1, source_target_pairs={{0,3},{1,0},{2,1},{3,2},{4,7},{5,4},{6,5},{7,6},{8,11},{9,8},{10,9... | collective-permute-start | bytes 2654216 | tf_op jit(solution)/shard_map/ppermute | solution.py:27
  21.5 12.3 %collective-permute-start.4 = (bf16[144,1024]{1,0:T(8,128)(2,1)S(1)}, bf16[144,1024]{1,0:T(8,128)(2,1)S(1)}, u32[]{:S(2)}, u32[]{:S(2)}) collective-permute-start(bf16[144,1024]{1,0:T(8,128)(2,1)S(1)} %collective-permute-done.3.before_1.refs_4_), channel_id=1, source_target_pairs={{0,4},{1,5},{2,6},{3,7},{4,8},{5,9},{6,10},{7,11},{8,12},{9,13},{1... | collective-permute-start | bytes 884744 | tf_op jit(solution)/shard_map/ppermute | solution.py:27
  23.4 15.6 %collective-permute-start.6 = (bf16[144,1024]{1,0:T(8,128)(2,1)S(1)}, bf16[144,1024]{1,0:T(8,128)(2,1)S(1)}, u32[]{:S(2)}, u32[]{:S(2)}) collective-permute-start(bf16[144,1024]{1,0:T(8,128)(2,1)S(1)} %collective-permute-done.3.before_1.refs_4_), channel_id=1, source_target_pairs={{0,12},{1,13},{2,14},{3,15},{4,0},{5,1},{6,2},{7,3},{8,4},{9,5},{1... | collective-permute-start | bytes 884744 | tf_op jit(solution)/shard_map/ppermute | solution.py:27
  31.8 18.7 %collective-permute-start.7 = (bf16[2016,128]{1,0:T(8,128)(2,1)S(1)}, bf16[2016,128]{1,0:T(8,128)(2,1)S(1)}, u32[]{:S(2)}, u32[]{:S(2)}) collective-permute-start(bf16[2016,128]{1,0:T(8,128)(2,1)S(1)} %get-tuple-element.16), channel_id=1, source_target_pairs={{0,1},{1,2},{2,3},{3,0},{4,5},{5,6},{6,7},{7,4},{8,9},{9,10},{10,1... | collective-permute-start | bytes 1548296 | tf_op jit(solution)/shard_map/ppermute | solution.py:52
  33.7 29.4 %collective-permute-start.8 = (bf16[2016,128]{1,0:T(8,128)(2,1)S(1)}, bf16[2016,128]{1,0:T(8,128)(2,1)S(1)}, u32[]{:S(2)}, u32[]{:S(2)}) collective-permute-start(bf16[2016,128]{1,0:T(8,128)(2,1)S(1)} %get-tuple-element.15), channel_id=1, source_target_pairs={{0,2},{1,3},{2,0},{3,1},{4,6},{5,7},{6,4},{7,5},{8,10},{9,11},{10,... | collective-permute-start | bytes 1548296 | tf_op jit(solution)/shard_map/ppermute | solution.py:52
  38.9 25.5 %collective-permute-start.9 = (bf16[2016,128]{1,0:T(8,128)(2,1)S(1)}, bf16[2016,128]{1,0:T(8,128)(2,1)S(1)}, u32[]{:S(2)}, u32[]{:S(2)}) collective-permute-start(bf16[2016,128]{1,0:T(8,128)(2,1)S(1)} %get-tuple-element.14), channel_id=1, source_target_pairs={{0,3},{1,0},{2,1},{3,2},{4,7},{5,4},{6,5},{7,6},{8,11},{9,8},{10,9... | collective-permute-start | bytes 1548296 | tf_op jit(solution)/shard_map/ppermute | solution.py:52
  64.5 21.3 %collective-permute-start.10 = (bf16[3,2016,128]{2,1,0:T(8,128)(2,1)S(1)}, bf16[3,2016,128]{2,1,0:T(8,128)(2,1)S(1)}, u32[]{:S(2)}, u32[]{:S(2)}) collective-permute-start(bf16[3,2016,128]{2,1,0:T(8,128)(2,1)S(1)} %join.1.mine_ref), channel_id=1, source_target_pairs={{0,16},{16,0},{32,48},{48,32},{64,80},{80,64},{96,112},{112,96},{1... | collective-permute-start | bytes 4644872 | tf_op jit(solution)/shard_map/ppermute | solution.py:42
  76.1 22.0 %collective-permute-start.1 = (bf16[432,1024]{1,0:T(8,128)(2,1)S(1)}, bf16[432,1024]{1,0:T(8,128)(2,1)}, u32[]{:S(2)}, u32[]{:S(2)}) collective-permute-start(bf16[432,1024]{1,0:T(8,128)(2,1)S(1)} %collective-permute-done.rest_0_.refs_1_), channel_id=1, source_target_pairs={{0,1},{1,2},{2,3},{3,0},{4,5},{5,6},{6,7},{7,4},{8,9},{9,10},{10,1... | collective-permute-start | bytes 2654216 | tf_op jit(solution)/shard_map/ppermute | solution.py:27
  81.4 16.6 %collective-permute-start.5 = (bf16[144,1024]{1,0:T(8,128)(2,1)S(1)}, bf16[144,1024]{1,0:T(8,128)(2,1)}, u32[]{:S(2)}, u32[]{:S(2)}) collective-permute-start(bf16[144,1024]{1,0:T(8,128)(2,1)S(1)} %collective-permute-done.4.rest_2_.refs_5_), channel_id=1, source_target_pairs={{0,4},{1,5},{2,6},{3,7},{4,8},{5,9},{6,10},{7,11},{8,12},{9,13},{1... | collective-permute-start | bytes 884744 | tf_op jit(solution)/shard_map/ppermute | solution.py:27

commit v3 on v2

--- a/solution.py
+++ b/solution.py
@@ -52,7 +52,7 @@
     return lax.ppermute(value, ("row", "col"), pairs)
 
 
-def pack_kernel(own_c, at_ref, amps_ref, before_1, before_2, sent_ref, own_ref):
+def pack_kernel(own_c, at_ref, amps_ref, sent_ref, own_ref):
     x, yh, core = at_ref[0], at_ref[1], at_ref[2]
     rows, nv = amps_ref.shape
     tail = SIDE * own_c - LANES
@@ -97,32 +97,47 @@
         sent_ref[i, rows:, :] = carry[i].astype(jnp.bfloat16)
 
 
-def unpack_kernel(core_ref, own_ref, mine_ref, other_ref, ab_ref, ba_ref):
+def unpack_kernel(pairs_p, core_ref, own_ref, mine_ref, other_ref, ab_ref, ba_ref, main, end, turned_main, turned_end):
     core = core_ref[0]
-    rows = ab_ref.shape[1]
+    rows, wide = ab_ref.shape[1:]
     part = rows // CHUNKS
-    tail = ab_ref.shape[2] - LANES
-
-    def put(from_ref, to_ref):
+    tail = wide - LANES
+
+    def put(ab_from, ba_from):
         for s in range(3):
-            to_ref[s + 1, :, :LANES] = from_ref[s, :rows, :]
-            end = from_ref[s, rows:, :].astype(jnp.float32)
+            ab_ref[s + 1, :, :LANES] = ab_from[s, :rows, :]
+            main[(s + 1) * rows : (s + 2) * rows, :] = ba_from[s, :rows, :].astype(jnp.float32)
+            ab_end = ab_from[s, rows:, :].astype(jnp.float32)
+            ba_end = ba_from[s, rows:, :].astype(jnp.float32)
             for k in range(CHUNKS):
-                turned = end if k == 0 else pltpu.roll(end, LANES - k * tail, 1)
-                to_ref[s + 1, k * part : (k + 1) * part, LANES:] = turned[:, :tail].astype(jnp.bfloat16)
+                shift = (LANES - k * tail) % LANES
+                at = k * part
+                ab_ref[s + 1, at : at + part, LANES:] = pltpu.roll(ab_end, shift, 1)[:, :tail].astype(jnp.bfloat16)
+                at += (s + 1) * rows
+                end[at : at + part, :] = pltpu.roll(ba_end, shift, 1)
 
     ab_ref[0] = own_ref[0]
-    ba_ref[0] = own_ref[1]
+    main[:rows, :] = own_ref[1, :, :LANES].astype(jnp.float32)
+    end[:rows, :tail] = own_ref[1, :, LANES:].astype(jnp.float32)
 
     @pl.when(core == 0)
     def _():
-        put(mine_ref, ab_ref)
-        put(other_ref, ba_ref)
+        put(mine_ref, other_ref)
 
     @pl.when(core == 1)
     def _():
-        put(other_ref, ab_ref)
-        put(mine_ref, ba_ref)
+        put(other_ref, mine_ref)
+
+    def one(p, carry):
+        body = jnp.concatenate([main[pl.ds(p, wide, stride=pairs_p), :].T, end[pl.ds(p, wide, stride=pairs_p), :].T[:tail]], 0)
+        turned_main[pl.ds(p, wide, stride=pairs_p), :] = body[:, :LANES]
+        turned_end[pl.ds(p, wide, stride=pairs_p), :tail] = body[:, LANES:]
+        return carry
+
+    lax.fori_loop(0, pairs_p, one, 0, unroll=4)
+    for s in range(SIDE):
+        ba_ref[s, :, :LANES] = turned_main[s * rows : (s + 1) * rows, :].astype(jnp.bfloat16)
+        ba_ref[s, :, LANES:] = turned_end[s * rows : (s + 1) * rows, :tail].astype(jnp.bfloat16)
 
 
 def join_kernel(first, second, third, *rest):
@@ -198,11 +213,11 @@
     sent, own = pl.pallas_call(
         functools.partial(pack_kernel, own_c),
         out_shape=(jax.ShapeDtypeStruct((3, rows + rows // CHUNKS, LANES), bf16), jax.ShapeDtypeStruct((2, rows, wide), bf16)),
-        in_specs=[smem, vmem, hbm, hbm],
+        in_specs=[smem, vmem],
         out_specs=(vmem, vmem),
         compiler_params=params,
         name="pack",
-    )(at, amps, partner, resident)
+    )(at, amps)
     lines = gathered(resident, 1, 0)
     mine = [core_0_along_x_core_1_along_y(sent[s - 1], s) for s in (1, 2, 3)]
     partners = gathered(partner, 0, 1)
@@ -216,14 +231,14 @@
     )(*mine, lines[1], lines[3], partners[1], partners[3])
     other = between_cores(mine)
     ab, ba = pl.pallas_call(
-        unpack_kernel,
+        functools.partial(unpack_kernel, pairs_p),
         out_shape=(jax.ShapeDtypeStruct((SIDE, rows, wide), bf16),) * 2,
         in_specs=[smem, vmem, vmem, vmem],
         out_specs=(vmem, vmem),
+        scratch_shapes=[pltpu.VMEM((SIDE * rows, LANES), f32)] * 4,
         compiler_params=params,
         name="unpack",
     )(at[2:], own, mine, other)
-    ba = jnp.transpose(ba.reshape(wide, pairs_p, wide), (2, 1, 0)).reshape(SIDE, rows, wide)
     part = pl.pallas_call(
         functools.partial(ladder_kernel, own_a, own_c, pairs_p),
         out_shape=jax.ShapeDtypeStruct((own_a * WIN, LANES), f32),

time: 129 us -> 117 us (0.907)
  the two profiles are of different devices: /device:TPU:1 before, /device:TPU:16 now
where the time goes in v3:
time: 117 us
  starting transfers between devices  49.5 us (42%)
  Pallas kernels  24 us (21%)
  blocking collectives  22.7 us (19%)
  waiting for transfers between devices  14.2 us (12%)
  local copies, waits for them, and re-layouts  5.43 us (5%)
    all_to_all x1, blocking collectives, shards(): lax.all_to_all(jnp.broadcast_to(part, (SIDE * SIDE, *part.shape)), 'col',...  22.7 us
    ppermute x6, starting transfers between devices, moved(): return lax.ppermute(value, ('row', 'col'), pairs)  21.3 us
    ppermute x1, starting transfers between devices, from_next_row(): lax.ppermute(value, 'row', [(source, (source - 1) % rows) for source in r...  14.3 us
    pallas_call x1, Pallas kernels, shards(): pl.pallas_call(functools.partial(ladder_kernel, own_a, own_c, pairs_p), o...  11.2 us
    ppermute x6, waiting for transfers between devices, moved(): return lax.ppermute(value, ('row', 'col'), pairs)  10.5 us
    ppermute x3, starting transfers between devices, core_0_along_x_core_1_along_y(): return lax.ppermute(value, ('row', 'col'), pairs)  10.4 us
    pallas_call x1, Pallas kernels, shards(): pl.pallas_call(functools.partial(unpack_kernel, pairs_p), out_shape=(jax....  9.08 us
    ppermute x3, waiting for transfers between devices, core_0_along_x_core_1_along_y(): return lax.ppermute(value, ('row', 'col'), pairs)  3.71 us
  transfers between devices with their start and end apart: 11, of which 4 were waited for; matrix products, arithmetic and copies ran while one was open for 2% of the time, Pallas kernels for 10%

profile of v3, /device:TPU:16, one launch (start us, length us, event | category | flops | bytes accessed | tf_op | source)
XLA Modules:
  0.0 116.8 jit_solution(14838936560518904784)
XLA Ops:
  0.6 1.7 %copy.5 = bf16[36,12,1024]{2,1,0:T(8,128)(2,1)S(1)} copy(bf16[36,12,1024]{2,0,1:T(8,128)(2,1)} %bitcast.16) | data formatting | bytes 1769472 | tf_op jit(solution)/shard_map/transpose | solution.py:211
  2.3 0.2 reshape.19.refs_0_
  2.5 3.4 %collective-permute-start = (bf16[432,1024]{1,0:T(8,128)(2,1)S(1)}, bf16[432,1024]{1,0:T(8,128)(2,1)S(1)}, u32[]{:S(2)}, u32[]{:S(2)}) collective-permute-start(bf16[432,1024]{1,0:T(8,128)(2,1)S(1)} %reshape.19.refs_0_), channel_id=1, source_target_pairs={{0,1},{1,2},{2,3},{3,0},{4,5},{5,6},{6,7},{7,4},{8,9},{9,10},{10,1... | collective-permute-start | bytes 2654216 | tf_op jit(solution)/shard_map/ppermute | solution.py:27
  6.0 3.7 %collective-permute-start.2 = (bf16[432,1024]{1,0:T(8,128)(2,1)S(1)}, bf16[432,1024]{1,0:T(8,128)(2,1)S(1)}, u32[]{:S(2)}, u32[]{:S(2)}) collective-permute-start(bf16[432,1024]{1,0:T(8,128)(2,1)S(1)} %reshape.19.refs_0_), channel_id=1, source_target_pairs={{0,3},{1,0},{2,1},{3,2},{4,7},{5,4},{6,5},{7,6},{8,11},{9,8},{10,9... | collective-permute-start | bytes 2654216 | tf_op jit(solution)/shard_map/ppermute | solution.py:27
  9.6 1.0 slice.12
  10.6 0.8 reshape.20
  11.4 14.3 %collective-permute-start.3 = (bf16[144,1024]{1,0:T(8,128)(2,1)}, bf16[144,1024]{1,0:T(8,128)(2,1)S(1)}, u32[]{:S(2)}, u32[]{:S(2)}) collective-permute-start(bf16[144,1024]{1,0:T(8,128)(2,1)} %reshape.20), channel_id=1, source_target_pairs={{0,752},{16,0},{32,16},{48,32},{64,48},{80,64},{96,80},{112,96},{1... | collective-permute-start | bytes 884744 | tf_op jit(solution)/shard_map/ppermute | solution.py:37
  25.7 0.1 pad_add_fusion.at_ref
  25.8 0.0 copy-start
  25.8 1.6 %copy-done = bf16[48,36,576]{2,0,1:T(8,128)(2,1)S(1)} copy-done((bf16[48,36,576]{2,0,1:T(8,128)(2,1)S(1)}, bf16[48,36,576]{2,0,1:T(8,128)(2,1)}, u32[]{:S(2)}) %copy-start) | copy-done | bytes 1990680
  27.4 2.9 %pack.1 = (bf16[3,2016,128]{2,1,0:T(8,128)(2,1)S(1)}, bf16[2,1728,144]{2,1,0:T(8,128)(2,1)S(1)}) custom-call(s32[3]{0:T(128)S(1)} %pad_add_fusion.at_ref, bf16[1728,576]{1,0:T(8,128)(2,1)S(1)} %bitcast.15), custom_call_target="tpu_custom_call" | custom-call | tf_op jit(solution)/shard_map/pack/pallas_call | solution.py:213
  30.3 0.1 slice_bitcast_fusion
  30.4 2.4 %collective-permute-start.7 = (bf16[2016,128]{1,0:T(8,128)(2,1)S(1)}, bf16[2016,128]{1,0:T(8,128)(2,1)S(1)}, u32[]{:S(2)}, u32[]{:S(2)}) collective-permute-start(bf16[2016,128]{1,0:T(8,128)(2,1)S(1)} %get-tuple-element.16), channel_id=1, source_target_pairs={{0,1},{1,2},{2,3},{3,0},{4,5},{5,6},{6,7},{7,4},{8,9},{9,10},{10,1... | collective-permute-start | bytes 1548296 | tf_op jit(solution)/shard_map/ppermute | solution.py:52
  32.8 5.8 %collective-permute-start.8 = (bf16[2016,128]{1,0:T(8,128)(2,1)S(1)}, bf16[2016,128]{1,0:T(8,128)(2,1)S(1)}, u32[]{:S(2)}, u32[]{:S(2)}) collective-permute-start(bf16[2016,128]{1,0:T(8,128)(2,1)S(1)} %get-tuple-element.15), channel_id=1, source_target_pairs={{0,2},{1,3},{2,0},{3,1},{4,6},{5,7},{6,4},{7,5},{8,10},{9,11},{10,... | collective-permute-start | bytes 1548296 | tf_op jit(solution)/shard_map/ppermute | solution.py:52
  38.7 0.0 collective-permute-done.3.refs_4_
  38.7 2.1 %collective-permute-start.9 = (bf16[2016,128]{1,0:T(8,128)(2,1)S(1)}, bf16[2016,128]{1,0:T(8,128)(2,1)S(1)}, u32[]{:S(2)}, u32[]{:S(2)}) collective-permute-start(bf16[2016,128]{1,0:T(8,128)(2,1)S(1)} %get-tuple-element.14), channel_id=1, source_target_pairs={{0,3},{1,0},{2,1},{3,2},{4,7},{5,4},{6,5},{7,6},{8,11},{9,8},{10,9... | collective-permute-start | bytes 1548296 | tf_op jit(solution)/shard_map/ppermute | solution.py:52
  40.8 1.8 %collective-permute-done.7.first = bf16[2016,128]{1,0:T(8,128)(2,1)S(1)} collective-permute-done((bf16[2016,128]{1,0:T(8,128)(2,1)S(1)}, bf16[2016,128]{1,0:T(8,128)(2,1)S(1)}, u32[]{:S(2)}, u32[]{:S(2)}) %collective-permute-start.7) | collective-permute-done | bytes 516128 | tf_op jit(solution)/shard_map/ppermute | solution.py:52
  42.6 4.8 %collective-permute-start.4 = (bf16[144,1024]{1,0:T(8,128)(2,1)S(1)}, bf16[144,1024]{1,0:T(8,128)(2,1)S(1)}, u32[]{:S(2)}, u32[]{:S(2)}) collective-permute-start(bf16[144,1024]{1,0:T(8,128)(2,1)S(1)} %collective-permute-done.3.refs_4_), channel_id=1, source_target_pairs={{0,4},{1,5},{2,6},{3,7},{4,8},{5,9},{6,10},{7,11},{8,12},{9,13},{1... | collective-permute-start | bytes 884744 | tf_op jit(solution)/shard_map/ppermute | solution.py:27
  47.4 1.9 %collective-permute-done.8.second = bf16[2016,128]{1,0:T(8,128)(2,1)S(1)} collective-permute-done((bf16[2016,128]{1,0:T(8,128)(2,1)S(1)}, bf16[2016,128]{1,0:T(8,128)(2,1)S(1)}, u32[]{:S(2)}, u32[]{:S(2)}) %collective-permute-start.8) | collective-permute-done | bytes 516128 | tf_op jit(solution)/shard_map/ppermute | solution.py:52
  49.3 2.2 %collective-permute-start.6 = (bf16[144,1024]{1,0:T(8,128)(2,1)S(1)}, bf16[144,1024]{1,0:T(8,128)(2,1)S(1)}, u32[]{:S(2)}, u32[]{:S(2)}) collective-permute-start(bf16[144,1024]{1,0:T(8,128)(2,1)S(1)} %collective-permute-done.3.refs_4_), channel_id=1, source_target_pairs={{0,12},{1,13},{2,14},{3,15},{4,0},{5,1},{6,2},{7,3},{8,4},{9,5},{1... | collective-permute-start | bytes 884744 | tf_op jit(solution)/shard_map/ppermute | solution.py:27
  51.6 0.0 collective-permute-done.9.third
  51.6 5.0 %collective-permute-done.4.rest_2_.refs_5_ = bf16[144,1024]{1,0:T(8,128)(2,1)S(1)} collective-permute-done((bf16[144,1024]{1,0:T(8,128)(2,1)S(1)}, bf16[144,1024]{1,0:T(8,128)(2,1)S(1)}, u32[]{:S(2)}, u32[]{:S(2)}) %collective-permute-start.4) | collective-permute-done | bytes 294944 | tf_op jit(solution)/shard_map/ppermute | solution.py:27
  56.5 5.5 %collective-permute-done.6.rest_3_.refs_7_ = bf16[144,1024]{1,0:T(8,128)(2,1)S(1)} collective-permute-done((bf16[144,1024]{1,0:T(8,128)(2,1)S(1)}, bf16[144,1024]{1,0:T(8,128)(2,1)S(1)}, u32[]{:S(2)}, u32[]{:S(2)}) %collective-permute-start.6) | collective-permute-done | bytes 294944 | tf_op jit(solution)/shard_map/ppermute | solution.py:27
  62.0 0.0 collective-permute-done.rest_0_.refs_1_
  62.0 0.0 collective-permute-done.2.rest_1_.refs_3_
  62.0 0.1 join.1.mine_ref
  62.2 3.6 %collective-permute-start.10 = (bf16[3,2016,128]{2,1,0:T(8,128)(2,1)S(1)}, bf16[3,2016,128]{2,1,0:T(8,128)(2,1)S(1)}, u32[]{:S(2)}, u32[]{:S(2)}) collective-permute-start(bf16[3,2016,128]{2,1,0:T(8,128)(2,1)S(1)} %join.1.mine_ref), channel_id=1, source_target_pairs={{0,16},{16,0},{32,48},{48,32},{64,80},{80,64},{96,112},{112,96},{1... | collective-permute-start | bytes 4644872 | tf_op jit(solution)/shard_map/ppermute | solution.py:42
  65.7 2.8 %collective-permute-start.1 = (bf16[432,1024]{1,0:T(8,128)(2,1)S(1)}, bf16[432,1024]{1,0:T(8,128)(2,1)S(1)}, u32[]{:S(2)}, u32[]{:S(2)}) collective-permute-start(bf16[432,1024]{1,0:T(8,128)(2,1)S(1)} %collective-permute-done.rest_0_.refs_1_), channel_id=1, source_target_pairs={{0,1},{1,2},{2,3},{3,0},{4,5},{5,6},{6,7},{7,4},{8,9},{9,10},{10,1... | collective-permute-start | bytes 2654216 | tf_op jit(solution)/shard_map/ppermute | solution.py:27
  68.5 4.4 %collective-permute-start.5 = (bf16[144,1024]{1,0:T(8,128)(2,1)S(1)}, bf16[144,1024]{1,0:T(8,128)(2,1)S(1)}, u32[]{:S(2)}, u32[]{:S(2)}) collective-permute-start(bf16[144,1024]{1,0:T(8,128)(2,1)S(1)} %collective-permute-done.4.rest_2_.refs_5_), channel_id=1, source_target_pairs={{0,4},{1,5},{2,6},{3,7},{4,8},{5,9},{6,10},{7,11},{8,12},{9,13},{1... | collective-permute-start | bytes 884744 | tf_op jit(solution)/shard_map/ppermute | solution.py:27
  73.0 0.0 collective-permute-done.10.other_ref
  73.0 9.1 %unpack.1 = (bf16[4,1728,144]{2,1,0:T(8,128)(2,1)}, bf16[4,1728,144]{2,1,0:T(8,128)(2,1)}) custom-call(s32[1]{0:T(128)} %bitcast.core_ref, bf16[2,1728,144]{2,1,0:T(8,128)(2,1)S(1)} %get-tuple-element.8.own_ref, bf16[3,2016,128]{2,1,0:T(8,128)(2,1)S(1)} %join.1.mine_ref, bf16[3,2016,128]{2,1,0:T(8,128)(2,1)S(1)} %collective-permute-done.10.other_ref), custom_call_target="tpu_custom_call" | custom-call | tf_op jit(solution)/shard_map/unpack/pallas_call | solution.py:233
  82.1 0.0 collective-permute-done.5.refs_6_
  82.1 0.0 collective-permute-done.1.refs_2_
  82.1 11.2 %ladders.1 = f32[48,128]{1,0:T(8,128)S(1)} custom-call(s32[1]{0:T(128)} %bitcast.core_ref, bf16[432,1024]{1,0:T(8,128)(2,1)S(1)} %reshape.19.refs_0_, bf16[432,1024]{1,0:T(8,128)(2,1)S(1)} %collective-permute-done.rest_0_.refs_1_, bf16[432,1024]{1,0:T(8,128)(2,1)S(1)} %collective-permute-done.1.refs_2_, ...), custom_call_target="tpu_custom_call" | custom-call | tf_op jit(solution)/shard_map/ladders/pallas_call | solution.py:242
  93.3 22.7 %all_to_all.5.parts_ref = f32[16,48,128]{2,1,0:T(8,128)S(1)} all-to-all(f32[16,48,128]{2,1,0:T(8,128)S(1)} %broadcast_in_dim.3), channel_id=1, replica_groups=mesh['row'=48,'col'=16] {'col'}, dimensions={0} | all-to-all | bytes 786432 | tf_op jit(solution)/shard_map/all_to_all | solution.py:255
  116.1 0.7 add.15
  (1 shorter events, 0.0 us)
Async XLA Ops:
  2.5 59.5 %collective-permute-start = (bf16[432,1024]{1,0:T(8,128)(2,1)S(1)}, bf16[432,1024]{1,0:T(8,128)(2,1)S(1)}, u32[]{:S(2)}, u32[]{:S(2)}) collective-permute-start(bf16[432,1024]{1,0:T(8,128)(2,1)S(1)} %reshape.19.refs_0_), channel_id=1, source_target_pairs={{0,1},{1,2},{2,3},{3,0},{4,5},{5,6},{6,7},{7,4},{8,9},{9,10},{10,1... | collective-permute-start | bytes 2654216 | tf_op jit(solution)/shard_map/ppermute | solution.py:27
  6.0 56.1 %collective-permute-start.2 = (bf16[432,1024]{1,0:T(8,128)(2,1)S(1)}, bf16[432,1024]{1,0:T(8,128)(2,1)S(1)}, u32[]{:S(2)}, u32[]{:S(2)}) collective-permute-start(bf16[432,1024]{1,0:T(8,128)(2,1)S(1)} %reshape.19.refs_0_), channel_id=1, source_target_pairs={{0,3},{1,0},{2,1},{3,2},{4,7},{5,4},{6,5},{7,6},{8,11},{9,8},{10,9... | collective-permute-start | bytes 2654216 | tf_op jit(solution)/shard_map/ppermute | solution.py:27
  11.4 27.3 %collective-permute-start.3 = (bf16[144,1024]{1,0:T(8,128)(2,1)}, bf16[144,1024]{1,0:T(8,128)(2,1)S(1)}, u32[]{:S(2)}, u32[]{:S(2)}) collective-permute-start(bf16[144,1024]{1,0:T(8,128)(2,1)} %reshape.20), channel_id=1, source_target_pairs={{0,752},{16,0},{32,16},{48,32},{64,48},{80,64},{96,80},{112,96},{1... | collective-permute-start | bytes 884744 | tf_op jit(solution)/shard_map/ppermute | solution.py:37
  25.8 1.6 %copy-start = (bf16[48,36,576]{2,0,1:T(8,128)(2,1)S(1)}, bf16[48,36,576]{2,0,1:T(8,128)(2,1)}, u32[]{:S(2)}) copy-start(bf16[48,36,576]{2,0,1:T(8,128)(2,1)} %param.3) | copy-start | bytes 5971972
  30.4 12.2 %collective-permute-start.7 = (bf16[2016,128]{1,0:T(8,128)(2,1)S(1)}, bf16[2016,128]{1,0:T(8,128)(2,1)S(1)}, u32[]{:S(2)}, u32[]{:S(2)}) collective-permute-start(bf16[2016,128]{1,0:T(8,128)(2,1)S(1)} %get-tuple-element.16), channel_id=1, source_target_pairs={{0,1},{1,2},{2,3},{3,0},{4,5},{5,6},{6,7},{7,4},{8,9},{9,10},{10,1... | collective-permute-start | bytes 1548296 | tf_op jit(solution)/shard_map/ppermute | solution.py:52
  32.8 16.5 %collective-permute-start.8 = (bf16[2016,128]{1,0:T(8,128)(2,1)S(1)}, bf16[2016,128]{1,0:T(8,128)(2,1)S(1)}, u32[]{:S(2)}, u32[]{:S(2)}) collective-permute-start(bf16[2016,128]{1,0:T(8,128)(2,1)S(1)} %get-tuple-element.15), channel_id=1, source_target_pairs={{0,2},{1,3},{2,0},{3,1},{4,6},{5,7},{6,4},{7,5},{8,10},{9,11},{10,... | collective-permute-start | bytes 1548296 | tf_op jit(solution)/shard_map/ppermute | solution.py:52
  38.7 12.9 %collective-permute-start.9 = (bf16[2016,128]{1,0:T(8,128)(2,1)S(1)}, bf16[2016,128]{1,0:T(8,128)(2,1)S(1)}, u32[]{:S(2)}, u32[]{:S(2)}) collective-permute-start(bf16[2016,128]{1,0:T(8,128)(2,1)S(1)} %get-tuple-element.14), channel_id=1, source_target_pairs={{0,3},{1,0},{2,1},{3,2},{4,7},{5,4},{6,5},{7,6},{8,11},{9,8},{10,9... | collective-permute-start | bytes 1548296 | tf_op jit(solution)/shard_map/ppermute | solution.py:52
  42.6 13.9 %collective-permute-start.4 = (bf16[144,1024]{1,0:T(8,128)(2,1)S(1)}, bf16[144,1024]{1,0:T(8,128)(2,1)S(1)}, u32[]{:S(2)}, u32[]{:S(2)}) collective-permute-start(bf16[144,1024]{1,0:T(8,128)(2,1)S(1)} %collective-permute-done.3.refs_4_), channel_id=1, source_target_pairs={{0,4},{1,5},{2,6},{3,7},{4,8},{5,9},{6,10},{7,11},{8,12},{9,13},{1... | collective-permute-start | bytes 884744 | tf_op jit(solution)/shard_map/ppermute | solution.py:27
  49.3 12.7 %collective-permute-start.6 = (bf16[144,1024]{1,0:T(8,128)(2,1)S(1)}, bf16[144,1024]{1,0:T(8,128)(2,1)S(1)}, u32[]{:S(2)}, u32[]{:S(2)}) collective-permute-start(bf16[144,1024]{1,0:T(8,128)(2,1)S(1)} %collective-permute-done.3.refs_4_), channel_id=1, source_target_pairs={{0,12},{1,13},{2,14},{3,15},{4,0},{5,1},{6,2},{7,3},{8,4},{9,5},{1... | collective-permute-start | bytes 884744 | tf_op jit(solution)/shard_map/ppermute | solution.py:27
  62.2 10.8 %collective-permute-start.10 = (bf16[3,2016,128]{2,1,0:T(8,128)(2,1)S(1)}, bf16[3,2016,128]{2,1,0:T(8,128)(2,1)S(1)}, u32[]{:S(2)}, u32[]{:S(2)}) collective-permute-start(bf16[3,2016,128]{2,1,0:T(8,128)(2,1)S(1)} %join.1.mine_ref), channel_id=1, source_target_pairs={{0,16},{16,0},{32,48},{48,32},{64,80},{80,64},{96,112},{112,96},{1... | collective-permute-start | bytes 4644872 | tf_op jit(solution)/shard_map/ppermute | solution.py:42
  65.7 16.3 %collective-permute-start.1 = (bf16[432,1024]{1,0:T(8,128)(2,1)S(1)}, bf16[432,1024]{1,0:T(8,128)(2,1)S(1)}, u32[]{:S(2)}, u32[]{:S(2)}) collective-permute-start(bf16[432,1024]{1,0:T(8,128)(2,1)S(1)} %collective-permute-done.rest_0_.refs_1_), channel_id=1, source_target_pairs={{0,1},{1,2},{2,3},{3,0},{4,5},{5,6},{6,7},{7,4},{8,9},{9,10},{10,1... | collective-permute-start | bytes 2654216 | tf_op jit(solution)/shard_map/ppermute | solution.py:27
  68.5 13.6 %collective-permute-start.5 = (bf16[144,1024]{1,0:T(8,128)(2,1)S(1)}, bf16[144,1024]{1,0:T(8,128)(2,1)S(1)}, u32[]{:S(2)}, u32[]{:S(2)}) collective-permute-start(bf16[144,1024]{1,0:T(8,128)(2,1)S(1)} %collective-permute-done.4.rest_2_.refs_5_), channel_id=1, source_target_pairs={{0,4},{1,5},{2,6},{3,7},{4,8},{5,9},{6,10},{7,11},{8,12},{9,13},{1... | collective-permute-start | bytes 884744 | tf_op jit(solution)/shard_map/ppermute | solution.py:27

commit v4 on v3

--- a/solution.py
+++ b/solution.py
@@ -16,25 +16,21 @@
 ROWS_BY_ROWS = (((1,), (1,)), ((), ()))
 
 
-def moved(value, dx, dy):
+def moved(value, dx, dy, rows_on=0):
     pairs = []
-    for row in range(lax.axis_size("row")):
+    rows = lax.axis_size("row")
+    for row in range(rows):
         sign = 1 - 2 * (row % 2)
         for yh in range(SIDE):
             for x in range(SIDE):
                 to = (yh + sign * dy) % SIDE * SIDE + (x + sign * dx) % SIDE
-                pairs.append(((row * SIDE + yh) * SIDE + x, row * SIDE * SIDE + to))
+                pairs.append((((row + rows_on) % rows * SIDE + yh) * SIDE + x, row * SIDE * SIDE + to))
     return lax.ppermute(value, ("row", "col"), pairs)
 
 
 def gathered(value, dx, dy):
     first = moved(value, dx, dy)
     return [value, first, moved(first, dx, dy), moved(value, -dx, -dy)]
-
-
-def from_next_row(value):
-    rows = lax.axis_size("row")
-    return lax.ppermute(value, "row", [(source, (source - 1) % rows) for source in range(rows)])
 
 
 def between_cores(value):
@@ -207,7 +203,7 @@
     place, core = lax.axis_index("col"), lax.axis_index("row") % 2
     at = jnp.stack([place % SIDE, place // SIDE, core]).astype(jnp.int32)
 
-    partner = from_next_row(df_blocks[:WIN].reshape(WIN * own_c, aux))
+    partner = df_blocks[:WIN].reshape(WIN * own_c, aux)
     resident = jnp.transpose(df_blocks, (1, 0, 2)).reshape(own_c * own_a, aux)
     amps = jnp.transpose(amplitudes, (1, 0, 2)).reshape(rows, nv)
     sent, own = pl.pallas_call(
@@ -220,15 +216,16 @@
     )(at, amps)
     lines = gathered(resident, 1, 0)
     mine = [core_0_along_x_core_1_along_y(sent[s - 1], s) for s in (1, 2, 3)]
-    partners = gathered(partner, 0, 1)
+    first = moved(partner, 0, 1, 1)
+    partners = [moved(partner, 0, 0, 1), first, moved(first, 0, 1), moved(partner, 0, -1, 1)]
     mine = pl.pallas_call(
         join_kernel,
         out_shape=jax.ShapeDtypeStruct(sent.shape, bf16),
-        in_specs=[vmem] * 3 + [hbm] * 4,
+        in_specs=[vmem] * 3 + [hbm] * 2,
         out_specs=vmem,
         compiler_params=params,
         name="join",
-    )(*mine, lines[1], lines[3], partners[1], partners[3])
+    )(*mine, lines[1], partners[1])
     other = between_cores(mine)
     ab, ba = pl.pallas_call(
         functools.partial(unpack_kernel, pairs_p),

time: 117 us -> 126 us (1.077)
  the two profiles are of different devices: /device:TPU:16 before, /device:TPU:1 now
where the time goes in v4:
time: 126 us
  starting transfers between devices  56.3 us (45%)
  Pallas kernels  25.4 us (20%)
  waiting for transfers between devices  19.9 us (16%)
  blocking collectives  15.2 us (12%)
  local copies, waits for them, and re-layouts  8.22 us (7%)
    ppermute x7, starting transfers between devices, moved(): return lax.ppermute(value, ('row', 'col'), pairs)  39.6 us
    all_to_all x1, blocking collectives, shards(): lax.all_to_all(jnp.broadcast_to(part, (SIDE * SIDE, *part.shape)), 'col',...  15.2 us
    ppermute x3, starting transfers between devices, core_0_along_x_core_1_along_y(): return lax.ppermute(value, ('row', 'col'), pairs)  14.8 us
    ppermute x7, waiting for transfers between devices, moved(): return lax.ppermute(value, ('row', 'col'), pairs)  13.1 us
    pallas_call x1, Pallas kernels, shards(): pl.pallas_call(functools.partial(ladder_kernel, own_a, own_c, pairs_p), o...  11.2 us
    pallas_call x1, Pallas kernels, shards(): pl.pallas_call(functools.partial(unpack_kernel, pairs_p), out_shape=(jax....  9.08 us
    ppermute x3, waiting for transfers between devices, core_0_along_x_core_1_along_y(): return lax.ppermute(value, ('row', 'col'), pairs)  6.77 us
    pallas_call x1, Pallas kernels, shards(): pl.pallas_call(functools.partial(pack_kernel, own_c), out_shape=(jax.Shap...  2.94 us
  transfers between devices with their start and end apart: 11, of which 2 were waited for; matrix products, arithmetic and copies ran while one was open for 4% of the time, Pallas kernels for 10%

profile of v4, /device:TPU:1, one launch (start us, length us, event | category | flops | bytes accessed | tf_op | source)
XLA Modules:
  0.0 125.9 jit_solution(4355632137205912975)
XLA Ops:
  0.6 1.7 %copy.5 = bf16[36,12,1024]{2,1,0:T(8,128)(2,1)S(1)} copy(bf16[36,12,1024]{2,0,1:T(8,128)(2,1)} %bitcast.16) | data formatting | bytes 1769472 | tf_op jit(solution)/shard_map/transpose | solution.py:207
  2.3 0.2 reshape.19.refs_0_
  2.5 5.2 %collective-permute-start = (bf16[432,1024]{1,0:T(8,128)(2,1)S(1)}, bf16[432,1024]{1,0:T(8,128)(2,1)S(1)}, u32[]{:S(2)}, u32[]{:S(2)}) collective-permute-start(bf16[432,1024]{1,0:T(8,128)(2,1)S(1)} %reshape.19.refs_0_), channel_id=1, source_target_pairs={{0,1},{1,2},{2,3},{3,0},{4,5},{5,6},{6,7},{7,4},{8,9},{9,10},{10,1... | collective-permute-start | bytes 2654216 | tf_op jit(solution)/shard_map/ppermute | solution.py:28
  7.8 0.1 pad_add_fusion.at_ref
  7.9 0.0 copy-start
  7.9 1.6 %copy-done = bf16[48,36,576]{2,0,1:T(8,128)(2,1)S(1)} copy-done((bf16[48,36,576]{2,0,1:T(8,128)(2,1)S(1)}, bf16[48,36,576]{2,0,1:T(8,128)(2,1)}, u32[]{:S(2)}) %copy-start) | copy-done | bytes 1990680
  9.5 2.9 %pack.1 = (bf16[3,2016,128]{2,1,0:T(8,128)(2,1)S(1)}, bf16[2,1728,144]{2,1,0:T(8,128)(2,1)S(1)}) custom-call(s32[3]{0:T(128)S(1)} %pad_add_fusion.at_ref, bf16[1728,576]{1,0:T(8,128)(2,1)S(1)} %bitcast.15), custom_call_target="tpu_custom_call" | custom-call | tf_op jit(solution)/shard_map/pack/pallas_call | solution.py:209
  12.4 1.2 slice_bitcast_fusion
  13.6 4.2 %collective-permute-start.7 = (bf16[2016,128]{1,0:T(8,128)(2,1)}, bf16[2016,128]{1,0:T(8,128)(2,1)}, u32[]{:S(2)}, u32[]{:S(2)}) collective-permute-start(bf16[2016,128]{1,0:T(8,128)(2,1)} %get-tuple-element.16), channel_id=1, source_target_pairs={{0,1},{1,2},{2,3},{3,0},{4,5},{5,6},{6,7},{7,4},{8,9},{9,10},{10,1... | collective-permute-start | bytes 1548296 | tf_op jit(solution)/shard_map/ppermute | solution.py:48
  17.9 5.7 %collective-permute-start.8 = (bf16[2016,128]{1,0:T(8,128)(2,1)}, bf16[2016,128]{1,0:T(8,128)(2,1)}, u32[]{:S(2)}, u32[]{:S(2)}) collective-permute-start(bf16[2016,128]{1,0:T(8,128)(2,1)} %get-tuple-element.15), channel_id=1, source_target_pairs={{0,2},{1,3},{2,0},{3,1},{4,6},{5,7},{6,4},{7,5},{8,10},{9,11},{10,... | collective-permute-start | bytes 1548296 | tf_op jit(solution)/shard_map/ppermute | solution.py:48
  23.5 5.0 %collective-permute-start.9 = (bf16[2016,128]{1,0:T(8,128)(2,1)}, bf16[2016,128]{1,0:T(8,128)(2,1)}, u32[]{:S(2)}, u32[]{:S(2)}) collective-permute-start(bf16[2016,128]{1,0:T(8,128)(2,1)} %get-tuple-element.14), channel_id=1, source_target_pairs={{0,3},{1,0},{2,1},{3,2},{4,7},{5,4},{6,5},{7,6},{8,11},{9,8},{10,9... | collective-permute-start | bytes 1548296 | tf_op jit(solution)/shard_map/ppermute | solution.py:48
  28.5 1.7 %slice.12 = bf16[4,36,1024]{2,1,0:T(8,128)(2,1)} slice(bf16[12,36,1024]{2,1,0:T(8,128)(2,1)} %param.2), slice={[0:4], [0:36], [0:1024]} | slice | bytes 589824 | tf_op jit(solution)/shard_map/slice | solution.py:206
  30.2 1.7 %reshape.20 = bf16[144,1024]{1,0:T(8,128)(2,1)} reshape(bf16[4,36,1024]{2,1,0:T(8,128)(2,1)} %slice.12) | data formatting | bytes 589824 | tf_op jit(solution)/shard_map/reshape | solution.py:206
  32.0 0.0 copy-start.1
  32.0 2.0 %collective-permute-start.4 = (bf16[144,1024]{1,0:T(8,128)(2,1)}, bf16[144,1024]{1,0:T(8,128)(2,1)S(1)}, u32[]{:S(2)}, u32[]{:S(2)}) collective-permute-start(bf16[144,1024]{1,0:T(8,128)(2,1)} %reshape.20), channel_id=1, source_target_pairs={{16,4},{17,5},{18,6},{19,7},{20,8},{21,9},{22,10},{23,11},{24,12},... | collective-permute-start | bytes 884744 | tf_op jit(solution)/shard_map/ppermute | solution.py:28
  34.0 13.1 %collective-permute-done.4.rest_1_.refs_5_ = bf16[144,1024]{1,0:T(8,128)(2,1)S(1)} collective-permute-done((bf16[144,1024]{1,0:T(8,128)(2,1)}, bf16[144,1024]{1,0:T(8,128)(2,1)S(1)}, u32[]{:S(2)}, u32[]{:S(2)}) %collective-permute-start.4) | collective-permute-done | bytes 294944 | tf_op jit(solution)/shard_map/ppermute | solution.py:28
  47.1 0.0 collective-permute-done.7.first
  47.1 0.0 collective-permute-done.8.second
  47.1 6.8 %collective-permute-done.9.third = bf16[2016,128]{1,0:T(8,128)(2,1)} collective-permute-done((bf16[2016,128]{1,0:T(8,128)(2,1)}, bf16[2016,128]{1,0:T(8,128)(2,1)}, u32[]{:S(2)}, u32[]{:S(2)}) %collective-permute-start.9) | collective-permute-done | bytes 516128 | tf_op jit(solution)/shard_map/ppermute | solution.py:48
  53.9 0.0 collective-permute-done.rest_0_.refs_1_
  53.9 1.4 %join.1.mine_ref = bf16[3,2016,128]{2,1,0:T(8,128)(2,1)S(1)} custom-call(bf16[2016,128]{1,0:T(8,128)(2,1)} %collective-permute-done.7.first, bf16[2016,128]{1,0:T(8,128)(2,1)} %collective-permute-done.8.second, bf16[2016,128]{1,0:T(8,128)(2,1)} %collective-permute-done.9.third, bf16[432,1024]{1,0:T(8,128)(2,1)S(1)} %collective-permute-done.rest_0_.refs_1_, ...), custom_call_target="tpu_custom_call" | custom-call | tf_op jit(solution)/shard_map/join/pallas_call | solution.py:221
  55.3 1.9 %collective-permute-start.10 = (bf16[3,2016,128]{2,1,0:T(8,128)(2,1)S(1)}, bf16[3,2016,128]{2,1,0:T(8,128)(2,1)S(1)}, u32[]{:S(2)}, u32[]{:S(2)}) collective-permute-start(bf16[3,2016,128]{2,1,0:T(8,128)(2,1)S(1)} %join.1.mine_ref), channel_id=1, source_target_pairs={{0,16},{16,0},{32,48},{48,32},{64,80},{80,64},{96,112},{112,96},{1... | collective-permute-start | bytes 4644872 | tf_op jit(solution)/shard_map/ppermute | solution.py:38
  57.3 1.9 %collective-permute-start.2 = (bf16[432,1024]{1,0:T(8,128)(2,1)S(1)}, bf16[432,1024]{1,0:T(8,128)(2,1)S(1)}, u32[]{:S(2)}, u32[]{:S(2)}) collective-permute-start(bf16[432,1024]{1,0:T(8,128)(2,1)S(1)} %reshape.19.refs_0_), channel_id=1, source_target_pairs={{0,3},{1,0},{2,1},{3,2},{4,7},{5,4},{6,5},{7,6},{8,11},{9,8},{10,9... | collective-permute-start | bytes 2654216 | tf_op jit(solution)/shard_map/ppermute | solution.py:28
  59.2 4.6 %collective-permute-start.1 = (bf16[432,1024]{1,0:T(8,128)(2,1)S(1)}, bf16[432,1024]{1,0:T(8,128)(2,1)S(1)}, u32[]{:S(2)}, u32[]{:S(2)}) collective-permute-start(bf16[432,1024]{1,0:T(8,128)(2,1)S(1)} %collective-permute-done.rest_0_.refs_1_), channel_id=1, source_target_pairs={{0,1},{1,2},{2,3},{3,0},{4,5},{5,6},{6,7},{7,4},{8,9},{9,10},{10,1... | collective-permute-start | bytes 2654216 | tf_op jit(solution)/shard_map/ppermute | solution.py:28
  63.8 0.0 copy-done.1
  63.8 1.9 %collective-permute-start.3 = (bf16[144,1024]{1,0:T(8,128)(2,1)S(1)}, bf16[144,1024]{1,0:T(8,128)(2,1)S(1)}, u32[]{:S(2)}, u32[]{:S(2)}) collective-permute-start(bf16[144,1024]{1,0:T(8,128)(2,1)S(1)} %copy-done.1), channel_id=1, source_target_pairs={{16,0},{17,1},{18,2},{19,3},{20,4},{21,5},{22,6},{23,7},{24,8},{25... | collective-permute-start | bytes 884744 | tf_op jit(solution)/shard_map/ppermute | solution.py:28
  65.7 20.1 %collective-permute-start.6 = (bf16[144,1024]{1,0:T(8,128)(2,1)S(1)}, bf16[144,1024]{1,0:T(8,128)(2,1)S(1)}, u32[]{:S(2)}, u32[]{:S(2)}) collective-permute-start(bf16[144,1024]{1,0:T(8,128)(2,1)S(1)} %copy-done.1), channel_id=1, source_target_pairs={{16,12},{17,13},{18,14},{19,15},{20,0},{21,1},{22,2},{23,3},{24,4}... | collective-permute-start | bytes 884744 | tf_op jit(solution)/shard_map/ppermute | solution.py:28
  85.8 0.0 collective-permute-done.10.other_ref
  85.8 3.8 %collective-permute-start.5 = (bf16[144,1024]{1,0:T(8,128)(2,1)S(1)}, bf16[144,1024]{1,0:T(8,128)(2,1)S(1)}, u32[]{:S(2)}, u32[]{:S(2)}) collective-permute-start(bf16[144,1024]{1,0:T(8,128)(2,1)S(1)} %collective-permute-done.4.rest_1_.refs_5_), channel_id=1, source_target_pairs={{0,4},{1,5},{2,6},{3,7},{4,8},{5,9},{6,10},{7,11},{8,12},{9,13},{1... | collective-permute-start | bytes 884744 | tf_op jit(solution)/shard_map/ppermute | solution.py:28
  89.6 9.1 %unpack.1 = (bf16[4,1728,144]{2,1,0:T(8,128)(2,1)}, bf16[4,1728,144]{2,1,0:T(8,128)(2,1)}) custom-call(s32[1]{0:T(128)} %bitcast.core_ref, bf16[2,1728,144]{2,1,0:T(8,128)(2,1)S(1)} %get-tuple-element.8.own_ref, bf16[3,2016,128]{2,1,0:T(8,128)(2,1)S(1)} %join.1.mine_ref, bf16[3,2016,128]{2,1,0:T(8,128)(2,1)S(1)} %collective-permute-done.10.other_ref), custom_call_target="tpu_custom_call" | custom-call | tf_op jit(solution)/shard_map/unpack/pallas_call | solution.py:230
  98.7 0.0 collective-permute-done.3.refs_4_
  98.7 0.0 collective-permute-done.6.refs_7_
  98.7 0.0 collective-permute-done.5.refs_6_
  98.7 0.0 collective-permute-done.2.refs_3_
  98.7 0.0 collective-permute-done.1.refs_2_
  98.7 11.2 %ladders.1 = f32[48,128]{1,0:T(8,128)S(1)} custom-call(s32[1]{0:T(128)} %bitcast.core_ref, bf16[432,1024]{1,0:T(8,128)(2,1)S(1)} %reshape.19.refs_0_, bf16[432,1024]{1,0:T(8,128)(2,1)S(1)} %collective-permute-done.rest_0_.refs_1_, bf16[432,1024]{1,0:T(8,128)(2,1)S(1)} %collective-permute-done.1.refs_2_, ...), custom_call_target="tpu_custom_call" | custom-call | tf_op jit(solution)/shard_map/ladders/pallas_call | solution.py:239
  110.0 15.2 %all_to_all.5.parts_ref = f32[16,48,128]{2,1,0:T(8,128)S(1)} all-to-all(f32[16,48,128]{2,1,0:T(8,128)S(1)} %broadcast_in_dim.3), channel_id=1, replica_groups=mesh['row'=48,'col'=16] {'col'}, dimensions={0} | all-to-all | bytes 786432 | tf_op jit(solution)/shard_map/all_to_all | solution.py:252
  125.2 0.7 add.15
  (1 shorter events, 0.0 us)
Async XLA Ops:
  2.5 51.3 %collective-permute-start = (bf16[432,1024]{1,0:T(8,128)(2,1)S(1)}, bf16[432,1024]{1,0:T(8,128)(2,1)S(1)}, u32[]{:S(2)}, u32[]{:S(2)}) collective-permute-start(bf16[432,1024]{1,0:T(8,128)(2,1)S(1)} %reshape.19.refs_0_), channel_id=1, source_target_pairs={{0,1},{1,2},{2,3},{3,0},{4,5},{5,6},{6,7},{7,4},{8,9},{9,10},{10,1... | collective-permute-start | bytes 2654216 | tf_op jit(solution)/shard_map/ppermute | solution.py:28
  7.9 1.6 %copy-start = (bf16[48,36,576]{2,0,1:T(8,128)(2,1)S(1)}, bf16[48,36,576]{2,0,1:T(8,128)(2,1)}, u32[]{:S(2)}) copy-start(bf16[48,36,576]{2,0,1:T(8,128)(2,1)} %param.3) | copy-start | bytes 5971972
  13.6 33.5 %collective-permute-start.7 = (bf16[2016,128]{1,0:T(8,128)(2,1)}, bf16[2016,128]{1,0:T(8,128)(2,1)}, u32[]{:S(2)}, u32[]{:S(2)}) collective-permute-start(bf16[2016,128]{1,0:T(8,128)(2,1)} %get-tuple-element.16), channel_id=1, source_target_pairs={{0,1},{1,2},{2,3},{3,0},{4,5},{5,6},{6,7},{7,4},{8,9},{9,10},{10,1... | collective-permute-start | bytes 1548296 | tf_op jit(solution)/shard_map/ppermute | solution.py:48
  17.9 29.3 %collective-permute-start.8 = (bf16[2016,128]{1,0:T(8,128)(2,1)}, bf16[2016,128]{1,0:T(8,128)(2,1)}, u32[]{:S(2)}, u32[]{:S(2)}) collective-permute-start(bf16[2016,128]{1,0:T(8,128)(2,1)} %get-tuple-element.15), channel_id=1, source_target_pairs={{0,2},{1,3},{2,0},{3,1},{4,6},{5,7},{6,4},{7,5},{8,10},{9,11},{10,... | collective-permute-start | bytes 1548296 | tf_op jit(solution)/shard_map/ppermute | solution.py:48
  23.5 30.4 %collective-permute-start.9 = (bf16[2016,128]{1,0:T(8,128)(2,1)}, bf16[2016,128]{1,0:T(8,128)(2,1)}, u32[]{:S(2)}, u32[]{:S(2)}) collective-permute-start(bf16[2016,128]{1,0:T(8,128)(2,1)} %get-tuple-element.14), channel_id=1, source_target_pairs={{0,3},{1,0},{2,1},{3,2},{4,7},{5,4},{6,5},{7,6},{8,11},{9,8},{10,9... | collective-permute-start | bytes 1548296 | tf_op jit(solution)/shard_map/ppermute | solution.py:48
  32.0 31.8 %copy-start.1 = (bf16[144,1024]{1,0:T(8,128)(2,1)S(1)}, bf16[144,1024]{1,0:T(8,128)(2,1)}, u32[]{:S(2)}) copy-start(bf16[144,1024]{1,0:T(8,128)(2,1)} %reshape.20) | copy-start | bytes 884740
  32.0 15.1 %collective-permute-start.4 = (bf16[144,1024]{1,0:T(8,128)(2,1)}, bf16[144,1024]{1,0:T(8,128)(2,1)S(1)}, u32[]{:S(2)}, u32[]{:S(2)}) collective-permute-start(bf16[144,1024]{1,0:T(8,128)(2,1)} %reshape.20), channel_id=1, source_target_pairs={{16,4},{17,5},{18,6},{19,7},{20,8},{21,9},{22,10},{23,11},{24,12},... | collective-permute-start | bytes 884744 | tf_op jit(solution)/shard_map/ppermute | solution.py:28
  55.3 30.5 %collective-permute-start.10 = (bf16[3,2016,128]{2,1,0:T(8,128)(2,1)S(1)}, bf16[3,2016,128]{2,1,0:T(8,128)(2,1)S(1)}, u32[]{:S(2)}, u32[]{:S(2)}) collective-permute-start(bf16[3,2016,128]{2,1,0:T(8,128)(2,1)S(1)} %join.1.mine_ref), channel_id=1, source_target_pairs={{0,16},{16,0},{32,48},{48,32},{64,80},{80,64},{96,112},{112,96},{1... | collective-permute-start | bytes 4644872 | tf_op jit(solution)/shard_map/ppermute | solution.py:38
  57.3 41.4 %collective-permute-start.2 = (bf16[432,1024]{1,0:T(8,128)(2,1)S(1)}, bf16[432,1024]{1,0:T(8,128)(2,1)S(1)}, u32[]{:S(2)}, u32[]{:S(2)}) collective-permute-start(bf16[432,1024]{1,0:T(8,128)(2,1)S(1)} %reshape.19.refs_0_), channel_id=1, source_target_pairs={{0,3},{1,0},{2,1},{3,2},{4,7},{5,4},{6,5},{7,6},{8,11},{9,8},{10,9... | collective-permute-start | bytes 2654216 | tf_op jit(solution)/shard_map/ppermute | solution.py:28
  59.2 39.5 %collective-permute-start.1 = (bf16[432,1024]{1,0:T(8,128)(2,1)S(1)}, bf16[432,1024]{1,0:T(8,128)(2,1)S(1)}, u32[]{:S(2)}, u32[]{:S(2)}) collective-permute-start(bf16[432,1024]{1,0:T(8,128)(2,1)S(1)} %collective-permute-done.rest_0_.refs_1_), channel_id=1, source_target_pairs={{0,1},{1,2},{2,3},{3,0},{4,5},{5,6},{6,7},{7,4},{8,9},{9,10},{10,1... | collective-permute-start | bytes 2654216 | tf_op jit(solution)/shard_map/ppermute | solution.py:28
  63.8 34.9 %collective-permute-start.3 = (bf16[144,1024]{1,0:T(8,128)(2,1)S(1)}, bf16[144,1024]{1,0:T(8,128)(2,1)S(1)}, u32[]{:S(2)}, u32[]{:S(2)}) collective-permute-start(bf16[144,1024]{1,0:T(8,128)(2,1)S(1)} %copy-done.1), channel_id=1, source_target_pairs={{16,0},{17,1},{18,2},{19,3},{20,4},{21,5},{22,6},{23,7},{24,8},{25... | collective-permute-start | bytes 884744 | tf_op jit(solution)/shard_map/ppermute | solution.py:28
  65.7 33.0 %collective-permute-start.6 = (bf16[144,1024]{1,0:T(8,128)(2,1)S(1)}, bf16[144,1024]{1,0:T(8,128)(2,1)S(1)}, u32[]{:S(2)}, u32[]{:S(2)}) collective-permute-start(bf16[144,1024]{1,0:T(8,128)(2,1)S(1)} %copy-done.1), channel_id=1, source_target_pairs={{16,12},{17,13},{18,14},{19,15},{20,0},{21,1},{22,2},{23,3},{24,4}... | collective-permute-start | bytes 884744 | tf_op jit(solution)/shard_map/ppermute | solution.py:28
  85.8 12.9 %collective-permute-start.5 = (bf16[144,1024]{1,0:T(8,128)(2,1)S(1)}, bf16[144,1024]{1,0:T(8,128)(2,1)S(1)}, u32[]{:S(2)}, u32[]{:S(2)}) collective-permute-start(bf16[144,1024]{1,0:T(8,128)(2,1)S(1)} %collective-permute-done.4.rest_1_.refs_5_), channel_id=1, source_target_pairs={{0,4},{1,5},{2,6},{3,7},{4,8},{5,9},{6,10},{7,11},{8,12},{9,13},{1... | collective-permute-start | bytes 884744 | tf_op jit(solution)/shard_map/ppermute | solution.py:28

commit v5 on v3

--- a/solution.py
+++ b/solution.py
@@ -134,7 +134,7 @@
         turned_end[pl.ds(p, wide, stride=pairs_p), :tail] = body[:, LANES:]
         return carry
 
-    lax.fori_loop(0, pairs_p, one, 0, unroll=4)
+    lax.fori_loop(0, pairs_p, one, 0, unroll=16)
     for s in range(SIDE):
         ba_ref[s, :, :LANES] = turned_main[s * rows : (s + 1) * rows, :].astype(jnp.bfloat16)
         ba_ref[s, :, LANES:] = turned_end[s * rows : (s + 1) * rows, :tail].astype(jnp.bfloat16)
@@ -159,26 +159,29 @@
     ab_ref, ba_ref, out_ref, window, tile, total = refs[2 * SIDE :]
     wide = SIDE * own_c
     high = GROUP * own_a
+    shape = (wide, SIDE * WIN * own_c)
+    row = lax.broadcasted_iota(jnp.int32, shape, 0)
+    column = lax.broadcasted_iota(jnp.int32, shape, 1)
+    arrived = column // (WIN * own_c)
+    far = jnp.where(arrived == 1, distance[1], jnp.where(arrived == 3, distance[3], arrived))
+    kept = (column % own_c + far * own_c) == row
+    held = jnp.concatenate([partner[...] for partner in partners], 0)
+    every = jnp.concatenate([line[...] for line in lines], 0)
     for j in range(WIN):
-        rows = 0.0
-        for s in range(SIDE):
-            place = one_hot((wide, WIN * own_c), lambda r: r - distance[s] * own_c, lambda c: jnp.where((c >= j * own_c) & (c < (j + 1) * own_c), c - j * own_c, -wide - 1), jnp.bfloat16)
-            rows += jnp.dot(place, partners[s][...], preferred_element_type=jnp.float32)
-        window[j] = rows.astype(jnp.bfloat16)
+        place = jnp.where(kept & (column // own_c % WIN == j), 1.0, 0.0).astype(jnp.bfloat16)
+        window[...] = jnp.dot(place, held, preferred_element_type=jnp.float32).astype(jnp.bfloat16)
+        v = lax.dot_general(every, window[...], ROWS_BY_ROWS, preferred_element_type=jnp.float32)
+        tile[:, j] = v.astype(jnp.bfloat16).reshape(SIDE * own_c // GROUP, high, wide)
     total[...] = jnp.zeros_like(total)
+    groups = own_c // GROUP
     for s in range(SIDE):
-        for j in range(WIN):
-            v = lax.dot_general(lines[s][...], window[j], ROWS_BY_ROWS, preferred_element_type=jnp.float32)
-            tile[:, j] = v.astype(jnp.bfloat16).reshape(own_c // GROUP, high, wide)
-
-        def one(g, carry):
-            v = tile[g].reshape(WIN * high, wide)
-            at = pl.ds(pl.multiple_of(g * GROUP * pairs_p, 16), GROUP * pairs_p)
-            for i, amps in enumerate((ab_ref, ba_ref)):
-                total[i] += lax.dot_general(v, amps[distance[s], at, :], ROWS_BY_ROWS, preferred_element_type=jnp.float32)
-            return carry
-
-        lax.fori_loop(0, own_c // GROUP, one, 0, unroll=True)
+        for i, amps in enumerate((ab_ref, ba_ref)):
+            more = total[i]
+            for g in range(groups):
+                v = tile[s * groups + g].reshape(WIN * high, wide)
+                part = amps[distance[s], g * GROUP * pairs_p : (g + 1) * GROUP * pairs_p, :]
+                more += lax.dot_general(v, part, ROWS_BY_ROWS, preferred_element_type=jnp.float32)
+            total[i] = more
     shape = total.shape[1:]
     row = lax.broadcasted_iota(jnp.int32, shape, 0)
     column = lax.broadcasted_iota(jnp.int32, shape, 1)
@@ -224,11 +227,11 @@
     mine = pl.pallas_call(
         join_kernel,
         out_shape=jax.ShapeDtypeStruct(sent.shape, bf16),
-        in_specs=[vmem] * 3 + [hbm] * 4,
+        in_specs=[vmem] * 3 + [hbm] * 3,
         out_specs=vmem,
         compiler_params=params,
         name="join",
-    )(*mine, lines[1], lines[3], partners[1], partners[3])
+    )(*mine, lines[1], lines[3], partners[1])
     other = between_cores(mine)
     ab, ba = pl.pallas_call(
         functools.partial(unpack_kernel, pairs_p),
@@ -245,8 +248,8 @@
         in_specs=[smem] + [vmem] * (2 * SIDE + 2),
         out_specs=vmem,
         scratch_shapes=[
-            pltpu.VMEM((WIN, wide, aux), bf16),
-            pltpu.VMEM((own_c // GROUP, WIN, GROUP * own_a, wide), bf16),
+            pltpu.VMEM((wide, aux), bf16),
+            pltpu.VMEM((wide // GROUP, WIN, GROUP * own_a, wide), bf16),
             pltpu.VMEM((2, WIN * GROUP * own_a, GROUP * pairs_p), f32),
         ],
         compiler_params=params,

time: 117 us -> 116 us (level)
  the two profiles are of different devices: /device:TPU:16 before, /device:TPU:1 now
where the time goes in v5:
time: 116 us; the launch traced here: 115 us
  starting transfers between devices  41.9 us (36%)
  Pallas kernels  23.1 us (20%)
  waiting for transfers between devices  23 us (20%)
  blocking collectives  20.3 us (18%)
  local copies, waits for them, and re-layouts  5.43 us (5%)
    all_to_all x1, blocking collectives, shards(): lax.all_to_all(jnp.broadcast_to(part, (SIDE * SIDE, *part.shape)), 'col',...  20.3 us
    ppermute x6, starting transfers between devices, moved(): return lax.ppermute(value, ('row', 'col'), pairs)  18.4 us
    ppermute x3, waiting for transfers between devices, core_0_along_x_core_1_along_y(): return lax.ppermute(value, ('row', 'col'), pairs)  16.5 us
    ppermute x1, starting transfers between devices, from_next_row(): lax.ppermute(value, 'row', [(source, (source - 1) % rows) for source in r...  12.3 us
    pallas_call x1, Pallas kernels, shards(): pl.pallas_call(functools.partial(ladder_kernel, own_a, own_c, pairs_p), o...  11 us
    ppermute x3, starting transfers between devices, core_0_along_x_core_1_along_y(): return lax.ppermute(value, ('row', 'col'), pairs)  9.31 us
    pallas_call x1, Pallas kernels, shards(): pl.pallas_call(functools.partial(unpack_kernel, pairs_p), out_shape=(jax....  8.36 us
    ppermute x6, waiting for transfers between devices, moved(): return lax.ppermute(value, ('row', 'col'), pairs)  6.52 us
  transfers between devices with their start and end apart: 11, of which 4 were waited for; matrix products, arithmetic and copies ran while one was open for 2% of the time, Pallas kernels for 10%

profile of v5, /device:TPU:1, one launch (start us, length us, event | category | flops | bytes accessed | tf_op | source)
XLA Modules:
  0.0 114.7 jit_solution(2710041197421025176)
XLA Ops:
  0.6 1.7 %copy.5 = bf16[36,12,1024]{2,1,0:T(8,128)(2,1)S(1)} copy(bf16[36,12,1024]{2,0,1:T(8,128)(2,1)} %bitcast.16) | data formatting | bytes 1769472 | tf_op jit(solution)/shard_map/transpose | solution.py:214
  2.3 0.2 reshape.19.refs_0_
  2.5 5.2 %collective-permute-start = (bf16[432,1024]{1,0:T(8,128)(2,1)S(1)}, bf16[432,1024]{1,0:T(8,128)(2,1)S(1)}, u32[]{:S(2)}, u32[]{:S(2)}) collective-permute-start(bf16[432,1024]{1,0:T(8,128)(2,1)S(1)} %reshape.19.refs_0_), channel_id=1, source_target_pairs={{0,1},{1,2},{2,3},{3,0},{4,5},{5,6},{6,7},{7,4},{8,9},{9,10},{10,1... | collective-permute-start | bytes 2654216 | tf_op jit(solution)/shard_map/ppermute | solution.py:27
  7.8 1.9 %collective-permute-start.2 = (bf16[432,1024]{1,0:T(8,128)(2,1)S(1)}, bf16[432,1024]{1,0:T(8,128)(2,1)S(1)}, u32[]{:S(2)}, u32[]{:S(2)}) collective-permute-start(bf16[432,1024]{1,0:T(8,128)(2,1)S(1)} %reshape.19.refs_0_), channel_id=1, source_target_pairs={{0,3},{1,0},{2,1},{3,2},{4,7},{5,4},{6,5},{7,6},{8,11},{9,8},{10,9... | collective-permute-start | bytes 2654216 | tf_op jit(solution)/shard_map/ppermute | solution.py:27
  9.7 1.0 slice.12
  10.7 0.8 reshape.20
  11.5 12.3 %collective-permute-start.3 = (bf16[144,1024]{1,0:T(8,128)(2,1)}, bf16[144,1024]{1,0:T(8,128)(2,1)S(1)}, u32[]{:S(2)}, u32[]{:S(2)}) collective-permute-start(bf16[144,1024]{1,0:T(8,128)(2,1)} %reshape.20), channel_id=1, source_target_pairs={{0,752},{16,0},{32,16},{48,32},{64,48},{80,64},{96,80},{112,96},{1... | collective-permute-start | bytes 884744 | tf_op jit(solution)/shard_map/ppermute | solution.py:37
  23.8 0.1 pad_add_fusion.at_ref
  23.9 0.0 copy-start
  23.9 1.6 %copy-done = bf16[48,36,576]{2,0,1:T(8,128)(2,1)S(1)} copy-done((bf16[48,36,576]{2,0,1:T(8,128)(2,1)S(1)}, bf16[48,36,576]{2,0,1:T(8,128)(2,1)}, u32[]{:S(2)}) %copy-start) | copy-done | bytes 1990680
  25.5 2.9 %pack.1 = (bf16[3,2016,128]{2,1,0:T(8,128)(2,1)S(1)}, bf16[2,1728,144]{2,1,0:T(8,128)(2,1)S(1)}) custom-call(s32[3]{0:T(128)S(1)} %pad_add_fusion.at_ref, bf16[1728,576]{1,0:T(8,128)(2,1)S(1)} %bitcast.15), custom_call_target="tpu_custom_call" | custom-call | tf_op jit(solution)/shard_map/pack/pallas_call | solution.py:216
  28.5 0.1 slice_bitcast_fusion
  28.6 1.9 %collective-permute-start.7 = (bf16[2016,128]{1,0:T(8,128)(2,1)S(1)}, bf16[2016,128]{1,0:T(8,128)(2,1)S(1)}, u32[]{:S(2)}, u32[]{:S(2)}) collective-permute-start(bf16[2016,128]{1,0:T(8,128)(2,1)S(1)} %get-tuple-element.16), channel_id=1, source_target_pairs={{0,1},{1,2},{2,3},{3,0},{4,5},{5,6},{6,7},{7,4},{8,9},{9,10},{10,1... | collective-permute-start | bytes 1548296 | tf_op jit(solution)/shard_map/ppermute | solution.py:52
  30.5 1.9 %collective-permute-start.8 = (bf16[2016,128]{1,0:T(8,128)(2,1)S(1)}, bf16[2016,128]{1,0:T(8,128)(2,1)S(1)}, u32[]{:S(2)}, u32[]{:S(2)}) collective-permute-start(bf16[2016,128]{1,0:T(8,128)(2,1)S(1)} %get-tuple-element.15), channel_id=1, source_target_pairs={{0,2},{1,3},{2,0},{3,1},{4,6},{5,7},{6,4},{7,5},{8,10},{9,11},{10,... | collective-permute-start | bytes 1548296 | tf_op jit(solution)/shard_map/ppermute | solution.py:52
  32.4 0.0 collective-permute-done.3.refs_4_
  32.5 5.5 %collective-permute-start.9 = (bf16[2016,128]{1,0:T(8,128)(2,1)S(1)}, bf16[2016,128]{1,0:T(8,128)(2,1)S(1)}, u32[]{:S(2)}, u32[]{:S(2)}) collective-permute-start(bf16[2016,128]{1,0:T(8,128)(2,1)S(1)} %get-tuple-element.14), channel_id=1, source_target_pairs={{0,3},{1,0},{2,1},{3,2},{4,7},{5,4},{6,5},{7,6},{8,11},{9,8},{10,9... | collective-permute-start | bytes 1548296 | tf_op jit(solution)/shard_map/ppermute | solution.py:52
  37.9 8.7 %collective-permute-done.7.first = bf16[2016,128]{1,0:T(8,128)(2,1)S(1)} collective-permute-done((bf16[2016,128]{1,0:T(8,128)(2,1)S(1)}, bf16[2016,128]{1,0:T(8,128)(2,1)S(1)}, u32[]{:S(2)}, u32[]{:S(2)}) %collective-permute-start.7) | collective-permute-done | bytes 516128 | tf_op jit(solution)/shard_map/ppermute | solution.py:52
  46.6 1.9 %collective-permute-start.4 = (bf16[144,1024]{1,0:T(8,128)(2,1)S(1)}, bf16[144,1024]{1,0:T(8,128)(2,1)S(1)}, u32[]{:S(2)}, u32[]{:S(2)}) collective-permute-start(bf16[144,1024]{1,0:T(8,128)(2,1)S(1)} %collective-permute-done.3.refs_4_), channel_id=1, source_target_pairs={{0,4},{1,5},{2,6},{3,7},{4,8},{5,9},{6,10},{7,11},{8,12},{9,13},{1... | collective-permute-start | bytes 884744 | tf_op jit(solution)/shard_map/ppermute | solution.py:27
  48.5 0.0 collective-permute-done.8.second
  48.6 7.8 %collective-permute-done.9.third = bf16[2016,128]{1,0:T(8,128)(2,1)S(1)} collective-permute-done((bf16[2016,128]{1,0:T(8,128)(2,1)S(1)}, bf16[2016,128]{1,0:T(8,128)(2,1)S(1)}, u32[]{:S(2)}, u32[]{:S(2)}) %collective-permute-start.9) | collective-permute-done | bytes 516128 | tf_op jit(solution)/shard_map/ppermute | solution.py:52
  56.4 3.2 %collective-permute-done.4.rest_2_.refs_5_ = bf16[144,1024]{1,0:T(8,128)(2,1)S(1)} collective-permute-done((bf16[144,1024]{1,0:T(8,128)(2,1)S(1)}, bf16[144,1024]{1,0:T(8,128)(2,1)S(1)}, u32[]{:S(2)}, u32[]{:S(2)}) %collective-permute-start.4) | collective-permute-done | bytes 294944 | tf_op jit(solution)/shard_map/ppermute | solution.py:27
  59.5 0.0 collective-permute-done.rest_0_.refs_1_
  59.5 0.0 collective-permute-done.2.rest_1_.refs_3_
  59.5 0.1 join.1.mine_ref
  59.6 1.9 %collective-permute-start.10 = (bf16[3,2016,128]{2,1,0:T(8,128)(2,1)S(1)}, bf16[3,2016,128]{2,1,0:T(8,128)(2,1)S(1)}, u32[]{:S(2)}, u32[]{:S(2)}) collective-permute-start(bf16[3,2016,128]{2,1,0:T(8,128)(2,1)S(1)} %join.1.mine_ref), channel_id=1, source_target_pairs={{0,16},{16,0},{32,48},{48,32},{64,80},{80,64},{96,112},{112,96},{1... | collective-permute-start | bytes 4644872 | tf_op jit(solution)/shard_map/ppermute | solution.py:42
  61.6 1.9 %collective-permute-start.1 = (bf16[432,1024]{1,0:T(8,128)(2,1)S(1)}, bf16[432,1024]{1,0:T(8,128)(2,1)S(1)}, u32[]{:S(2)}, u32[]{:S(2)}) collective-permute-start(bf16[432,1024]{1,0:T(8,128)(2,1)S(1)} %collective-permute-done.rest_0_.refs_1_), channel_id=1, source_target_pairs={{0,1},{1,2},{2,3},{3,0},{4,5},{5,6},{6,7},{7,4},{8,9},{9,10},{10,1... | collective-permute-start | bytes 2654216 | tf_op jit(solution)/shard_map/ppermute | solution.py:27
  63.5 4.2 %collective-permute-start.6 = (bf16[144,1024]{1,0:T(8,128)(2,1)S(1)}, bf16[144,1024]{1,0:T(8,128)(2,1)S(1)}, u32[]{:S(2)}, u32[]{:S(2)}) collective-permute-start(bf16[144,1024]{1,0:T(8,128)(2,1)S(1)} %collective-permute-done.3.refs_4_), channel_id=1, source_target_pairs={{0,12},{1,13},{2,14},{3,15},{4,0},{5,1},{6,2},{7,3},{8,4},{9,5},{1... | collective-permute-start | bytes 884744 | tf_op jit(solution)/shard_map/ppermute | solution.py:27
  67.7 3.2 %collective-permute-start.5 = (bf16[144,1024]{1,0:T(8,128)(2,1)S(1)}, bf16[144,1024]{1,0:T(8,128)(2,1)S(1)}, u32[]{:S(2)}, u32[]{:S(2)}) collective-permute-start(bf16[144,1024]{1,0:T(8,128)(2,1)S(1)} %collective-permute-done.4.rest_2_.refs_5_), channel_id=1, source_target_pairs={{0,4},{1,5},{2,6},{3,7},{4,8},{5,9},{6,10},{7,11},{8,12},{9,13},{1... | collective-permute-start | bytes 884744 | tf_op jit(solution)/shard_map/ppermute | solution.py:27
  70.9 0.0 collective-permute-done.10.other_ref
  70.9 8.4 %unpack.1 = (bf16[4,1728,144]{2,1,0:T(8,128)(2,1)}, bf16[4,1728,144]{2,1,0:T(8,128)(2,1)}) custom-call(s32[1]{0:T(128)} %bitcast.core_ref, bf16[2,1728,144]{2,1,0:T(8,128)(2,1)S(1)} %get-tuple-element.8.own_ref, bf16[3,2016,128]{2,1,0:T(8,128)(2,1)S(1)} %join.1.mine_ref, bf16[3,2016,128]{2,1,0:T(8,128)(2,1)S(1)} %collective-permute-done.10.other_ref), custom_call_target="tpu_custom_call" | custom-call | tf_op jit(solution)/shard_map/unpack/pallas_call | solution.py:236
  79.3 0.0 collective-permute-done.6.refs_7_
  79.3 3.3 %collective-permute-done.5.refs_6_ = bf16[144,1024]{1,0:T(8,128)(2,1)S(1)} collective-permute-done((bf16[144,1024]{1,0:T(8,128)(2,1)S(1)}, bf16[144,1024]{1,0:T(8,128)(2,1)S(1)}, u32[]{:S(2)}, u32[]{:S(2)}) %collective-permute-start.5) | collective-permute-done | bytes 294944 | tf_op jit(solution)/shard_map/ppermute | solution.py:27
  82.6 0.0 collective-permute-done.1.refs_2_
  82.6 11.0 %ladders.1 = f32[48,128]{1,0:T(8,128)S(1)} custom-call(s32[1]{0:T(128)} %bitcast.core_ref, bf16[432,1024]{1,0:T(8,128)(2,1)S(1)} %reshape.19.refs_0_, bf16[432,1024]{1,0:T(8,128)(2,1)S(1)} %collective-permute-done.rest_0_.refs_1_, bf16[432,1024]{1,0:T(8,128)(2,1)S(1)} %collective-permute-done.1.refs_2_, ...), custom_call_target="tpu_custom_call" | custom-call | tf_op jit(solution)/shard_map/ladders/pallas_call | solution.py:245
  93.6 20.3 %all_to_all.5.parts_ref = f32[16,48,128]{2,1,0:T(8,128)S(1)} all-to-all(f32[16,48,128]{2,1,0:T(8,128)S(1)} %broadcast_in_dim.3), channel_id=1, replica_groups=mesh['row'=48,'col'=16] {'col'}, dimensions={0} | all-to-all | bytes 786432 | tf_op jit(solution)/shard_map/all_to_all | solution.py:258
  114.0 0.7 add.15
  (1 shorter events, 0.0 us)
Async XLA Ops:
  2.5 57.0 %collective-permute-start = (bf16[432,1024]{1,0:T(8,128)(2,1)S(1)}, bf16[432,1024]{1,0:T(8,128)(2,1)S(1)}, u32[]{:S(2)}, u32[]{:S(2)}) collective-permute-start(bf16[432,1024]{1,0:T(8,128)(2,1)S(1)} %reshape.19.refs_0_), channel_id=1, source_target_pairs={{0,1},{1,2},{2,3},{3,0},{4,5},{5,6},{6,7},{7,4},{8,9},{9,10},{10,1... | collective-permute-start | bytes 2654216 | tf_op jit(solution)/shard_map/ppermute | solution.py:27
  7.8 51.8 %collective-permute-start.2 = (bf16[432,1024]{1,0:T(8,128)(2,1)S(1)}, bf16[432,1024]{1,0:T(8,128)(2,1)S(1)}, u32[]{:S(2)}, u32[]{:S(2)}) collective-permute-start(bf16[432,1024]{1,0:T(8,128)(2,1)S(1)} %reshape.19.refs_0_), channel_id=1, source_target_pairs={{0,3},{1,0},{2,1},{3,2},{4,7},{5,4},{6,5},{7,6},{8,11},{9,8},{10,9... | collective-permute-start | bytes 2654216 | tf_op jit(solution)/shard_map/ppermute | solution.py:27
  11.5 21.0 %collective-permute-start.3 = (bf16[144,1024]{1,0:T(8,128)(2,1)}, bf16[144,1024]{1,0:T(8,128)(2,1)S(1)}, u32[]{:S(2)}, u32[]{:S(2)}) collective-permute-start(bf16[144,1024]{1,0:T(8,128)(2,1)} %reshape.20), channel_id=1, source_target_pairs={{0,752},{16,0},{32,16},{48,32},{64,48},{80,64},{96,80},{112,96},{1... | collective-permute-start | bytes 884744 | tf_op jit(solution)/shard_map/ppermute | solution.py:37
  23.9 1.6 %copy-start = (bf16[48,36,576]{2,0,1:T(8,128)(2,1)S(1)}, bf16[48,36,576]{2,0,1:T(8,128)(2,1)}, u32[]{:S(2)}) copy-start(bf16[48,36,576]{2,0,1:T(8,128)(2,1)} %param.3) | copy-start | bytes 5971972
  28.6 18.0 %collective-permute-start.7 = (bf16[2016,128]{1,0:T(8,128)(2,1)S(1)}, bf16[2016,128]{1,0:T(8,128)(2,1)S(1)}, u32[]{:S(2)}, u32[]{:S(2)}) collective-permute-start(bf16[2016,128]{1,0:T(8,128)(2,1)S(1)} %get-tuple-element.16), channel_id=1, source_target_pairs={{0,1},{1,2},{2,3},{3,0},{4,5},{5,6},{6,7},{7,4},{8,9},{9,10},{10,1... | collective-permute-start | bytes 1548296 | tf_op jit(solution)/shard_map/ppermute | solution.py:52
  30.5 18.0 %collective-permute-start.8 = (bf16[2016,128]{1,0:T(8,128)(2,1)S(1)}, bf16[2016,128]{1,0:T(8,128)(2,1)S(1)}, u32[]{:S(2)}, u32[]{:S(2)}) collective-permute-start(bf16[2016,128]{1,0:T(8,128)(2,1)S(1)} %get-tuple-element.15), channel_id=1, source_target_pairs={{0,2},{1,3},{2,0},{3,1},{4,6},{5,7},{6,4},{7,5},{8,10},{9,11},{10,... | collective-permute-start | bytes 1548296 | tf_op jit(solution)/shard_map/ppermute | solution.py:52
  32.5 23.9 %collective-permute-start.9 = (bf16[2016,128]{1,0:T(8,128)(2,1)S(1)}, bf16[2016,128]{1,0:T(8,128)(2,1)S(1)}, u32[]{:S(2)}, u32[]{:S(2)}) collective-permute-start(bf16[2016,128]{1,0:T(8,128)(2,1)S(1)} %get-tuple-element.14), channel_id=1, source_target_pairs={{0,3},{1,0},{2,1},{3,2},{4,7},{5,4},{6,5},{7,6},{8,11},{9,8},{10,9... | collective-permute-start | bytes 1548296 | tf_op jit(solution)/shard_map/ppermute | solution.py:52
  46.6 12.9 %collective-permute-start.4 = (bf16[144,1024]{1,0:T(8,128)(2,1)S(1)}, bf16[144,1024]{1,0:T(8,128)(2,1)S(1)}, u32[]{:S(2)}, u32[]{:S(2)}) collective-permute-start(bf16[144,1024]{1,0:T(8,128)(2,1)S(1)} %collective-permute-done.3.refs_4_), channel_id=1, source_target_pairs={{0,4},{1,5},{2,6},{3,7},{4,8},{5,9},{6,10},{7,11},{8,12},{9,13},{1... | collective-permute-start | bytes 884744 | tf_op jit(solution)/shard_map/ppermute | solution.py:27
  59.6 11.3 %collective-permute-start.10 = (bf16[3,2016,128]{2,1,0:T(8,128)(2,1)S(1)}, bf16[3,2016,128]{2,1,0:T(8,128)(2,1)S(1)}, u32[]{:S(2)}, u32[]{:S(2)}) collective-permute-start(bf16[3,2016,128]{2,1,0:T(8,128)(2,1)S(1)} %join.1.mine_ref), channel_id=1, source_target_pairs={{0,16},{16,0},{32,48},{48,32},{64,80},{80,64},{96,112},{112,96},{1... | collective-permute-start | bytes 4644872 | tf_op jit(solution)/shard_map/ppermute | solution.py:42
  61.6 21.1 %collective-permute-start.1 = (bf16[432,1024]{1,0:T(8,128)(2,1)S(1)}, bf16[432,1024]{1,0:T(8,128)(2,1)S(1)}, u32[]{:S(2)}, u32[]{:S(2)}) collective-permute-start(bf16[432,1024]{1,0:T(8,128)(2,1)S(1)} %collective-permute-done.rest_0_.refs_1_), channel_id=1, source_target_pairs={{0,1},{1,2},{2,3},{3,0},{4,5},{5,6},{6,7},{7,4},{8,9},{9,10},{10,1... | collective-permute-start | bytes 2654216 | tf_op jit(solution)/shard_map/ppermute | solution.py:27
  63.5 15.8 %collective-permute-start.6 = (bf16[144,1024]{1,0:T(8,128)(2,1)S(1)}, bf16[144,1024]{1,0:T(8,128)(2,1)S(1)}, u32[]{:S(2)}, u32[]{:S(2)}) collective-permute-start(bf16[144,1024]{1,0:T(8,128)(2,1)S(1)} %collective-permute-done.3.refs_4_), channel_id=1, source_target_pairs={{0,12},{1,13},{2,14},{3,15},{4,0},{5,1},{6,2},{7,3},{8,4},{9,5},{1... | collective-permute-start | bytes 884744 | tf_op jit(solution)/shard_map/ppermute | solution.py:27
  67.7 14.9 %collective-permute-start.5 = (bf16[144,1024]{1,0:T(8,128)(2,1)S(1)}, bf16[144,1024]{1,0:T(8,128)(2,1)S(1)}, u32[]{:S(2)}, u32[]{:S(2)}) collective-permute-start(bf16[144,1024]{1,0:T(8,128)(2,1)S(1)} %collective-permute-done.4.rest_2_.refs_5_), channel_id=1, source_target_pairs={{0,4},{1,5},{2,6},{3,7},{4,8},{5,9},{6,10},{7,11},{8,12},{9,13},{1... | collective-permute-start | bytes 884744 | tf_op jit(solution)/shard_map/ppermute | solution.py:27

commit v6 on v5

--- a/solution.py
+++ b/solution.py
@@ -97,7 +97,8 @@
         sent_ref[i, rows:, :] = carry[i].astype(jnp.bfloat16)
 
 
-def unpack_kernel(pairs_p, core_ref, own_ref, mine_ref, other_ref, ab_ref, ba_ref, main, end, turned_main, turned_end):
+def unpack_kernel(pairs_p, core_ref, own_ref, mine_ref, other_ref, *refs):
+    ab_ref, ba_ref, main, end, turned_main, turned_end = refs[-6:]
     core = core_ref[0]
     rows, wide = ab_ref.shape[1:]
     part = rows // CHUNKS
@@ -227,21 +228,21 @@
     mine = pl.pallas_call(
         join_kernel,
         out_shape=jax.ShapeDtypeStruct(sent.shape, bf16),
-        in_specs=[vmem] * 3 + [hbm] * 3,
+        in_specs=[vmem] * 3 + [hbm] * 2,
         out_specs=vmem,
         compiler_params=params,
         name="join",
-    )(*mine, lines[1], lines[3], partners[1])
+    )(*mine, lines[1], partners[0])
     other = between_cores(mine)
     ab, ba = pl.pallas_call(
         functools.partial(unpack_kernel, pairs_p),
         out_shape=(jax.ShapeDtypeStruct((SIDE, rows, wide), bf16),) * 2,
-        in_specs=[smem, vmem, vmem, vmem],
+        in_specs=[smem, vmem, vmem, vmem] + [hbm] * 1,
         out_specs=(vmem, vmem),
         scratch_shapes=[pltpu.VMEM((SIDE * rows, LANES), f32)] * 4,
         compiler_params=params,
         name="unpack",
-    )(at[2:], own, mine, other)
+    )(at[2:], own, mine, other, partners[1])
     part = pl.pallas_call(
         functools.partial(ladder_kernel, own_a, own_c, pairs_p),
         out_shape=jax.ShapeDtypeStruct((own_a * WIN, LANES), f32),

time: 116 us -> 121 us (1.043)
  the two profiles are of different devices: /device:TPU:1 before, /device:TPU:8 now
where the time goes in v6:
time: 121 us; the launch traced here: 120 us
  starting transfers between devices  50.7 us (42%)
  Pallas kernels  24.4 us (20%)
  waiting for transfers between devices  18.4 us (15%)
  blocking collectives  17.7 us (15%)
  local copies, waits for them, and re-layouts  8.2 us (7%)
    ppermute x6, starting transfers between devices, moved(): return lax.ppermute(value, ('row', 'col'), pairs)  19.1 us
    ppermute x1, starting transfers between devices, from_next_row(): lax.ppermute(value, 'row', [(source, (source - 1) % rows) for source in r...  18.6 us
    all_to_all x1, blocking collectives, shards(): lax.all_to_all(jnp.broadcast_to(part, (SIDE * SIDE, *part.shape)), 'col',...  17.7 us
    ppermute x6, waiting for transfers between devices, moved(): return lax.ppermute(value, ('row', 'col'), pairs)  12.9 us
    ppermute x3, starting transfers between devices, core_0_along_x_core_1_along_y(): return lax.ppermute(value, ('row', 'col'), pairs)  11.1 us
    pallas_call x1, Pallas kernels, shards(): pl.pallas_call(functools.partial(ladder_kernel, own_a, own_c, pairs_p), o...  11 us
    pallas_call x1, Pallas kernels, shards(): pl.pallas_call(functools.partial(unpack_kernel, pairs_p), out_shape=(jax....  8.37 us
    ppermute x1, waiting for transfers between devices, from_next_row(): lax.ppermute(value, 'row', [(source, (source - 1) % rows) for source in r...  5.52 us
  transfers between devices with their start and end apart: 11, of which 3 were waited for; matrix products, arithmetic and copies ran while one was open for 4% of the time, Pallas kernels for 9%

profile of v6, /device:TPU:8, one launch (start us, length us, event | category | flops | bytes accessed | tf_op | source)
XLA Modules:
  0.0 120.4 jit_solution(12405685218040155035)
XLA Ops:
  0.6 1.7 %copy.5 = bf16[36,12,1024]{2,1,0:T(8,128)(2,1)S(1)} copy(bf16[36,12,1024]{2,0,1:T(8,128)(2,1)} %bitcast.16) | data formatting | bytes 1769472 | tf_op jit(solution)/shard_map/transpose | solution.py:215
  2.3 0.2 reshape.19.refs_0_
  2.5 3.4 %collective-permute-start = (bf16[432,1024]{1,0:T(8,128)(2,1)S(1)}, bf16[432,1024]{1,0:T(8,128)(2,1)S(1)}, u32[]{:S(2)}, u32[]{:S(2)}) collective-permute-start(bf16[432,1024]{1,0:T(8,128)(2,1)S(1)} %reshape.19.refs_0_), channel_id=1, source_target_pairs={{0,1},{1,2},{2,3},{3,0},{4,5},{5,6},{6,7},{7,4},{8,9},{9,10},{10,1... | collective-permute-start | bytes 2654216 | tf_op jit(solution)/shard_map/ppermute | solution.py:27
  6.0 0.1 pad_add_fusion.at_ref
  6.1 0.0 copy-start
  6.1 1.6 %copy-done = bf16[48,36,576]{2,0,1:T(8,128)(2,1)S(1)} copy-done((bf16[48,36,576]{2,0,1:T(8,128)(2,1)S(1)}, bf16[48,36,576]{2,0,1:T(8,128)(2,1)}, u32[]{:S(2)}) %copy-start) | copy-done | bytes 1990680
  7.7 2.9 %pack.1 = (bf16[3,2016,128]{2,1,0:T(8,128)(2,1)S(1)}, bf16[2,1728,144]{2,1,0:T(8,128)(2,1)S(1)}) custom-call(s32[3]{0:T(128)S(1)} %pad_add_fusion.at_ref, bf16[1728,576]{1,0:T(8,128)(2,1)S(1)} %bitcast.15), custom_call_target="tpu_custom_call" | custom-call | tf_op jit(solution)/shard_map/pack/pallas_call | solution.py:217
  10.6 1.2 slice_bitcast_fusion
  11.8 3.4 %collective-permute-start.7 = (bf16[2016,128]{1,0:T(8,128)(2,1)}, bf16[2016,128]{1,0:T(8,128)(2,1)}, u32[]{:S(2)}, u32[]{:S(2)}) collective-permute-start(bf16[2016,128]{1,0:T(8,128)(2,1)} %get-tuple-element.16), channel_id=1, source_target_pairs={{0,1},{1,2},{2,3},{3,0},{4,5},{5,6},{6,7},{7,4},{8,9},{9,10},{10,1... | collective-permute-start | bytes 1548296 | tf_op jit(solution)/shard_map/ppermute | solution.py:52
  15.2 3.6 %collective-permute-start.8 = (bf16[2016,128]{1,0:T(8,128)(2,1)}, bf16[2016,128]{1,0:T(8,128)(2,1)}, u32[]{:S(2)}, u32[]{:S(2)}) collective-permute-start(bf16[2016,128]{1,0:T(8,128)(2,1)} %get-tuple-element.15), channel_id=1, source_target_pairs={{0,2},{1,3},{2,0},{3,1},{4,6},{5,7},{6,4},{7,5},{8,10},{9,11},{10,... | collective-permute-start | bytes 1548296 | tf_op jit(solution)/shard_map/ppermute | solution.py:52
  18.8 4.1 %collective-permute-start.9 = (bf16[2016,128]{1,0:T(8,128)(2,1)}, bf16[2016,128]{1,0:T(8,128)(2,1)}, u32[]{:S(2)}, u32[]{:S(2)}) collective-permute-start(bf16[2016,128]{1,0:T(8,128)(2,1)} %get-tuple-element.14), channel_id=1, source_target_pairs={{0,3},{1,0},{2,1},{3,2},{4,7},{5,4},{6,5},{7,6},{8,11},{9,8},{10,9... | collective-permute-start | bytes 1548296 | tf_op jit(solution)/shard_map/ppermute | solution.py:52
  22.9 1.7 %slice.12 = bf16[4,36,1024]{2,1,0:T(8,128)(2,1)} slice(bf16[12,36,1024]{2,1,0:T(8,128)(2,1)} %param.2), slice={[0:4], [0:36], [0:1024]} | slice | bytes 589824 | tf_op jit(solution)/shard_map/slice | solution.py:214
  24.6 1.7 %reshape.20 = bf16[144,1024]{1,0:T(8,128)(2,1)} reshape(bf16[4,36,1024]{2,1,0:T(8,128)(2,1)} %slice.12) | data formatting | bytes 589824 | tf_op jit(solution)/shard_map/reshape | solution.py:214
  26.4 18.6 %collective-permute-start.3 = (bf16[144,1024]{1,0:T(8,128)(2,1)}, bf16[144,1024]{1,0:T(8,128)(2,1)S(1)}, u32[]{:S(2)}, u32[]{:S(2)}) collective-permute-start(bf16[144,1024]{1,0:T(8,128)(2,1)} %reshape.20), channel_id=1, source_target_pairs={{0,752},{16,0},{32,16},{48,32},{64,48},{80,64},{96,80},{112,96},{1... | collective-permute-start | bytes 884744 | tf_op jit(solution)/shard_map/ppermute | solution.py:37
  45.0 5.5 %collective-permute-done.3.rest_1_.refs_4_ = bf16[144,1024]{1,0:T(8,128)(2,1)S(1)} collective-permute-done((bf16[144,1024]{1,0:T(8,128)(2,1)}, bf16[144,1024]{1,0:T(8,128)(2,1)S(1)}, u32[]{:S(2)}, u32[]{:S(2)}) %collective-permute-start.3) | collective-permute-done | bytes 294944 | tf_op jit(solution)/shard_map/ppermute | solution.py:37
  50.5 0.0 collective-permute-done.7.first
  50.5 0.0 collective-permute-done.8.second
  50.6 0.0 collective-permute-done.9.third
  50.6 0.0 collective-permute-done.rest_0_.refs_1_
  50.6 1.5 %join.1.mine_ref = bf16[3,2016,128]{2,1,0:T(8,128)(2,1)S(1)} custom-call(bf16[2016,128]{1,0:T(8,128)(2,1)} %collective-permute-done.7.first, bf16[2016,128]{1,0:T(8,128)(2,1)} %collective-permute-done.8.second, bf16[2016,128]{1,0:T(8,128)(2,1)} %collective-permute-done.9.third, bf16[432,1024]{1,0:T(8,128)(2,1)S(1)} %collective-permute-done.rest_0_.refs_1_, ...), custom_call_target="tpu_custom_call" | custom-call | tf_op jit(solution)/shard_map/join/pallas_call | solution.py:228
  52.0 1.9 %collective-permute-start.10 = (bf16[3,2016,128]{2,1,0:T(8,128)(2,1)S(1)}, bf16[3,2016,128]{2,1,0:T(8,128)(2,1)S(1)}, u32[]{:S(2)}, u32[]{:S(2)}) collective-permute-start(bf16[3,2016,128]{2,1,0:T(8,128)(2,1)S(1)} %join.1.mine_ref), channel_id=1, source_target_pairs={{0,16},{16,0},{32,48},{48,32},{64,80},{80,64},{96,112},{112,96},{1... | collective-permute-start | bytes 4644872 | tf_op jit(solution)/shard_map/ppermute | solution.py:42
  54.0 2.7 %collective-permute-start.2 = (bf16[432,1024]{1,0:T(8,128)(2,1)S(1)}, bf16[432,1024]{1,0:T(8,128)(2,1)S(1)}, u32[]{:S(2)}, u32[]{:S(2)}) collective-permute-start(bf16[432,1024]{1,0:T(8,128)(2,1)S(1)} %reshape.19.refs_0_), channel_id=1, source_target_pairs={{0,3},{1,0},{2,1},{3,2},{4,7},{5,4},{6,5},{7,6},{8,11},{9,8},{10,9... | collective-permute-start | bytes 2654216 | tf_op jit(solution)/shard_map/ppermute | solution.py:27
  56.7 3.1 %collective-permute-start.1 = (bf16[432,1024]{1,0:T(8,128)(2,1)S(1)}, bf16[432,1024]{1,0:T(8,128)(2,1)S(1)}, u32[]{:S(2)}, u32[]{:S(2)}) collective-permute-start(bf16[432,1024]{1,0:T(8,128)(2,1)S(1)} %collective-permute-done.rest_0_.refs_1_), channel_id=1, source_target_pairs={{0,1},{1,2},{2,3},{3,0},{4,5},{5,6},{6,7},{7,4},{8,9},{9,10},{10,1... | collective-permute-start | bytes 2654216 | tf_op jit(solution)/shard_map/ppermute | solution.py:27
  59.8 1.9 %collective-permute-start.4 = (bf16[144,1024]{1,0:T(8,128)(2,1)S(1)}, bf16[144,1024]{1,0:T(8,128)(2,1)S(1)}, u32[]{:S(2)}, u32[]{:S(2)}) collective-permute-start(bf16[144,1024]{1,0:T(8,128)(2,1)S(1)} %collective-permute-done.3.rest_1_.refs_4_), channel_id=1, source_target_pairs={{0,4},{1,5},{2,6},{3,7},{4,8},{5,9},{6,10},{7,11},{8,12},{9,13},{1... | collective-permute-start | bytes 884744 | tf_op jit(solution)/shard_map/ppermute | solution.py:27
  61.7 6.0 %collective-permute-start.6 = (bf16[144,1024]{1,0:T(8,128)(2,1)S(1)}, bf16[144,1024]{1,0:T(8,128)(2,1)S(1)}, u32[]{:S(2)}, u32[]{:S(2)}) collective-permute-start(bf16[144,1024]{1,0:T(8,128)(2,1)S(1)} %collective-permute-done.3.rest_1_.refs_4_), channel_id=1, source_target_pairs={{0,12},{1,13},{2,14},{3,15},{4,0},{5,1},{6,2},{7,3},{8,4},{9,5},{1... | collective-permute-start | bytes 884744 | tf_op jit(solution)/shard_map/ppermute | solution.py:27
  67.8 11.4 %collective-permute-done.4.refs_0_.refs_5_ = bf16[144,1024]{1,0:T(8,128)(2,1)S(1)} collective-permute-done((bf16[144,1024]{1,0:T(8,128)(2,1)S(1)}, bf16[144,1024]{1,0:T(8,128)(2,1)S(1)}, u32[]{:S(2)}, u32[]{:S(2)}) %collective-permute-start.4) | collective-permute-done | bytes 294944 | tf_op jit(solution)/shard_map/ppermute | solution.py:27
  79.2 1.9 %collective-permute-start.5 = (bf16[144,1024]{1,0:T(8,128)(2,1)S(1)}, bf16[144,1024]{1,0:T(8,128)(2,1)S(1)}, u32[]{:S(2)}, u32[]{:S(2)}) collective-permute-start(bf16[144,1024]{1,0:T(8,128)(2,1)S(1)} %collective-permute-done.4.refs_0_.refs_5_), channel_id=1, source_target_pairs={{0,4},{1,5},{2,6},{3,7},{4,8},{5,9},{6,10},{7,11},{8,12},{9,13},{1... | collective-permute-start | bytes 884744 | tf_op jit(solution)/shard_map/ppermute | solution.py:27
  81.1 0.0 collective-permute-done.10.other_ref
  81.1 8.4 %unpack.1 = (bf16[4,1728,144]{2,1,0:T(8,128)(2,1)}, bf16[4,1728,144]{2,1,0:T(8,128)(2,1)}) custom-call(s32[1]{0:T(128)} %bitcast.core_ref, bf16[2,1728,144]{2,1,0:T(8,128)(2,1)S(1)} %get-tuple-element.8.own_ref, bf16[3,2016,128]{2,1,0:T(8,128)(2,1)S(1)} %join.1.mine_ref, bf16[3,2016,128]{2,1,0:T(8,128)(2,1)S(1)} %collective-permute-done.10.other_ref, ...), custom_call_target="tpu_custom_call" | custom-call | tf_op jit(solution)/shard_map/unpack/pallas_call | solution.py:237
  89.5 0.0 collective-permute-done.6.refs_7_
  89.5 1.5 %collective-permute-done.5.refs_6_ = bf16[144,1024]{1,0:T(8,128)(2,1)S(1)} collective-permute-done((bf16[144,1024]{1,0:T(8,128)(2,1)S(1)}, bf16[144,1024]{1,0:T(8,128)(2,1)S(1)}, u32[]{:S(2)}, u32[]{:S(2)}) %collective-permute-start.5) | collective-permute-done | bytes 294944 | tf_op jit(solution)/shard_map/ppermute | solution.py:27
  91.0 0.0 collective-permute-done.2.refs_3_
  91.0 0.0 collective-permute-done.1.refs_2_
  91.0 11.0 %ladders.1 = f32[48,128]{1,0:T(8,128)S(1)} custom-call(s32[1]{0:T(128)} %bitcast.core_ref, bf16[432,1024]{1,0:T(8,128)(2,1)S(1)} %reshape.19.refs_0_, bf16[432,1024]{1,0:T(8,128)(2,1)S(1)} %collective-permute-done.rest_0_.refs_1_, bf16[432,1024]{1,0:T(8,128)(2,1)S(1)} %collective-permute-done.1.refs_2_, ...), custom_call_target="tpu_custom_call" | custom-call | tf_op jit(solution)/shard_map/ladders/pallas_call | solution.py:246
  102.0 17.7 %all_to_all.5.parts_ref = f32[16,48,128]{2,1,0:T(8,128)S(1)} all-to-all(f32[16,48,128]{2,1,0:T(8,128)S(1)} %broadcast_in_dim.3), channel_id=1, replica_groups=mesh['row'=48,'col'=16] {'col'}, dimensions={0} | all-to-all | bytes 786432 | tf_op jit(solution)/shard_map/all_to_all | solution.py:259
  119.7 0.7 add.15
  (1 shorter events, 0.0 us)
Async XLA Ops:
  2.5 48.0 %collective-permute-start = (bf16[432,1024]{1,0:T(8,128)(2,1)S(1)}, bf16[432,1024]{1,0:T(8,128)(2,1)S(1)}, u32[]{:S(2)}, u32[]{:S(2)}) collective-permute-start(bf16[432,1024]{1,0:T(8,128)(2,1)S(1)} %reshape.19.refs_0_), channel_id=1, source_target_pairs={{0,1},{1,2},{2,3},{3,0},{4,5},{5,6},{6,7},{7,4},{8,9},{9,10},{10,1... | collective-permute-start | bytes 2654216 | tf_op jit(solution)/shard_map/ppermute | solution.py:27
  6.1 1.6 %copy-start = (bf16[48,36,576]{2,0,1:T(8,128)(2,1)S(1)}, bf16[48,36,576]{2,0,1:T(8,128)(2,1)}, u32[]{:S(2)}) copy-start(bf16[48,36,576]{2,0,1:T(8,128)(2,1)} %param.3) | copy-start | bytes 5971972
  11.8 38.7 %collective-permute-start.7 = (bf16[2016,128]{1,0:T(8,128)(2,1)}, bf16[2016,128]{1,0:T(8,128)(2,1)}, u32[]{:S(2)}, u32[]{:S(2)}) collective-permute-start(bf16[2016,128]{1,0:T(8,128)(2,1)} %get-tuple-element.16), channel_id=1, source_target_pairs={{0,1},{1,2},{2,3},{3,0},{4,5},{5,6},{6,7},{7,4},{8,9},{9,10},{10,1... | collective-permute-start | bytes 1548296 | tf_op jit(solution)/shard_map/ppermute | solution.py:52
  15.2 35.3 %collective-permute-start.8 = (bf16[2016,128]{1,0:T(8,128)(2,1)}, bf16[2016,128]{1,0:T(8,128)(2,1)}, u32[]{:S(2)}, u32[]{:S(2)}) collective-permute-start(bf16[2016,128]{1,0:T(8,128)(2,1)} %get-tuple-element.15), channel_id=1, source_target_pairs={{0,2},{1,3},{2,0},{3,1},{4,6},{5,7},{6,4},{7,5},{8,10},{9,11},{10,... | collective-permute-start | bytes 1548296 | tf_op jit(solution)/shard_map/ppermute | solution.py:52
  18.8 31.7 %collective-permute-start.9 = (bf16[2016,128]{1,0:T(8,128)(2,1)}, bf16[2016,128]{1,0:T(8,128)(2,1)}, u32[]{:S(2)}, u32[]{:S(2)}) collective-permute-start(bf16[2016,128]{1,0:T(8,128)(2,1)} %get-tuple-element.14), channel_id=1, source_target_pairs={{0,3},{1,0},{2,1},{3,2},{4,7},{5,4},{6,5},{7,6},{8,11},{9,8},{10,9... | collective-permute-start | bytes 1548296 | tf_op jit(solution)/shard_map/ppermute | solution.py:52
  26.4 24.2 %collective-permute-start.3 = (bf16[144,1024]{1,0:T(8,128)(2,1)}, bf16[144,1024]{1,0:T(8,128)(2,1)S(1)}, u32[]{:S(2)}, u32[]{:S(2)}) collective-permute-start(bf16[144,1024]{1,0:T(8,128)(2,1)} %reshape.20), channel_id=1, source_target_pairs={{0,752},{16,0},{32,16},{48,32},{64,48},{80,64},{96,80},{112,96},{1... | collective-permute-start | bytes 884744 | tf_op jit(solution)/shard_map/ppermute | solution.py:37
  52.0 29.1 %collective-permute-start.10 = (bf16[3,2016,128]{2,1,0:T(8,128)(2,1)S(1)}, bf16[3,2016,128]{2,1,0:T(8,128)(2,1)S(1)}, u32[]{:S(2)}, u32[]{:S(2)}) collective-permute-start(bf16[3,2016,128]{2,1,0:T(8,128)(2,1)S(1)} %join.1.mine_ref), channel_id=1, source_target_pairs={{0,16},{16,0},{32,48},{48,32},{64,80},{80,64},{96,112},{112,96},{1... | collective-permute-start | bytes 4644872 | tf_op jit(solution)/shard_map/ppermute | solution.py:42
  54.0 37.0 %collective-permute-start.2 = (bf16[432,1024]{1,0:T(8,128)(2,1)S(1)}, bf16[432,1024]{1,0:T(8,128)(2,1)S(1)}, u32[]{:S(2)}, u32[]{:S(2)}) collective-permute-start(bf16[432,1024]{1,0:T(8,128)(2,1)S(1)} %reshape.19.refs_0_), channel_id=1, source_target_pairs={{0,3},{1,0},{2,1},{3,2},{4,7},{5,4},{6,5},{7,6},{8,11},{9,8},{10,9... | collective-permute-start | bytes 2654216 | tf_op jit(solution)/shard_map/ppermute | solution.py:27
  56.7 34.3 %collective-permute-start.1 = (bf16[432,1024]{1,0:T(8,128)(2,1)S(1)}, bf16[432,1024]{1,0:T(8,128)(2,1)S(1)}, u32[]{:S(2)}, u32[]{:S(2)}) collective-permute-start(bf16[432,1024]{1,0:T(8,128)(2,1)S(1)} %collective-permute-done.rest_0_.refs_1_), channel_id=1, source_target_pairs={{0,1},{1,2},{2,3},{3,0},{4,5},{5,6},{6,7},{7,4},{8,9},{9,10},{10,1... | collective-permute-start | bytes 2654216 | tf_op jit(solution)/shard_map/ppermute | solution.py:27
  59.8 19.4 %collective-permute-start.4 = (bf16[144,1024]{1,0:T(8,128)(2,1)S(1)}, bf16[144,1024]{1,0:T(8,128)(2,1)S(1)}, u32[]{:S(2)}, u32[]{:S(2)}) collective-permute-start(bf16[144,1024]{1,0:T(8,128)(2,1)S(1)} %collective-permute-done.3.rest_1_.refs_4_), channel_id=1, source_target_pairs={{0,4},{1,5},{2,6},{3,7},{4,8},{5,9},{6,10},{7,11},{8,12},{9,13},{1... | collective-permute-start | bytes 884744 | tf_op jit(solution)/shard_map/ppermute | solution.py:27
  61.7 27.7 %collective-permute-start.6 = (bf16[144,1024]{1,0:T(8,128)(2,1)S(1)}, bf16[144,1024]{1,0:T(8,128)(2,1)S(1)}, u32[]{:S(2)}, u32[]{:S(2)}) collective-permute-start(bf16[144,1024]{1,0:T(8,128)(2,1)S(1)} %collective-permute-done.3.rest_1_.refs_4_), channel_id=1, source_target_pairs={{0,12},{1,13},{2,14},{3,15},{4,0},{5,1},{6,2},{7,3},{8,4},{9,5},{1... | collective-permute-start | bytes 884744 | tf_op jit(solution)/shard_map/ppermute | solution.py:27
  79.2 11.8 %collective-permute-start.5 = (bf16[144,1024]{1,0:T(8,128)(2,1)S(1)}, bf16[144,1024]{1,0:T(8,128)(2,1)S(1)}, u32[]{:S(2)}, u32[]{:S(2)}) collective-permute-start(bf16[144,1024]{1,0:T(8,128)(2,1)S(1)} %collective-permute-done.4.refs_0_.refs_5_), channel_id=1, source_target_pairs={{0,4},{1,5},{2,6},{3,7},{4,8},{5,9},{6,10},{7,11},{8,12},{9,13},{1... | collective-permute-start | bytes 884744 | tf_op jit(solution)/shard_map/ppermute | solution.py:27

commit v7 on v5

--- a/solution.py
+++ b/solution.py
@@ -134,7 +134,7 @@
         turned_end[pl.ds(p, wide, stride=pairs_p), :tail] = body[:, LANES:]
         return carry
 
-    lax.fori_loop(0, pairs_p, one, 0, unroll=16)
+    lax.fori_loop(0, pairs_p, one, 0, unroll=True)
     for s in range(SIDE):
         ba_ref[s, :, :LANES] = turned_main[s * rows : (s + 1) * rows, :].astype(jnp.bfloat16)
         ba_ref[s, :, LANES:] = turned_end[s * rows : (s + 1) * rows, :tail].astype(jnp.bfloat16)

time: 116 us -> 116 us (level)
  transfers between devices with their start and end apart: 11 -> 11, of which waited for: 4 -> 4; matrix products, arithmetic and copies ran while one was open for 2% -> 2% of each run, Pallas kernels for 10% -> 9%
where the time goes in v7:
time: 116 us; the launch traced here: 115 us
  starting transfers between devices  41.9 us (36%)
  waiting for transfers between devices  23.7 us (20%)
  Pallas kernels  22.4 us (19%)
  blocking collectives  20.3 us (18%)
  local copies, waits for them, and re-layouts  5.43 us (5%)
    all_to_all x1, blocking collectives, shards(): lax.all_to_all(jnp.broadcast_to(part, (SIDE * SIDE, *part.shape)), 'col',...  20.3 us
    ppermute x6, starting transfers between devices, moved(): return lax.ppermute(value, ('row', 'col'), pairs)  18.4 us
    ppermute x3, waiting for transfers between devices, core_0_along_x_core_1_along_y(): return lax.ppermute(value, ('row', 'col'), pairs)  16.5 us
    ppermute x1, starting transfers between devices, from_next_row(): lax.ppermute(value, 'row', [(source, (source - 1) % rows) for source in r...  12.3 us
    pallas_call x1, Pallas kernels, shards(): pl.pallas_call(functools.partial(ladder_kernel, own_a, own_c, pairs_p), o...  11 us
    ppermute x3, starting transfers between devices, core_0_along_x_core_1_along_y(): return lax.ppermute(value, ('row', 'col'), pairs)  9.31 us
    pallas_call x1, Pallas kernels, shards(): pl.pallas_call(functools.partial(unpack_kernel, pairs_p), out_shape=(jax....  7.7 us
    ppermute x6, waiting for transfers between devices, moved(): return lax.ppermute(value, ('row', 'col'), pairs)  7.18 us
  transfers between devices with their start and end apart: 11, of which 4 were waited for; matrix products, arithmetic and copies ran while one was open for 2% of the time, Pallas kernels for 9%

profile of v7, /device:TPU:1, one launch (start us, length us, event | category | flops | bytes accessed | tf_op | source)
XLA Modules:
  0.0 114.7 jit_solution(12594833224557525930)
XLA Ops:
  0.6 1.7 %copy.5 = bf16[36,12,1024]{2,1,0:T(8,128)(2,1)S(1)} copy(bf16[36,12,1024]{2,0,1:T(8,128)(2,1)} %bitcast.16) | data formatting | bytes 1769472 | tf_op jit(solution)/shard_map/transpose | solution.py:214
  2.3 0.2 reshape.19.refs_0_
  2.5 5.2 %collective-permute-start = (bf16[432,1024]{1,0:T(8,128)(2,1)S(1)}, bf16[432,1024]{1,0:T(8,128)(2,1)S(1)}, u32[]{:S(2)}, u32[]{:S(2)}) collective-permute-start(bf16[432,1024]{1,0:T(8,128)(2,1)S(1)} %reshape.19.refs_0_), channel_id=1, source_target_pairs={{0,1},{1,2},{2,3},{3,0},{4,5},{5,6},{6,7},{7,4},{8,9},{9,10},{10,1... | collective-permute-start | bytes 2654216 | tf_op jit(solution)/shard_map/ppermute | solution.py:27
  7.8 1.9 %collective-permute-start.2 = (bf16[432,1024]{1,0:T(8,128)(2,1)S(1)}, bf16[432,1024]{1,0:T(8,128)(2,1)S(1)}, u32[]{:S(2)}, u32[]{:S(2)}) collective-permute-start(bf16[432,1024]{1,0:T(8,128)(2,1)S(1)} %reshape.19.refs_0_), channel_id=1, source_target_pairs={{0,3},{1,0},{2,1},{3,2},{4,7},{5,4},{6,5},{7,6},{8,11},{9,8},{10,9... | collective-permute-start | bytes 2654216 | tf_op jit(solution)/shard_map/ppermute | solution.py:27
  9.7 1.0 slice.12
  10.7 0.8 reshape.20
  11.5 12.3 %collective-permute-start.3 = (bf16[144,1024]{1,0:T(8,128)(2,1)}, bf16[144,1024]{1,0:T(8,128)(2,1)S(1)}, u32[]{:S(2)}, u32[]{:S(2)}) collective-permute-start(bf16[144,1024]{1,0:T(8,128)(2,1)} %reshape.20), channel_id=1, source_target_pairs={{0,752},{16,0},{32,16},{48,32},{64,48},{80,64},{96,80},{112,96},{1... | collective-permute-start | bytes 884744 | tf_op jit(solution)/shard_map/ppermute | solution.py:37
  23.8 0.1 pad_add_fusion.at_ref
  23.9 0.0 copy-start
  23.9 1.6 %copy-done = bf16[48,36,576]{2,0,1:T(8,128)(2,1)S(1)} copy-done((bf16[48,36,576]{2,0,1:T(8,128)(2,1)S(1)}, bf16[48,36,576]{2,0,1:T(8,128)(2,1)}, u32[]{:S(2)}) %copy-start) | copy-done | bytes 1990680
  25.5 2.9 %pack.1 = (bf16[3,2016,128]{2,1,0:T(8,128)(2,1)S(1)}, bf16[2,1728,144]{2,1,0:T(8,128)(2,1)S(1)}) custom-call(s32[3]{0:T(128)S(1)} %pad_add_fusion.at_ref, bf16[1728,576]{1,0:T(8,128)(2,1)S(1)} %bitcast.15), custom_call_target="tpu_custom_call" | custom-call | tf_op jit(solution)/shard_map/pack/pallas_call | solution.py:216
  28.5 0.1 slice_bitcast_fusion
  28.6 1.9 %collective-permute-start.7 = (bf16[2016,128]{1,0:T(8,128)(2,1)S(1)}, bf16[2016,128]{1,0:T(8,128)(2,1)S(1)}, u32[]{:S(2)}, u32[]{:S(2)}) collective-permute-start(bf16[2016,128]{1,0:T(8,128)(2,1)S(1)} %get-tuple-element.16), channel_id=1, source_target_pairs={{0,1},{1,2},{2,3},{3,0},{4,5},{5,6},{6,7},{7,4},{8,9},{9,10},{10,1... | collective-permute-start | bytes 1548296 | tf_op jit(solution)/shard_map/ppermute | solution.py:52
  30.5 1.9 %collective-permute-start.8 = (bf16[2016,128]{1,0:T(8,128)(2,1)S(1)}, bf16[2016,128]{1,0:T(8,128)(2,1)S(1)}, u32[]{:S(2)}, u32[]{:S(2)}) collective-permute-start(bf16[2016,128]{1,0:T(8,128)(2,1)S(1)} %get-tuple-element.15), channel_id=1, source_target_pairs={{0,2},{1,3},{2,0},{3,1},{4,6},{5,7},{6,4},{7,5},{8,10},{9,11},{10,... | collective-permute-start | bytes 1548296 | tf_op jit(solution)/shard_map/ppermute | solution.py:52
  32.4 0.0 collective-permute-done.3.refs_4_
  32.5 5.5 %collective-permute-start.9 = (bf16[2016,128]{1,0:T(8,128)(2,1)S(1)}, bf16[2016,128]{1,0:T(8,128)(2,1)S(1)}, u32[]{:S(2)}, u32[]{:S(2)}) collective-permute-start(bf16[2016,128]{1,0:T(8,128)(2,1)S(1)} %get-tuple-element.14), channel_id=1, source_target_pairs={{0,3},{1,0},{2,1},{3,2},{4,7},{5,4},{6,5},{7,6},{8,11},{9,8},{10,9... | collective-permute-start | bytes 1548296 | tf_op jit(solution)/shard_map/ppermute | solution.py:52
  37.9 8.7 %collective-permute-done.7.first = bf16[2016,128]{1,0:T(8,128)(2,1)S(1)} collective-permute-done((bf16[2016,128]{1,0:T(8,128)(2,1)S(1)}, bf16[2016,128]{1,0:T(8,128)(2,1)S(1)}, u32[]{:S(2)}, u32[]{:S(2)}) %collective-permute-start.7) | collective-permute-done | bytes 516128 | tf_op jit(solution)/shard_map/ppermute | solution.py:52
  46.6 1.9 %collective-permute-start.4 = (bf16[144,1024]{1,0:T(8,128)(2,1)S(1)}, bf16[144,1024]{1,0:T(8,128)(2,1)S(1)}, u32[]{:S(2)}, u32[]{:S(2)}) collective-permute-start(bf16[144,1024]{1,0:T(8,128)(2,1)S(1)} %collective-permute-done.3.refs_4_), channel_id=1, source_target_pairs={{0,4},{1,5},{2,6},{3,7},{4,8},{5,9},{6,10},{7,11},{8,12},{9,13},{1... | collective-permute-start | bytes 884744 | tf_op jit(solution)/shard_map/ppermute | solution.py:27
  48.5 0.0 collective-permute-done.8.second
  48.6 7.8 %collective-permute-done.9.third = bf16[2016,128]{1,0:T(8,128)(2,1)S(1)} collective-permute-done((bf16[2016,128]{1,0:T(8,128)(2,1)S(1)}, bf16[2016,128]{1,0:T(8,128)(2,1)S(1)}, u32[]{:S(2)}, u32[]{:S(2)}) %collective-permute-start.9) | collective-permute-done | bytes 516128 | tf_op jit(solution)/shard_map/ppermute | solution.py:52
  56.4 3.2 %collective-permute-done.4.rest_2_.refs_5_ = bf16[144,1024]{1,0:T(8,128)(2,1)S(1)} collective-permute-done((bf16[144,1024]{1,0:T(8,128)(2,1)S(1)}, bf16[144,1024]{1,0:T(8,128)(2,1)S(1)}, u32[]{:S(2)}, u32[]{:S(2)}) %collective-permute-start.4) | collective-permute-done | bytes 294944 | tf_op jit(solution)/shard_map/ppermute | solution.py:27
  59.5 0.0 collective-permute-done.rest_0_.refs_1_
  59.5 0.0 collective-permute-done.2.rest_1_.refs_3_
  59.5 0.1 join.1.mine_ref
  59.6 1.9 %collective-permute-start.10 = (bf16[3,2016,128]{2,1,0:T(8,128)(2,1)S(1)}, bf16[3,2016,128]{2,1,0:T(8,128)(2,1)S(1)}, u32[]{:S(2)}, u32[]{:S(2)}) collective-permute-start(bf16[3,2016,128]{2,1,0:T(8,128)(2,1)S(1)} %join.1.mine_ref), channel_id=1, source_target_pairs={{0,16},{16,0},{32,48},{48,32},{64,80},{80,64},{96,112},{112,96},{1... | collective-permute-start | bytes 4644872 | tf_op jit(solution)/shard_map/ppermute | solution.py:42
  61.6 1.9 %collective-permute-start.1 = (bf16[432,1024]{1,0:T(8,128)(2,1)S(1)}, bf16[432,1024]{1,0:T(8,128)(2,1)S(1)}, u32[]{:S(2)}, u32[]{:S(2)}) collective-permute-start(bf16[432,1024]{1,0:T(8,128)(2,1)S(1)} %collective-permute-done.rest_0_.refs_1_), channel_id=1, source_target_pairs={{0,1},{1,2},{2,3},{3,0},{4,5},{5,6},{6,7},{7,4},{8,9},{9,10},{10,1... | collective-permute-start | bytes 2654216 | tf_op jit(solution)/shard_map/ppermute | solution.py:27
  63.5 4.2 %collective-permute-start.6 = (bf16[144,1024]{1,0:T(8,128)(2,1)S(1)}, bf16[144,1024]{1,0:T(8,128)(2,1)S(1)}, u32[]{:S(2)}, u32[]{:S(2)}) collective-permute-start(bf16[144,1024]{1,0:T(8,128)(2,1)S(1)} %collective-permute-done.3.refs_4_), channel_id=1, source_target_pairs={{0,12},{1,13},{2,14},{3,15},{4,0},{5,1},{6,2},{7,3},{8,4},{9,5},{1... | collective-permute-start | bytes 884744 | tf_op jit(solution)/shard_map/ppermute | solution.py:27
  67.7 3.2 %collective-permute-start.5 = (bf16[144,1024]{1,0:T(8,128)(2,1)S(1)}, bf16[144,1024]{1,0:T(8,128)(2,1)S(1)}, u32[]{:S(2)}, u32[]{:S(2)}) collective-permute-start(bf16[144,1024]{1,0:T(8,128)(2,1)S(1)} %collective-permute-done.4.rest_2_.refs_5_), channel_id=1, source_target_pairs={{0,4},{1,5},{2,6},{3,7},{4,8},{5,9},{6,10},{7,11},{8,12},{9,13},{1... | collective-permute-start | bytes 884744 | tf_op jit(solution)/shard_map/ppermute | solution.py:27
  70.9 0.0 collective-permute-done.10.other_ref
  70.9 7.7 %unpack.1 = (bf16[4,1728,144]{2,1,0:T(8,128)(2,1)}, bf16[4,1728,144]{2,1,0:T(8,128)(2,1)}) custom-call(s32[1]{0:T(128)} %bitcast.core_ref, bf16[2,1728,144]{2,1,0:T(8,128)(2,1)S(1)} %get-tuple-element.8.own_ref, bf16[3,2016,128]{2,1,0:T(8,128)(2,1)S(1)} %join.1.mine_ref, bf16[3,2016,128]{2,1,0:T(8,128)(2,1)S(1)} %collective-permute-done.10.other_ref), custom_call_target="tpu_custom_call" | custom-call | tf_op jit(solution)/shard_map/unpack/pallas_call | solution.py:236
  78.6 0.0 collective-permute-done.6.refs_7_
  78.6 4.0 %collective-permute-done.5.refs_6_ = bf16[144,1024]{1,0:T(8,128)(2,1)S(1)} collective-permute-done((bf16[144,1024]{1,0:T(8,128)(2,1)S(1)}, bf16[144,1024]{1,0:T(8,128)(2,1)S(1)}, u32[]{:S(2)}, u32[]{:S(2)}) %collective-permute-start.5) | collective-permute-done | bytes 294944 | tf_op jit(solution)/shard_map/ppermute | solution.py:27
  82.6 0.0 collective-permute-done.1.refs_2_
  82.6 11.0 %ladders.1 = f32[48,128]{1,0:T(8,128)S(1)} custom-call(s32[1]{0:T(128)} %bitcast.core_ref, bf16[432,1024]{1,0:T(8,128)(2,1)S(1)} %reshape.19.refs_0_, bf16[432,1024]{1,0:T(8,128)(2,1)S(1)} %collective-permute-done.rest_0_.refs_1_, bf16[432,1024]{1,0:T(8,128)(2,1)S(1)} %collective-permute-done.1.refs_2_, ...), custom_call_target="tpu_custom_call" | custom-call | tf_op jit(solution)/shard_map/ladders/pallas_call | solution.py:245
  93.6 20.3 %all_to_all.5.parts_ref = f32[16,48,128]{2,1,0:T(8,128)S(1)} all-to-all(f32[16,48,128]{2,1,0:T(8,128)S(1)} %broadcast_in_dim.3), channel_id=1, replica_groups=mesh['row'=48,'col'=16] {'col'}, dimensions={0} | all-to-all | bytes 786432 | tf_op jit(solution)/shard_map/all_to_all | solution.py:258
  114.0 0.7 add.15
  (1 shorter events, 0.0 us)
Async XLA Ops:
  2.5 57.0 %collective-permute-start = (bf16[432,1024]{1,0:T(8,128)(2,1)S(1)}, bf16[432,1024]{1,0:T(8,128)(2,1)S(1)}, u32[]{:S(2)}, u32[]{:S(2)}) collective-permute-start(bf16[432,1024]{1,0:T(8,128)(2,1)S(1)} %reshape.19.refs_0_), channel_id=1, source_target_pairs={{0,1},{1,2},{2,3},{3,0},{4,5},{5,6},{6,7},{7,4},{8,9},{9,10},{10,1... | collective-permute-start | bytes 2654216 | tf_op jit(solution)/shard_map/ppermute | solution.py:27
  7.8 51.8 %collective-permute-start.2 = (bf16[432,1024]{1,0:T(8,128)(2,1)S(1)}, bf16[432,1024]{1,0:T(8,128)(2,1)S(1)}, u32[]{:S(2)}, u32[]{:S(2)}) collective-permute-start(bf16[432,1024]{1,0:T(8,128)(2,1)S(1)} %reshape.19.refs_0_), channel_id=1, source_target_pairs={{0,3},{1,0},{2,1},{3,2},{4,7},{5,4},{6,5},{7,6},{8,11},{9,8},{10,9... | collective-permute-start | bytes 2654216 | tf_op jit(solution)/shard_map/ppermute | solution.py:27
  11.5 21.0 %collective-permute-start.3 = (bf16[144,1024]{1,0:T(8,128)(2,1)}, bf16[144,1024]{1,0:T(8,128)(2,1)S(1)}, u32[]{:S(2)}, u32[]{:S(2)}) collective-permute-start(bf16[144,1024]{1,0:T(8,128)(2,1)} %reshape.20), channel_id=1, source_target_pairs={{0,752},{16,0},{32,16},{48,32},{64,48},{80,64},{96,80},{112,96},{1... | collective-permute-start | bytes 884744 | tf_op jit(solution)/shard_map/ppermute | solution.py:37
  23.9 1.6 %copy-start = (bf16[48,36,576]{2,0,1:T(8,128)(2,1)S(1)}, bf16[48,36,576]{2,0,1:T(8,128)(2,1)}, u32[]{:S(2)}) copy-start(bf16[48,36,576]{2,0,1:T(8,128)(2,1)} %param.3) | copy-start | bytes 5971972
  28.6 18.0 %collective-permute-start.7 = (bf16[2016,128]{1,0:T(8,128)(2,1)S(1)}, bf16[2016,128]{1,0:T(8,128)(2,1)S(1)}, u32[]{:S(2)}, u32[]{:S(2)}) collective-permute-start(bf16[2016,128]{1,0:T(8,128)(2,1)S(1)} %get-tuple-element.16), channel_id=1, source_target_pairs={{0,1},{1,2},{2,3},{3,0},{4,5},{5,6},{6,7},{7,4},{8,9},{9,10},{10,1... | collective-permute-start | bytes 1548296 | tf_op jit(solution)/shard_map/ppermute | solution.py:52
  30.5 18.0 %collective-permute-start.8 = (bf16[2016,128]{1,0:T(8,128)(2,1)S(1)}, bf16[2016,128]{1,0:T(8,128)(2,1)S(1)}, u32[]{:S(2)}, u32[]{:S(2)}) collective-permute-start(bf16[2016,128]{1,0:T(8,128)(2,1)S(1)} %get-tuple-element.15), channel_id=1, source_target_pairs={{0,2},{1,3},{2,0},{3,1},{4,6},{5,7},{6,4},{7,5},{8,10},{9,11},{10,... | collective-permute-start | bytes 1548296 | tf_op jit(solution)/shard_map/ppermute | solution.py:52
  32.5 23.9 %collective-permute-start.9 = (bf16[2016,128]{1,0:T(8,128)(2,1)S(1)}, bf16[2016,128]{1,0:T(8,128)(2,1)S(1)}, u32[]{:S(2)}, u32[]{:S(2)}) collective-permute-start(bf16[2016,128]{1,0:T(8,128)(2,1)S(1)} %get-tuple-element.14), channel_id=1, source_target_pairs={{0,3},{1,0},{2,1},{3,2},{4,7},{5,4},{6,5},{7,6},{8,11},{9,8},{10,9... | collective-permute-start | bytes 1548296 | tf_op jit(solution)/shard_map/ppermute | solution.py:52
  46.6 12.9 %collective-permute-start.4 = (bf16[144,1024]{1,0:T(8,128)(2,1)S(1)}, bf16[144,1024]{1,0:T(8,128)(2,1)S(1)}, u32[]{:S(2)}, u32[]{:S(2)}) collective-permute-start(bf16[144,1024]{1,0:T(8,128)(2,1)S(1)} %collective-permute-done.3.refs_4_), channel_id=1, source_target_pairs={{0,4},{1,5},{2,6},{3,7},{4,8},{5,9},{6,10},{7,11},{8,12},{9,13},{1... | collective-permute-start | bytes 884744 | tf_op jit(solution)/shard_map/ppermute | solution.py:27
  59.6 11.3 %collective-permute-start.10 = (bf16[3,2016,128]{2,1,0:T(8,128)(2,1)S(1)}, bf16[3,2016,128]{2,1,0:T(8,128)(2,1)S(1)}, u32[]{:S(2)}, u32[]{:S(2)}) collective-permute-start(bf16[3,2016,128]{2,1,0:T(8,128)(2,1)S(1)} %join.1.mine_ref), channel_id=1, source_target_pairs={{0,16},{16,0},{32,48},{48,32},{64,80},{80,64},{96,112},{112,96},{1... | collective-permute-start | bytes 4644872 | tf_op jit(solution)/shard_map/ppermute | solution.py:42
  61.6 21.1 %collective-permute-start.1 = (bf16[432,1024]{1,0:T(8,128)(2,1)S(1)}, bf16[432,1024]{1,0:T(8,128)(2,1)S(1)}, u32[]{:S(2)}, u32[]{:S(2)}) collective-permute-start(bf16[432,1024]{1,0:T(8,128)(2,1)S(1)} %collective-permute-done.rest_0_.refs_1_), channel_id=1, source_target_pairs={{0,1},{1,2},{2,3},{3,0},{4,5},{5,6},{6,7},{7,4},{8,9},{9,10},{10,1... | collective-permute-start | bytes 2654216 | tf_op jit(solution)/shard_map/ppermute | solution.py:27
  63.5 15.1 %collective-permute-start.6 = (bf16[144,1024]{1,0:T(8,128)(2,1)S(1)}, bf16[144,1024]{1,0:T(8,128)(2,1)S(1)}, u32[]{:S(2)}, u32[]{:S(2)}) collective-permute-start(bf16[144,1024]{1,0:T(8,128)(2,1)S(1)} %collective-permute-done.3.refs_4_), channel_id=1, source_target_pairs={{0,12},{1,13},{2,14},{3,15},{4,0},{5,1},{6,2},{7,3},{8,4},{9,5},{1... | collective-permute-start | bytes 884744 | tf_op jit(solution)/shard_map/ppermute | solution.py:27
  67.7 14.9 %collective-permute-start.5 = (bf16[144,1024]{1,0:T(8,128)(2,1)S(1)}, bf16[144,1024]{1,0:T(8,128)(2,1)S(1)}, u32[]{:S(2)}, u32[]{:S(2)}) collective-permute-start(bf16[144,1024]{1,0:T(8,128)(2,1)S(1)} %collective-permute-done.4.rest_2_.refs_5_), channel_id=1, source_target_pairs={{0,4},{1,5},{2,6},{3,7},{4,8},{5,9},{6,10},{7,11},{8,12},{9,13},{1... | collective-permute-start | bytes 884744 | tf_op jit(solution)/shard_map/ppermute | solution.py:27

commit v8 on v5

--- a/solution.py
+++ b/solution.py
@@ -227,11 +227,11 @@
     mine = pl.pallas_call(
         join_kernel,
         out_shape=jax.ShapeDtypeStruct(sent.shape, bf16),
-        in_specs=[vmem] * 3 + [hbm] * 3,
+        in_specs=[vmem] * 3 + [hbm] * 2,
         out_specs=vmem,
         compiler_params=params,
         name="join",
-    )(*mine, lines[1], lines[3], partners[1])
+    )(*mine, lines[1], partners[1])
     other = between_cores(mine)
     ab, ba = pl.pallas_call(
         functools.partial(unpack_kernel, pairs_p),

time: 116 us -> 118 us (1.017)
  blocking collectives: 20.3 us -> 23 us
  starting transfers between devices: 41.9 us -> 43.5 us
  waiting for transfers between devices: 23 us -> 21.8 us
    ppermute x6, starting transfers between devices: 18.4 us -> 23.1 us  [moved(): return lax.ppermute(value, ('row', 'col'), pairs)]
    ppermute x1, starting transfers between devices: 12.3 us -> 9.13 us  [from_next_row(): lax.ppermute(value, 'row', [(source, (source - 1) % rows) for source in r...]
    all_to_all x1, blocking collectives: 20.3 us -> 23 us  [shards(): lax.all_to_all(jnp.broadcast_to(part, (SIDE * SIDE, *part.shape)), 'col',...]
  transfers between devices with their start and end apart: 11 -> 11, of which waited for: 4 -> 5; matrix products, arithmetic and copies ran while one was open for 2% -> 1% of each run, Pallas kernels for 10% -> 10%
where the time goes in v8:
time: 118 us; the launch traced here: 117 us
  starting transfers between devices  43.5 us (37%)
  Pallas kernels  23.1 us (20%)
  blocking collectives  23 us (19%)
  waiting for transfers between devices  21.8 us (18%)
  local copies, waits for them, and re-layouts  4.73 us (4%)
    ppermute x6, starting transfers between devices, moved(): return lax.ppermute(value, ('row', 'col'), pairs)  23.1 us
    all_to_all x1, blocking collectives, shards(): lax.all_to_all(jnp.broadcast_to(part, (SIDE * SIDE, *part.shape)), 'col',...  23 us
    ppermute x3, waiting for transfers between devices, core_0_along_x_core_1_along_y(): return lax.ppermute(value, ('row', 'col'), pairs)  16.2 us
    pallas_call x1, Pallas kernels, shards(): pl.pallas_call(functools.partial(ladder_kernel, own_a, own_c, pairs_p), o...  11 us
    ppermute x3, starting transfers between devices, core_0_along_x_core_1_along_y(): return lax.ppermute(value, ('row', 'col'), pairs)  9.31 us
    ppermute x1, starting transfers between devices, from_next_row(): lax.ppermute(value, 'row', [(source, (source - 1) % rows) for source in r...  9.13 us
    pallas_call x1, Pallas kernels, shards(): pl.pallas_call(functools.partial(unpack_kernel, pairs_p), out_shape=(jax....  8.36 us
    ppermute x6, waiting for transfers between devices, moved(): return lax.ppermute(value, ('row', 'col'), pairs)  5.61 us
  transfers between devices with their start and end apart: 11, of which 5 were waited for; matrix products, arithmetic and copies ran while one was open for 1% of the time, Pallas kernels for 10%

profile of v8, /device:TPU:1, one launch (start us, length us, event | category | flops | bytes accessed | tf_op | source)
XLA Modules:
  0.0 117.0 jit_solution(7367861325456848885)
XLA Ops:
  0.6 1.7 %copy.5 = bf16[36,12,1024]{2,1,0:T(8,128)(2,1)S(1)} copy(bf16[36,12,1024]{2,0,1:T(8,128)(2,1)} %bitcast.16) | data formatting | bytes 1769472 | tf_op jit(solution)/shard_map/transpose | solution.py:214
  2.3 0.2 reshape.19.refs_0_
  2.5 5.2 %collective-permute-start = (bf16[432,1024]{1,0:T(8,128)(2,1)S(1)}, bf16[432,1024]{1,0:T(8,128)(2,1)S(1)}, u32[]{:S(2)}, u32[]{:S(2)}) collective-permute-start(bf16[432,1024]{1,0:T(8,128)(2,1)S(1)} %reshape.19.refs_0_), channel_id=1, source_target_pairs={{0,1},{1,2},{2,3},{3,0},{4,5},{5,6},{6,7},{7,4},{8,9},{9,10},{10,1... | collective-permute-start | bytes 2654216 | tf_op jit(solution)/shard_map/ppermute | solution.py:27
  7.8 1.0 slice.12
  8.8 0.1 reshape.20
  8.8 9.1 %collective-permute-start.3 = (bf16[144,1024]{1,0:T(8,128)(2,1)S(1)}, bf16[144,1024]{1,0:T(8,128)(2,1)S(1)}, u32[]{:S(2)}, u32[]{:S(2)}) collective-permute-start(bf16[144,1024]{1,0:T(8,128)(2,1)S(1)} %reshape.20), channel_id=1, source_target_pairs={{0,752},{16,0},{32,16},{48,32},{64,48},{80,64},{96,80},{112,96},{1... | collective-permute-start | bytes 884744 | tf_op jit(solution)/shard_map/ppermute | solution.py:37
  18.0 0.1 pad_add_fusion.at_ref
  18.1 0.0 copy-start
  18.1 1.6 %copy-done = bf16[48,36,576]{2,0,1:T(8,128)(2,1)S(1)} copy-done((bf16[48,36,576]{2,0,1:T(8,128)(2,1)S(1)}, bf16[48,36,576]{2,0,1:T(8,128)(2,1)}, u32[]{:S(2)}) %copy-start) | copy-done | bytes 1990680
  19.7 2.9 %pack.1 = (bf16[3,2016,128]{2,1,0:T(8,128)(2,1)S(1)}, bf16[2,1728,144]{2,1,0:T(8,128)(2,1)S(1)}) custom-call(s32[3]{0:T(128)S(1)} %pad_add_fusion.at_ref, bf16[1728,576]{1,0:T(8,128)(2,1)S(1)} %bitcast.15), custom_call_target="tpu_custom_call" | custom-call | tf_op jit(solution)/shard_map/pack/pallas_call | solution.py:216
  22.7 0.1 slice_bitcast_fusion
  22.8 1.9 %collective-permute-start.7 = (bf16[2016,128]{1,0:T(8,128)(2,1)S(1)}, bf16[2016,128]{1,0:T(8,128)(2,1)S(1)}, u32[]{:S(2)}, u32[]{:S(2)}) collective-permute-start(bf16[2016,128]{1,0:T(8,128)(2,1)S(1)} %get-tuple-element.16), channel_id=1, source_target_pairs={{0,1},{1,2},{2,3},{3,0},{4,5},{5,6},{6,7},{7,4},{8,9},{9,10},{10,1... | collective-permute-start | bytes 1548296 | tf_op jit(solution)/shard_map/ppermute | solution.py:52
  24.7 1.9 %collective-permute-start.8 = (bf16[2016,128]{1,0:T(8,128)(2,1)S(1)}, bf16[2016,128]{1,0:T(8,128)(2,1)S(1)}, u32[]{:S(2)}, u32[]{:S(2)}) collective-permute-start(bf16[2016,128]{1,0:T(8,128)(2,1)S(1)} %get-tuple-element.15), channel_id=1, source_target_pairs={{0,2},{1,3},{2,0},{3,1},{4,6},{5,7},{6,4},{7,5},{8,10},{9,11},{10,... | collective-permute-start | bytes 1548296 | tf_op jit(solution)/shard_map/ppermute | solution.py:52
  26.6 5.5 %collective-permute-start.9 = (bf16[2016,128]{1,0:T(8,128)(2,1)S(1)}, bf16[2016,128]{1,0:T(8,128)(2,1)S(1)}, u32[]{:S(2)}, u32[]{:S(2)}) collective-permute-start(bf16[2016,128]{1,0:T(8,128)(2,1)S(1)} %get-tuple-element.14), channel_id=1, source_target_pairs={{0,3},{1,0},{2,1},{3,2},{4,7},{5,4},{6,5},{7,6},{8,11},{9,8},{10,9... | collective-permute-start | bytes 1548296 | tf_op jit(solution)/shard_map/ppermute | solution.py:52
  32.1 0.0 collective-permute-done.3.refs_4_
  32.1 4.0 %collective-permute-start.4 = (bf16[144,1024]{1,0:T(8,128)(2,1)S(1)}, bf16[144,1024]{1,0:T(8,128)(2,1)S(1)}, u32[]{:S(2)}, u32[]{:S(2)}) collective-permute-start(bf16[144,1024]{1,0:T(8,128)(2,1)S(1)} %collective-permute-done.3.refs_4_), channel_id=1, source_target_pairs={{0,4},{1,5},{2,6},{3,7},{4,8},{5,9},{6,10},{7,11},{8,12},{9,13},{1... | collective-permute-start | bytes 884744 | tf_op jit(solution)/shard_map/ppermute | solution.py:27
  36.1 6.5 %collective-permute-done.7.first = bf16[2016,128]{1,0:T(8,128)(2,1)S(1)} collective-permute-done((bf16[2016,128]{1,0:T(8,128)(2,1)S(1)}, bf16[2016,128]{1,0:T(8,128)(2,1)S(1)}, u32[]{:S(2)}, u32[]{:S(2)}) %collective-permute-start.7) | collective-permute-done | bytes 516128 | tf_op jit(solution)/shard_map/ppermute | solution.py:52
  42.6 0.0 collective-permute-done.8.second
  42.6 9.7 %collective-permute-done.9.third = bf16[2016,128]{1,0:T(8,128)(2,1)S(1)} collective-permute-done((bf16[2016,128]{1,0:T(8,128)(2,1)S(1)}, bf16[2016,128]{1,0:T(8,128)(2,1)S(1)}, u32[]{:S(2)}, u32[]{:S(2)}) %collective-permute-start.9) | collective-permute-done | bytes 516128 | tf_op jit(solution)/shard_map/ppermute | solution.py:52
  52.3 3.2 %collective-permute-done.4.rest_1_.refs_5_ = bf16[144,1024]{1,0:T(8,128)(2,1)S(1)} collective-permute-done((bf16[144,1024]{1,0:T(8,128)(2,1)S(1)}, bf16[144,1024]{1,0:T(8,128)(2,1)S(1)}, u32[]{:S(2)}, u32[]{:S(2)}) %collective-permute-start.4) | collective-permute-done | bytes 294944 | tf_op jit(solution)/shard_map/ppermute | solution.py:27
  55.5 0.0 collective-permute-done.rest_0_.refs_1_
  55.5 0.1 join.1.mine_ref
  55.6 1.9 %collective-permute-start.10 = (bf16[3,2016,128]{2,1,0:T(8,128)(2,1)S(1)}, bf16[3,2016,128]{2,1,0:T(8,128)(2,1)S(1)}, u32[]{:S(2)}, u32[]{:S(2)}) collective-permute-start(bf16[3,2016,128]{2,1,0:T(8,128)(2,1)S(1)} %join.1.mine_ref), channel_id=1, source_target_pairs={{0,16},{16,0},{32,48},{48,32},{64,80},{80,64},{96,112},{112,96},{1... | collective-permute-start | bytes 4644872 | tf_op jit(solution)/shard_map/ppermute | solution.py:42
  57.5 2.8 %collective-permute-start.2 = (bf16[432,1024]{1,0:T(8,128)(2,1)S(1)}, bf16[432,1024]{1,0:T(8,128)(2,1)S(1)}, u32[]{:S(2)}, u32[]{:S(2)}) collective-permute-start(bf16[432,1024]{1,0:T(8,128)(2,1)S(1)} %reshape.19.refs_0_), channel_id=1, source_target_pairs={{0,3},{1,0},{2,1},{3,2},{4,7},{5,4},{6,5},{7,6},{8,11},{9,8},{10,9... | collective-permute-start | bytes 2654216 | tf_op jit(solution)/shard_map/ppermute | solution.py:27
  60.3 3.7 %collective-permute-start.1 = (bf16[432,1024]{1,0:T(8,128)(2,1)S(1)}, bf16[432,1024]{1,0:T(8,128)(2,1)S(1)}, u32[]{:S(2)}, u32[]{:S(2)}) collective-permute-start(bf16[432,1024]{1,0:T(8,128)(2,1)S(1)} %collective-permute-done.rest_0_.refs_1_), channel_id=1, source_target_pairs={{0,1},{1,2},{2,3},{3,0},{4,5},{5,6},{6,7},{7,4},{8,9},{9,10},{10,1... | collective-permute-start | bytes 2654216 | tf_op jit(solution)/shard_map/ppermute | solution.py:27
  64.0 4.3 %collective-permute-start.6 = (bf16[144,1024]{1,0:T(8,128)(2,1)S(1)}, bf16[144,1024]{1,0:T(8,128)(2,1)S(1)}, u32[]{:S(2)}, u32[]{:S(2)}) collective-permute-start(bf16[144,1024]{1,0:T(8,128)(2,1)S(1)} %collective-permute-done.3.refs_4_), channel_id=1, source_target_pairs={{0,12},{1,13},{2,14},{3,15},{4,0},{5,1},{6,2},{7,3},{8,4},{9,5},{1... | collective-permute-start | bytes 884744 | tf_op jit(solution)/shard_map/ppermute | solution.py:27
  68.3 3.1 %collective-permute-start.5 = (bf16[144,1024]{1,0:T(8,128)(2,1)S(1)}, bf16[144,1024]{1,0:T(8,128)(2,1)S(1)}, u32[]{:S(2)}, u32[]{:S(2)}) collective-permute-start(bf16[144,1024]{1,0:T(8,128)(2,1)S(1)} %collective-permute-done.4.rest_1_.refs_5_), channel_id=1, source_target_pairs={{0,4},{1,5},{2,6},{3,7},{4,8},{5,9},{6,10},{7,11},{8,12},{9,13},{1... | collective-permute-start | bytes 884744 | tf_op jit(solution)/shard_map/ppermute | solution.py:27
  71.4 0.0 collective-permute-done.10.other_ref
  71.4 8.4 %unpack.1 = (bf16[4,1728,144]{2,1,0:T(8,128)(2,1)}, bf16[4,1728,144]{2,1,0:T(8,128)(2,1)}) custom-call(s32[1]{0:T(128)} %bitcast.core_ref, bf16[2,1728,144]{2,1,0:T(8,128)(2,1)S(1)} %get-tuple-element.8.own_ref, bf16[3,2016,128]{2,1,0:T(8,128)(2,1)S(1)} %join.1.mine_ref, bf16[3,2016,128]{2,1,0:T(8,128)(2,1)S(1)} %collective-permute-done.10.other_ref), custom_call_target="tpu_custom_call" | custom-call | tf_op jit(solution)/shard_map/unpack/pallas_call | solution.py:236
  79.8 0.1 collective-permute-done.6.refs_7_
  79.9 2.3 %collective-permute-done.5.refs_6_ = bf16[144,1024]{1,0:T(8,128)(2,1)S(1)} collective-permute-done((bf16[144,1024]{1,0:T(8,128)(2,1)S(1)}, bf16[144,1024]{1,0:T(8,128)(2,1)S(1)}, u32[]{:S(2)}, u32[]{:S(2)}) %collective-permute-start.5) | collective-permute-done | bytes 294944 | tf_op jit(solution)/shard_map/ppermute | solution.py:27
  82.3 0.0 collective-permute-done.2.refs_3_
  82.3 0.0 collective-permute-done.1.refs_2_
  82.3 11.0 %ladders.1 = f32[48,128]{1,0:T(8,128)S(1)} custom-call(s32[1]{0:T(128)} %bitcast.core_ref, bf16[432,1024]{1,0:T(8,128)(2,1)S(1)} %reshape.19.refs_0_, bf16[432,1024]{1,0:T(8,128)(2,1)S(1)} %collective-permute-done.rest_0_.refs_1_, bf16[432,1024]{1,0:T(8,128)(2,1)S(1)} %collective-permute-done.1.refs_2_, ...), custom_call_target="tpu_custom_call" | custom-call | tf_op jit(solution)/shard_map/ladders/pallas_call | solution.py:245
  93.3 23.0 %all_to_all.5.parts_ref = f32[16,48,128]{2,1,0:T(8,128)S(1)} all-to-all(f32[16,48,128]{2,1,0:T(8,128)S(1)} %broadcast_in_dim.3), channel_id=1, replica_groups=mesh['row'=48,'col'=16] {'col'}, dimensions={0} | all-to-all | bytes 786432 | tf_op jit(solution)/shard_map/all_to_all | solution.py:258
  116.3 0.7 add.15
  (1 shorter events, 0.0 us)
Async XLA Ops:
  2.5 52.9 %collective-permute-start = (bf16[432,1024]{1,0:T(8,128)(2,1)S(1)}, bf16[432,1024]{1,0:T(8,128)(2,1)S(1)}, u32[]{:S(2)}, u32[]{:S(2)}) collective-permute-start(bf16[432,1024]{1,0:T(8,128)(2,1)S(1)} %reshape.19.refs_0_), channel_id=1, source_target_pairs={{0,1},{1,2},{2,3},{3,0},{4,5},{5,6},{6,7},{7,4},{8,9},{9,10},{10,1... | collective-permute-start | bytes 2654216 | tf_op jit(solution)/shard_map/ppermute | solution.py:27
  8.8 23.3 %collective-permute-start.3 = (bf16[144,1024]{1,0:T(8,128)(2,1)S(1)}, bf16[144,1024]{1,0:T(8,128)(2,1)S(1)}, u32[]{:S(2)}, u32[]{:S(2)}) collective-permute-start(bf16[144,1024]{1,0:T(8,128)(2,1)S(1)} %reshape.20), channel_id=1, source_target_pairs={{0,752},{16,0},{32,16},{48,32},{64,48},{80,64},{96,80},{112,96},{1... | collective-permute-start | bytes 884744 | tf_op jit(solution)/shard_map/ppermute | solution.py:37
  18.1 1.6 %copy-start = (bf16[48,36,576]{2,0,1:T(8,128)(2,1)S(1)}, bf16[48,36,576]{2,0,1:T(8,128)(2,1)}, u32[]{:S(2)}) copy-start(bf16[48,36,576]{2,0,1:T(8,128)(2,1)} %param.3) | copy-start | bytes 5971972
  22.8 19.8 %collective-permute-start.7 = (bf16[2016,128]{1,0:T(8,128)(2,1)S(1)}, bf16[2016,128]{1,0:T(8,128)(2,1)S(1)}, u32[]{:S(2)}, u32[]{:S(2)}) collective-permute-start(bf16[2016,128]{1,0:T(8,128)(2,1)S(1)} %get-tuple-element.16), channel_id=1, source_target_pairs={{0,1},{1,2},{2,3},{3,0},{4,5},{5,6},{6,7},{7,4},{8,9},{9,10},{10,1... | collective-permute-start | bytes 1548296 | tf_op jit(solution)/shard_map/ppermute | solution.py:52
  24.7 17.9 %collective-permute-start.8 = (bf16[2016,128]{1,0:T(8,128)(2,1)S(1)}, bf16[2016,128]{1,0:T(8,128)(2,1)S(1)}, u32[]{:S(2)}, u32[]{:S(2)}) collective-permute-start(bf16[2016,128]{1,0:T(8,128)(2,1)S(1)} %get-tuple-element.15), channel_id=1, source_target_pairs={{0,2},{1,3},{2,0},{3,1},{4,6},{5,7},{6,4},{7,5},{8,10},{9,11},{10,... | collective-permute-start | bytes 1548296 | tf_op jit(solution)/shard_map/ppermute | solution.py:52
  26.6 25.7 %collective-permute-start.9 = (bf16[2016,128]{1,0:T(8,128)(2,1)S(1)}, bf16[2016,128]{1,0:T(8,128)(2,1)S(1)}, u32[]{:S(2)}, u32[]{:S(2)}) collective-permute-start(bf16[2016,128]{1,0:T(8,128)(2,1)S(1)} %get-tuple-element.14), channel_id=1, source_target_pairs={{0,3},{1,0},{2,1},{3,2},{4,7},{5,4},{6,5},{7,6},{8,11},{9,8},{10,9... | collective-permute-start | bytes 1548296 | tf_op jit(solution)/shard_map/ppermute | solution.py:52
  32.1 23.4 %collective-permute-start.4 = (bf16[144,1024]{1,0:T(8,128)(2,1)S(1)}, bf16[144,1024]{1,0:T(8,128)(2,1)S(1)}, u32[]{:S(2)}, u32[]{:S(2)}) collective-permute-start(bf16[144,1024]{1,0:T(8,128)(2,1)S(1)} %collective-permute-done.3.refs_4_), channel_id=1, source_target_pairs={{0,4},{1,5},{2,6},{3,7},{4,8},{5,9},{6,10},{7,11},{8,12},{9,13},{1... | collective-permute-start | bytes 884744 | tf_op jit(solution)/shard_map/ppermute | solution.py:27
  55.6 15.8 %collective-permute-start.10 = (bf16[3,2016,128]{2,1,0:T(8,128)(2,1)S(1)}, bf16[3,2016,128]{2,1,0:T(8,128)(2,1)S(1)}, u32[]{:S(2)}, u32[]{:S(2)}) collective-permute-start(bf16[3,2016,128]{2,1,0:T(8,128)(2,1)S(1)} %join.1.mine_ref), channel_id=1, source_target_pairs={{0,16},{16,0},{32,48},{48,32},{64,80},{80,64},{96,112},{112,96},{1... | collective-permute-start | bytes 4644872 | tf_op jit(solution)/shard_map/ppermute | solution.py:42
  57.5 24.7 %collective-permute-start.2 = (bf16[432,1024]{1,0:T(8,128)(2,1)S(1)}, bf16[432,1024]{1,0:T(8,128)(2,1)S(1)}, u32[]{:S(2)}, u32[]{:S(2)}) collective-permute-start(bf16[432,1024]{1,0:T(8,128)(2,1)S(1)} %reshape.19.refs_0_), channel_id=1, source_target_pairs={{0,3},{1,0},{2,1},{3,2},{4,7},{5,4},{6,5},{7,6},{8,11},{9,8},{10,9... | collective-permute-start | bytes 2654216 | tf_op jit(solution)/shard_map/ppermute | solution.py:27
  60.3 21.9 %collective-permute-start.1 = (bf16[432,1024]{1,0:T(8,128)(2,1)S(1)}, bf16[432,1024]{1,0:T(8,128)(2,1)S(1)}, u32[]{:S(2)}, u32[]{:S(2)}) collective-permute-start(bf16[432,1024]{1,0:T(8,128)(2,1)S(1)} %collective-permute-done.rest_0_.refs_1_), channel_id=1, source_target_pairs={{0,1},{1,2},{2,3},{3,0},{4,5},{5,6},{6,7},{7,4},{8,9},{9,10},{10,1... | collective-permute-start | bytes 2654216 | tf_op jit(solution)/shard_map/ppermute | solution.py:27
  64.0 15.9 %collective-permute-start.6 = (bf16[144,1024]{1,0:T(8,128)(2,1)S(1)}, bf16[144,1024]{1,0:T(8,128)(2,1)S(1)}, u32[]{:S(2)}, u32[]{:S(2)}) collective-permute-start(bf16[144,1024]{1,0:T(8,128)(2,1)S(1)} %collective-permute-done.3.refs_4_), channel_id=1, source_target_pairs={{0,12},{1,13},{2,14},{3,15},{4,0},{5,1},{6,2},{7,3},{8,4},{9,5},{1... | collective-permute-start | bytes 884744 | tf_op jit(solution)/shard_map/ppermute | solution.py:27
  68.3 13.9 %collective-permute-start.5 = (bf16[144,1024]{1,0:T(8,128)(2,1)S(1)}, bf16[144,1024]{1,0:T(8,128)(2,1)S(1)}, u32[]{:S(2)}, u32[]{:S(2)}) collective-permute-start(bf16[144,1024]{1,0:T(8,128)(2,1)S(1)} %collective-permute-done.4.rest_1_.refs_5_), channel_id=1, source_target_pairs={{0,4},{1,5},{2,6},{3,7},{4,8},{5,9},{6,10},{7,11},{8,12},{9,13},{1... | collective-permute-start | bytes 884744 | tf_op jit(solution)/shard_map/ppermute | solution.py:27
